TPU v7x, 32 devices: a whole 2x2x4 slice. The times are simulated.
32 devices in a mesh: dp: 8 (over z, y), row: 2 (over x), col: 2 (over core).
Axes of the slice: x: 2, y: 2, z: 4, core: 2. Of those that a mesh axis runs over, the one named last changes fastest.
Arguments:
- inputs: bfloat16 [12288, 1536], P(('dp', 'col'), 'row'), may hold values from -6 to 6
- segments: int32 [12288], P(('dp', 'row')), may hold values from 0 to 3, as said below
- positions: int32 [12288], P(('dp', 'row')), may hold values from 0 to 2558, as said below
- w_query: bfloat16 [1536, 1536], P('row', 'col'), may hold values from -0.15625 to 0.15625
- w_key: bfloat16 [1536, 256], P('row', 'col'), may hold values from -0.15625 to 0.15625
- w_value: bfloat16 [1536, 256], P('row', 'col'), may hold values from -0.15625 to 0.15625
- b_query: bfloat16 [1536], P('col'), may hold values from -3 to 3
- b_key: bfloat16 [256], P('col'), may hold values from -3 to 3
- b_value: bfloat16 [256], P('col'), may hold values from -3 to 3
- w_out: bfloat16 [1536, 1536], P('col', 'row'), may hold values from -0.625 to 0.625
- gain_one: bfloat16 [1536], P('row'), may hold values from 0.099609375 to 1.8984375
- gain_two: bfloat16 [1536], P('row'), may hold values from 0.099609375 to 1.8984375
- w_gate: bfloat16 [1536, 8960], P('row', 'col'), may hold values from -0.15625 to 0.15625
- w_up: bfloat16 [1536, 8960], P('row', 'col'), may hold values from -0.15625 to 0.15625
- w_down: bfloat16 [8960, 1536], P('col', 'row'), may hold values from -0.0625 to 0.0625
- cotangent: bfloat16 [12288, 1536], P(('dp', 'col'), 'row'), may hold values from -6 to 6
Outputs:
- output: bfloat16 [12288, 1536], P(('dp', 'col'), 'row')
- input_grad: float32 [12288, 1536], P(('dp', 'col'), 'row')
- query_grad: float32 [1536, 1536], P(('row', 'dp'), 'col')
- key_grad: float32 [1536, 256], P(('row', 'dp'), 'col')
- value_grad: float32 [1536, 256], P(('row', 'dp'), 'col')
- query_bias_grad: float32 [1536], P('col')
- key_bias_grad: float32 [256], P('col')
- value_bias_grad: float32 [256], P('col')
- out_grad: float32 [1536, 1536], P('col', ('row', 'dp'))
- gain_one_grad: float32 [1536], P('row')
- gain_two_grad: float32 [1536], P('row')
- gate_grad: float32 [1536, 8960], P(('row', 'dp'), 'col')
- up_grad: float32 [1536, 8960], P(('row', 'dp'), 'col')
- down_grad: float32 [8960, 1536], P('col', ('row', 'dp'))
Inputs may be any that keep to these rules, and one draw needn't show every extreme that they name: `segments`: within each aligned block of 768 tokens (the tokens of one device), document numbers start at 0 and never fall; every document lies inside one block and has at most 512 tokens, and each block holds one of exactly 512. Within a document, positions rise by one from token to token; a document's first position is 0 to 2047.
All inputs are finite; a program needn't handle non-finite values.
Results may differ from a plain program's by a relative error of at most 0.023.
Values may be sent and summed in bfloat16 or wider, within the bound.
No kernel may reach another device: no remote copies, remote signals or barrier semaphores. Data moves between devices by JAX's collectives and lax.ppermute only.
A program may use at most 384 MiB of HBM per device.

v0:
```python
import jax
import jax.numpy as jnp
from jax import lax
from jax.sharding import PartitionSpec as P

D = 1536
HQ = 12
KVH = 2
HD = 128


EPS = 1e-06
THETA = 1000000.0


def for_sending(value):

    def short(part):
        return part.astype(jnp.bfloat16) if part.dtype == jnp.float32 else part

    return jax.tree.map(short, value)


def row_total(values):
    return lax.psum(values, "row")


def col_collect(values):
    return lax.all_gather(values, "col", axis=0, tiled=True)


def col_reduce(values):
    return lax.psum_scatter(values, "col", scatter_dimension=0, tiled=True)


def row_reduce(values):
    return lax.psum_scatter(values, "row", scatter_dimension=0, tiled=True)


def row_collect(values):
    return jax.tree.map(
        lambda part, own: part.astype(own.dtype),
        lax.all_gather(for_sending(values), "row", axis=0, tiled=True),
        values,
    )


def ffn_total(values):
    return lax.psum(values, "row")


def product(left, right):
    return jnp.dot(left, right, preferred_element_type=jnp.float32)


def product_left(left, right):
    return lax.dot_general(
        left, right, (((0,), (0,)), ((), ())), preferred_element_type=jnp.float32
    )


def product_right(left, right):
    return lax.dot_general(
        left, right, (((1,), (1,)), ((), ())), preferred_element_type=jnp.float32
    )


def angles(positions):
    indices = jnp.arange(HD // 2, dtype=jnp.float32)
    inverse = jnp.exp(indices * (-2.0 / HD) * jnp.log(jnp.float32(THETA)))
    turned = positions.astype(jnp.float32)[:, None] * inverse[None, :]
    return (jnp.cos(turned)[:, None, :], jnp.sin(turned)[:, None, :])


def rotate(values, cosine, sine):
    halfway = HD // 2
    front_half = values[..., :halfway]
    back_half = values[..., halfway:]
    return jnp.concatenate(
        [front_half * cosine - back_half * sine, back_half * cosine + front_half * sine], axis=-1
    )


def masked_scores(grouped, keys_local, segments):
    length = grouped.shape[0]
    scores = jnp.einsum(
        "qkgd,pkd->kgqp", grouped, keys_local, preferred_element_type=jnp.float32
    ) * HD ** (-0.5)
    places = jnp.arange(length)
    allowed = (segments[:, None] == segments[None, :]) & (places[None, :] <= places[:, None])
    return jnp.where(allowed, scores, -1e30)


def gate_terms(hidden_grad, gate, upward):
    sigma = jax.nn.sigmoid(gate)
    gate_grad = hidden_grad * upward * sigma * (1.0 + gate * (1.0 - sigma))
    up_grad = hidden_grad * gate * sigma
    return (gate_grad.astype(jnp.bfloat16), up_grad.astype(jnp.bfloat16))


def body(
    inputs,
    segments,
    positions,
    w_query,
    w_key,
    w_value,
    b_query,
    b_key,
    b_value,
    w_out,
    gain_one,
    gain_two,
    w_gate,
    w_up,
    w_down,
    cotangent,
):
    length = inputs.shape[0]
    heads_here = w_query.shape[1] // HD
    pairs_here = w_key.shape[1] // HD
    group_size = HQ // KVH
    query_width = w_query.shape[1]
    key_width = w_key.shape[1]
    cosine, sine = angles(positions)
    gain_first = gain_one.astype(jnp.float32)
    gain_second = gain_two.astype(jnp.float32)
    residual = inputs.astype(jnp.float32)
    rstd_one = lax.rsqrt(row_total(jnp.sum(residual * residual, axis=1)) / D + EPS)[:, None]
    normed_one = residual * rstd_one
    full_one = col_collect((normed_one * gain_first).astype(jnp.bfloat16))
    query_sum, key_sum, value_sum = row_reduce(
        (product(full_one, w_query), product(full_one, w_key), product(full_one, w_value))
    )
    queries = rotate(
        (query_sum + b_query.astype(jnp.float32)).reshape(length, heads_here, HD), cosine, sine
    ).astype(jnp.bfloat16)
    keys_local = rotate(
        (key_sum + b_key.astype(jnp.float32)).reshape(length, pairs_here, HD), cosine, sine
    ).astype(jnp.bfloat16)
    values_local = (
        (value_sum + b_value.astype(jnp.float32))
        .astype(jnp.bfloat16)
        .reshape(length, pairs_here, HD)
    )
    grouped = queries.reshape(length, pairs_here, group_size, HD)
    scores = masked_scores(grouped, keys_local, segments)
    row_max = jnp.max(scores, axis=-1, keepdims=True)
    row_sum = jnp.sum(jnp.exp(scores - row_max), axis=-1, keepdims=True)
    log_total = row_max + jnp.log(row_sum)
    weights = jnp.exp(scores - log_total).astype(jnp.bfloat16)
    attended = jnp.einsum(
        "kgqp,pkd->qkgd", weights, values_local, preferred_element_type=jnp.float32
    )
    attended = attended.reshape(length, query_width).astype(jnp.bfloat16)
    full_att = row_collect(attended)
    middle = residual + col_reduce(product(full_att, w_out))
    rstd_two = lax.rsqrt(row_total(jnp.sum(middle * middle, axis=1)) / D + EPS)[:, None]
    normed_two = middle * rstd_two
    full_two = col_collect((normed_two * gain_second).astype(jnp.bfloat16))
    gate, upward = ffn_total((product(full_two, w_gate), product(full_two, w_up)))
    full_hidden = (jax.nn.silu(gate) * upward).astype(jnp.bfloat16)
    output = (middle + col_reduce(product(full_hidden, w_down))).astype(jnp.bfloat16)
    full_cot = col_collect(cotangent)
    grad_down = product_left(full_hidden, full_cot)
    gate_low, up_low = gate_terms(ffn_total(product_right(full_cot, w_down)), gate, upward)
    grad_gate = product_left(full_two, gate_low)
    grad_up = product_left(full_two, up_low)
    normed_grad_two = col_reduce(product_right(gate_low, w_gate) + product_right(up_low, w_up))
    scaled_two = normed_grad_two * gain_second
    gain_two_part = jnp.sum(normed_grad_two * normed_two, axis=0)
    mean_two = row_total(jnp.sum(scaled_two * normed_two, axis=1)) / D
    middle_grad = cotangent.astype(jnp.float32) + rstd_two * (
        scaled_two - normed_two * mean_two[:, None]
    )
    full_mid = col_collect(middle_grad.astype(jnp.bfloat16))
    grad_out = product_left(full_att, full_mid)
    att_grad = row_reduce(product_right(full_mid, w_out)).astype(jnp.bfloat16)
    att_grouped = att_grad.reshape(length, pairs_here, group_size, HD)
    scores = masked_scores(grouped, keys_local, segments)
    probs = jnp.exp(scores - log_total)
    weights = probs.astype(jnp.bfloat16)
    prob_grad = jnp.einsum(
        "qkgd,pkd->kgqp", att_grouped, values_local, preferred_element_type=jnp.float32
    )
    delta = jnp.sum(probs * prob_grad, axis=-1, keepdims=True)
    score_grad = (probs * (prob_grad - delta)).astype(jnp.bfloat16)
    query_turned = jnp.einsum(
        "kgqp,pkd->qkgd", score_grad, keys_local, preferred_element_type=jnp.float32
    ) * HD ** (-0.5)
    key_turned = jnp.einsum(
        "kgqp,qkgd->pkd", score_grad, grouped, preferred_element_type=jnp.float32
    ) * HD ** (-0.5)
    value_back = jnp.einsum(
        "kgqp,qkgd->pkd", weights, att_grouped, preferred_element_type=jnp.float32
    )
    query_low = (
        rotate(query_turned.reshape(length, heads_here, HD), cosine, -sine)
        .reshape(length, query_width)
        .astype(jnp.bfloat16)
    )
    key_low = rotate(key_turned, cosine, -sine).reshape(length, key_width).astype(jnp.bfloat16)
    value_low = value_back.reshape(length, key_width).astype(jnp.bfloat16)
    bias_parts = jnp.concatenate(
        [
            jnp.sum(query_low.astype(jnp.float32), axis=0),
            jnp.sum(key_low.astype(jnp.float32), axis=0),
            jnp.sum(value_low.astype(jnp.float32), axis=0),
        ]
    )
    full_query, full_key, full_value = row_collect((query_low, key_low, value_low))
    grad_query = product_left(full_one, full_query)
    grad_key = product_left(full_one, full_key)
    grad_value = product_left(full_one, full_value)
    input_part = (
        product_right(full_query, w_query)
        + product_right(full_key, w_key)
        + product_right(full_value, w_value)
    )
    normed_grad_one = col_reduce(input_part)
    scaled_one = normed_grad_one * gain_first
    gain_one_part = jnp.sum(normed_grad_one * normed_one, axis=0)
    mean_one = row_total(jnp.sum(scaled_one * normed_one, axis=1)) / D
    input_grad = middle_grad + rstd_one * (scaled_one - normed_one * mean_one[:, None])
    col_pick = (jnp.arange(lax.axis_size("col")) == lax.axis_index("col")).astype(jnp.float32)[
        :, None
    ]
    row_pick = (jnp.arange(lax.axis_size("row")) == lax.axis_index("row")).astype(jnp.float32)[
        :, None, None
    ]
    gains_stacked = jnp.stack([gain_one_part, gain_two_part])
    bias_all, gain_all = lax.psum(
        (col_pick * bias_parts[None, :], row_pick * gains_stacked[None]), ("dp", "row", "col")
    )
    bias_mine = lax.dynamic_index_in_dim(bias_all, lax.axis_index("col"), 0, keepdims=False)
    gain_mine = lax.dynamic_index_in_dim(gain_all, lax.axis_index("row"), 0, keepdims=False)
    attention_parts = (
        lax.psum_scatter(
            grad_query.astype(jnp.bfloat16), "dp", scatter_dimension=0, tiled=True
        ).astype(jnp.float32),
        lax.psum_scatter(
            grad_key.astype(jnp.bfloat16), "dp", scatter_dimension=0, tiled=True
        ).astype(jnp.float32),
        lax.psum_scatter(
            grad_value.astype(jnp.bfloat16), "dp", scatter_dimension=0, tiled=True
        ).astype(jnp.float32),
        lax.psum_scatter(
            grad_out.astype(jnp.bfloat16), "dp", scatter_dimension=1, tiled=True
        ).astype(jnp.float32),
    )
    ffn_parts = (
        lax.psum_scatter(
            grad_gate.astype(jnp.bfloat16), "dp", scatter_dimension=0, tiled=True
        ).astype(jnp.float32),
        lax.psum_scatter(
            grad_up.astype(jnp.bfloat16), "dp", scatter_dimension=0, tiled=True
        ).astype(jnp.float32),
        lax.psum_scatter(
            grad_down.astype(jnp.bfloat16), "dp", scatter_dimension=1, tiled=True
        ).astype(jnp.float32),
    )
    return (
        output,
        input_grad,
        attention_parts[0],
        attention_parts[1],
        attention_parts[2],
        bias_mine[:query_width],
        bias_mine[query_width : query_width + key_width],
        bias_mine[query_width + key_width :],
        attention_parts[3],
        gain_mine[0],
        gain_mine[1],
        ffn_parts[0],
        ffn_parts[1],
        ffn_parts[2],
    )


def solution(mesh):
    return jax.shard_map(
        body,
        mesh=mesh,
        in_specs=(
            P(("dp", "col"), "row"),
            P(("dp", "row")),
            P(("dp", "row")),
            P("row", "col"),
            P("row", "col"),
            P("row", "col"),
            P("col"),
            P("col"),
            P("col"),
            P("col", "row"),
            P("row"),
            P("row"),
            P("row", "col"),
            P("row", "col"),
            P("col", "row"),
            P(("dp", "col"), "row"),
        ),
        out_specs=(
            P(("dp", "col"), "row"),
            P(("dp", "col"), "row"),
            P(("row", "dp"), "col"),
            P(("row", "dp"), "col"),
            P(("row", "dp"), "col"),
            P("col"),
            P("col"),
            P("col"),
            P("col", ("row", "dp")),
            P("row"),
            P("row"),
            P(("row", "dp"), "col"),
            P(("row", "dp"), "col"),
            P("col", ("row", "dp")),
        ),
        check_vma=False,
    )
```

profile of v0, /device:TPU:0, one launch (start us, length us, event | category | flops | bytes accessed | tf_op | source)
XLA Modules:
  0.0 3051.4 jit_solution(10093312231766530095)
XLA Ops:
  18.2 12.9 all-gather.9.cloned.1.call-done
  56.8 58.9 %reduce-scatter.20.cloned.1.call-done = f32[768,768]{1,0:T(8,128)} async-done(((f32[1536,768]{1,0:T(8,128)}), f32[768,768]{1,0:T(8,128)}) %reduce-scatter.20.cloned.1.call-update) | async-done | bytes 2359312 | tf_op jit(solution)/shard_map/reduce_scatter | solution.py:37
  143.8 8.7 fusion.22
  152.5 36.3 %all-gather.11.cloned.1.call-done = bf16[1536,768]{0,1:T(8,128)(2,1)} async-done(((bf16[768,768]{0,1:T(8,128)(2,1)}), bf16[1536,768]{0,1:T(8,128)(2,1)}) %all-gather.11.cloned.1.call-update) | async-done | bytes 2359312 | tf_op jit(solution)/shard_map/all_gather | solution.py:43
  195.5 11.9 reduce-scatter.22.cloned.1.call-done
  221.2 19.6 fusion.78
  240.8 19.6 fusion.75
  260.4 17.5 fusion.76
  278.1 1796.7 %all-reduce.4.cloned.1.call-done = (f32[1536,4480]{1,0:T(8,128)}, f32[1536,4480]{1,0:T(8,128)}, f32[1536,4480]{1,0:T(8,128)}) async-done(((f32[1536,4480]{1,0:T(8,128)}, f32[1536,4480]{1,0:T(8,128)}, f32[1536,4480]{1,0:T(8,128)}), (f32[1536,4480]{1,0:T(8,128)}, f32[1536,4480]{1,0:T(8,128)}, f32[1536,4480]{1,0:T(8,128)})) %all-reduce.4.cloned.1.call-update) | async-done | bytes 82575376 | tf_op jit(solution)/shard_map/psum | solution.py:49
  2074.8 37.6 %multiply_convert_fusion = (bf16[1536,4480]{1,0:T(8,128)(2,1)}, bf16[1536,4480]{1,0:T(8,128)(2,1)S(1)}, bf16[1536,4480]{1,0:T(8,128)(2,1)}) fusion(f32[1536,4480]{1,0:T(8,128)} %get-tuple-element.24, f32[1536,4480]{1,0:T(8,128)} %get-tuple-element.23, f32[1536,4480]{1,0:T(8,128)} %get-tuple-element.22), kind=kLoop, calls=%fused_computation | loop fusion | flops 110100480 | bytes 123863040 | tf_op jit(solution)/shard_map/convert_element_type | solution.py:98
  2112.4 16.6 fusion.79
  2129.1 18.3 convolution_add_fusion
  2147.5 12.7 reduce-scatter.26.cloned.1.call-done
  2173.1 12.2 all-gather.17.cloned.1.call-done
  2191.4 61.0 %reduce-scatter.28.cloned.1.call-done = f32[768,768]{1,0:T(8,128)} async-done(((f32[1536,768]{1,0:T(8,128)}), f32[768,768]{1,0:T(8,128)}) %reduce-scatter.28.cloned.1.call-update) | async-done | bytes 2359312 | tf_op jit(solution)/shard_map/reduce_scatter | solution.py:37
  2256.9 11.4 fusion
  2271.0 7.0 fusion.5
  2287.1 16.9 convolution_convert_fusion.2
  2304.1 17.0 convolution_convert_fusion.1
  2321.3 17.1 convolution_convert_fusion
  2344.0 8.4 convert_reduce_fusion.1
  2352.3 7.6 all-gather.1
  2392.5 17.1 fusion.77
  2411.2 42.1 %reduce-scatter.40.cloned.1.call-done = bf16[96,4480]{1,0:T(8,128)(2,1)} async-done(((bf16[768,4480]{1,0:T(8,128)(2,1)}), bf16[96,4480]{1,0:T(8,128)(2,1)}) %reduce-scatter.40.cloned.1.call-update) | async-done | bytes 860176 | tf_op jit(solution)/shard_map/reduce_scatter | solution.py:252
  2455.7 126.9 %reduce-scatter.42.cloned.1.call-done = bf16[96,4480]{1,0:T(8,128)(2,1)} async-done(((bf16[768,4480]{1,0:T(8,128)(2,1)}), bf16[96,4480]{1,0:T(8,128)(2,1)}) %reduce-scatter.42.cloned.1.call-update) | async-done | bytes 860176 | tf_op jit(solution)/shard_map/reduce_scatter | solution.py:255
  2585.1 126.9 %reduce-scatter.44.cloned.1.call-done = bf16[4480,96]{0,1:T(8,128)(2,1)} async-done(((bf16[4480,768]{0,1:T(8,128)(2,1)}), bf16[4480,96]{0,1:T(8,128)(2,1)}) %reduce-scatter.44.cloned.1.call-update) | async-done | bytes 860176 | tf_op jit(solution)/shard_map/reduce_scatter | solution.py:258
  2714.4 64.5 %reduce-scatter.38.cloned.1.call-done = bf16[768,96]{0,1:T(8,128)(2,1)} async-done(((bf16[768,768]{0,1:T(8,128)(2,1)}), bf16[768,96]{0,1:T(8,128)(2,1)}) %reduce-scatter.38.cloned.1.call-update) | async-done | bytes 147472 | tf_op jit(solution)/shard_map/reduce_scatter | solution.py:247
  2782.6 59.5 %reduce-scatter.36.cloned.1.call-done = bf16[96,128]{1,0:T(8,128)(2,1)} async-done(((bf16[768,128]{1,0:T(8,128)(2,1)}), bf16[96,128]{1,0:T(8,128)(2,1)}) %reduce-scatter.36.cloned.1.call-update) | async-done | bytes 24592 | tf_op jit(solution)/shard_map/reduce_scatter | solution.py:244
  2843.5 62.6 %reduce-scatter.34.cloned.1.call-done = bf16[96,128]{1,0:T(8,128)(2,1)} async-done(((bf16[768,128]{1,0:T(8,128)(2,1)}), bf16[96,128]{1,0:T(8,128)(2,1)}) %reduce-scatter.34.cloned.1.call-update) | async-done | bytes 24592 | tf_op jit(solution)/shard_map/reduce_scatter | solution.py:241
  2907.4 65.6 %reduce-scatter.32.cloned.1.call-done = bf16[96,768]{1,0:T(8,128)(2,1)} async-done(((bf16[768,768]{1,0:T(8,128)(2,1)}), bf16[96,768]{1,0:T(8,128)(2,1)}) %reduce-scatter.32.cloned.1.call-update) | async-done | bytes 147472 | tf_op jit(solution)/shard_map/reduce_scatter | solution.py:238
  2974.6 12.3 reduce-scatter.30.cloned.1.call-done
  2990.0 40.9 %all-reduce = (f32[2,1024]{1,0:T(2,128)S(1)}, f32[2,2,768]{2,1,0:T(2,128)S(1)}) all-reduce(f32[2,1024]{1,0:T(2,128)} %broadcast_multiply_fusion.1, f32[2,2,768]{2,1,0:T(2,128)S(1)} %broadcast_multiply_fusion), channel_id=1, replica_groups=mesh['dp'=8,'row'=2,'col'=2] {'dp','row','col'}, use_global_device_ids=true, to_apply=%region_28.29 | all-reduce | flops 5120 | bytes 40960 | tf_op jit(solution)/shard_map/psum | solution.py:232
  (233 shorter events, 192.1 us)
Async XLA Ops:
  7.2 181.6 %copy-start = (bf16[768,768]{1,0:T(8,128)(2,1)S(1)}, bf16[768,768]{1,0:T(8,128)(2,1)}, u32[]{:S(2)}) copy-start(bf16[768,768]{1,0:T(8,128)(2,1)} %param.25) | copy-start | bytes 3538948
  7.2 23.8 all-gather.9.cloned.1.call-start
  18.1 35.2 %reduce-scatter.18.cloned.1.call-start = ((), (), s32[]{:S(2)}) async-start(), calls=%async_computation.17 | async-start | bytes 1179648 | tf_op jit(solution)/shard_map/reduce_scatter | solution.py:37
  34.5 81.2 %reduce-scatter.20.cloned.1.call-start = ((), (), s32[]{:S(2)}) async-start(), calls=%async_computation.18 | async-start | bytes 7077888 | tf_op jit(solution)/shard_map/reduce_scatter | solution.py:37
  40.0 103.7 %reduce-scatter.16.cloned.1.call-start = ((), (), s32[]{:S(2)}) async-start(), calls=%async_computation.16 | async-start | bytes 1179648 | tf_op jit(solution)/shard_map/reduce_scatter | solution.py:37
  49.6 139.3 %all-gather.11.cloned.1.call-start = ((), (), s32[]{:S(2)}) async-start(), calls=%async_computation.19 | async-start | bytes 3538944 | tf_op jit(solution)/shard_map/all_gather | solution.py:43
  152.5 55.0 %reduce-scatter.22.cloned.1.call-start = ((), (), s32[]{:S(2)}) async-start(), calls=%async_computation.20 | async-start | bytes 7077888 | tf_op jit(solution)/shard_map/reduce_scatter | solution.py:33
  194.7 26.5 all-gather.15.cloned.1.call-start
  195.4 45.3 %all-gather.13.cloned.1.call-start = ((), (), s32[]{:S(2)}) async-start(), calls=%async_computation.21 | async-start | bytes 3538944 | tf_op jit(solution)/shard_map/all_gather | solution.py:29
  195.5 19.3 copy-start.24
  216.7 1858.1 %all-reduce.4.cloned.1.call-start = ((), (), s32[]{:S(2)}) async-start(), calls=%async_computation.36 | async-start | bytes 165150720 | tf_op jit(solution)/shard_map/psum | solution.py:49
  240.8 19.6 copy-start.46
  277.9 1882.4 %reduce-scatter.26.cloned.1.call-start = ((), (), s32[]{:S(2)}) async-start(), calls=%async_computation.24 | async-start | bytes 7077888 | tf_op jit(solution)/shard_map/reduce_scatter | solution.py:33
  2112.4 16.7 copy-start.8
  2147.5 37.8 %all-gather.17.cloned.1.call-start = ((), (), s32[]{:S(2)}) async-start(), calls=%async_computation.25 | async-start | bytes 3538944 | tf_op jit(solution)/shard_map/all_gather | solution.py:29
  2173.0 79.4 %reduce-scatter.28.cloned.1.call-start = ((), (), s32[]{:S(2)}) async-start(), calls=%async_computation.26 | async-start | bytes 7077888 | tf_op jit(solution)/shard_map/reduce_scatter | solution.py:37
  2191.1 65.7 %copy-start.41 = (f32[128]{0:T(128)S(1)}, f32[128]{0:T(128)}, u32[]{:S(2)}) copy-start(f32[128]{0:T(128)} %convert_element_type.171) | copy-start | bytes 1540
  2191.2 188.3 %all-gather.19.cloned.1.call-start = ((), (), s32[]{:S(2)}) async-start(), calls=%async_computation.27 | async-start | bytes 3538944 | tf_op jit(solution)/shard_map/all_gather | solution.py:43
  2286.7 166.6 %reduce-scatter.40.cloned.1.call-start = ((), (), s32[]{:S(2)}) async-start(), calls=%async_computation.33 | async-start | bytes 7741440 | tf_op jit(solution)/shard_map/reduce_scatter | solution.py:252
  2304.0 278.6 %reduce-scatter.42.cloned.1.call-start = ((), (), s32[]{:S(2)}) async-start(), calls=%async_computation.34 | async-start | bytes 7741440 | tf_op jit(solution)/shard_map/reduce_scatter | solution.py:255
  2321.1 390.9 %reduce-scatter.44.cloned.1.call-start = ((), (), s32[]{:S(2)}) async-start(), calls=%async_computation.35 | async-start | bytes 7741440 | tf_op jit(solution)/shard_map/reduce_scatter | solution.py:258
  2338.4 440.5 %reduce-scatter.38.cloned.1.call-start = ((), (), s32[]{:S(2)}) async-start(), calls=%async_computation.32 | async-start | bytes 1327104 | tf_op jit(solution)/shard_map/reduce_scatter | solution.py:247
  2343.9 498.2 %reduce-scatter.36.cloned.1.call-start = ((), (), s32[]{:S(2)}) async-start(), calls=%async_computation.31 | async-start | bytes 221184 | tf_op jit(solution)/shard_map/reduce_scatter | solution.py:244
  2344.0 16.0 copy-start.10
  2344.0 16.0 copy-start.12
  2369.5 536.6 %reduce-scatter.34.cloned.1.call-start = ((), (), s32[]{:S(2)}) async-start(), calls=%async_computation.30 | async-start | bytes 221184 | tf_op jit(solution)/shard_map/reduce_scatter | solution.py:241
  2379.4 593.6 %reduce-scatter.32.cloned.1.call-start = ((), (), s32[]{:S(2)}) async-start(), calls=%async_computation.29 | async-start | bytes 1327104 | tf_op jit(solution)/shard_map/reduce_scatter | solution.py:238
  2385.0 601.9 %reduce-scatter.30.cloned.1.call-start = ((), (), s32[]{:S(2)}) async-start(), calls=%async_computation.28 | async-start | bytes 7077888 | tf_op jit(solution)/shard_map/reduce_scatter | solution.py:33
  2392.2 646.4 %reduce-scatter.24.cloned.1.call-start = ((), (), s32[]{:S(2)}) async-start(), calls=%async_computation.22 | async-start | bytes 7077888 | tf_op jit(solution)/shard_map/reduce_scatter | solution.py:33
  2585.1 401.8 %copy-start.6 = (bf16[768,768]{1,0:T(8,128)(2,1)S(1)}, bf16[768,768]{1,0:T(8,128)(2,1)}, u32[]{:S(2)}) copy-start(bf16[768,768]{1,0:T(8,128)(2,1)} %param.16) | copy-start | bytes 3538948
  2585.1 401.8 %copy-start.31 = (f32[768]{0:T(1024)S(1)}, f32[768]{0:T(1024)}, u32[]{:S(2)}) copy-start(f32[768]{0:T(1024)} %copy-done.30) | copy-start | bytes 9220
  2585.1 401.8 %copy-start.33 = (f32[768]{0:T(1024)S(1)}, f32[768]{0:T(1024)}, u32[]{:S(2)}) copy-start(f32[768]{0:T(1024)} %copy-done.32) | copy-start | bytes 9220
  (43 other events, 261.4 us)
Sparse Core Ops, SparseCore 0:
  18.2 12.7 all-gather.8
  34.6 18.5 reduce-scatter.17
  55.7 59.9 reduce-scatter.19
  117.8 17.4 reduce-scatter.15
  152.6 36.1 all-gather.10
  194.8 12.6 reduce-scatter.21
  209.0 12.1 all-gather.14
  223.3 12.1 all-gather.12
  278.0 1796.7 all-reduce.3
  2147.6 12.6 reduce-scatter.25
  2173.1 12.1 all-gather.16
  2191.3 61.1 reduce-scatter.27
  2286.8 36.0 all-gather.18
  2326.4 126.7 reduce-scatter.39
  2456.7 125.8 reduce-scatter.41
  2586.1 125.8 reduce-scatter.43
  2715.8 63.1 reduce-scatter.37
  2782.0 60.0 reduce-scatter.35
  2845.9 60.0 reduce-scatter.33
  2909.8 63.0 reduce-scatter.31
  2975.3 11.5 reduce-scatter.29
  2989.3 13.7 reduce-scatter.23
where the time goes:
time: 3060 us; the launch traced here: 3050 us
  waiting for transfers between devices  2570 us (84%)
  matrix products  248 us (8%)
  other arithmetic  117 us (4%)
  blocking collectives  76.7 us (3%)
    psum x1, waiting for transfers between devices, ffn_total(): return lax.psum(values, 'row')  1800 us
    reduce_scatter x1, waiting for transfers between devices, body(): lax.psum_scatter(grad_down.astype(jnp.bfloat16), 'dp', scatter_dimension=...  127 us
    reduce_scatter x1, waiting for transfers between devices, body(): lax.psum_scatter(grad_up.astype(jnp.bfloat16), 'dp', scatter_dimension=0,...  127 us
    reduce_scatter x4, waiting for transfers between devices, row_reduce(): return lax.psum_scatter(values, 'row', scatter_dimension=0, tiled=True)  123 us
    dot_general x7, matrix products, product(): return jnp.dot(left, right, preferred_element_type=jnp.float32)  71.5 us
    dot_general x7, matrix products, product_left(): lax.dot_general(left, right, (((0,), (0,)), ((), ())), preferred_element_...  66.5 us
    dot_general x7, matrix products, product_right(): lax.dot_general(left, right, (((1,), (1,)), ((), ())), preferred_element_...  66.3 us
    reduce_scatter x1, waiting for transfers between devices, body(): lax.psum_scatter(grad_query.astype(jnp.bfloat16), 'dp', scatter_dimension...  65.6 us
  transfers between devices with their start and end apart: 22, of which 18 were waited for; matrix products, arithmetic and copies ran while one was open for 6% of the time, Pallas kernels for 0%

commit v1 on v0

v1 whole, which is shorter than its diff:
```python
import jax
import jax.numpy as jnp
from jax import lax
from jax.sharding import PartitionSpec as P

D = 1536
HQ = 12
KVH = 2
HD = 128
LANES = 128


EPS = 1e-06
THETA = 1000000.0
BF = jnp.bfloat16
F32 = jnp.float32


def swap_row(value):
    return lax.ppermute(value, "row", [(0, 1), (1, 0)])


def swap_col(value):
    return lax.ppermute(value, "col", [(0, 1), (1, 0)])


def swap_pair(value):
    size = lax.axis_size("dp")
    return lax.ppermute(value, "dp", [(i, i ^ 1) for i in range(size)])


def shift_outer(value, step):
    size = lax.axis_size("dp")
    return lax.ppermute(value, "dp", [(i, (i + 2 * step) % size) for i in range(size)])


def turn_square(value):
    return lax.ppermute(value, ("row", "col"), [(0, 0), (1, 2), (2, 1), (3, 3)])


def product(left, right):
    return jnp.dot(left, right, preferred_element_type=F32)


def product_left(left, right):
    return lax.dot_general(
        left, right, (((0,), (0,)), ((), ())), preferred_element_type=F32
    )


def product_right(left, right):
    return lax.dot_general(
        left, right, (((1,), (1,)), ((), ())), preferred_element_type=F32
    )


def angles(positions):
    indices = jnp.arange(HD // 2, dtype=F32)
    inverse = jnp.exp(indices * (-2.0 / HD) * jnp.log(F32(THETA)))
    turned = positions.astype(F32)[:, None] * inverse[None, :]
    return (jnp.cos(turned)[:, None, :], jnp.sin(turned)[:, None, :])


def rotate(values, cosine, sine):
    halfway = HD // 2
    front_half = values[..., :halfway]
    back_half = values[..., halfway:]
    return jnp.concatenate(
        [front_half * cosine - back_half * sine, back_half * cosine + front_half * sine], axis=-1
    )


def masked_scores(grouped, keys_local, segments):
    length = grouped.shape[0]
    scores = jnp.einsum(
        "qkgd,pkd->kgqp", grouped, keys_local, preferred_element_type=F32
    ) * HD ** (-0.5)
    places = jnp.arange(length)
    allowed = (segments[:, None] == segments[None, :]) & (places[None, :] <= places[:, None])
    return jnp.where(allowed, scores, -1e30)


def pick(array, index, axis=0):
    return lax.dynamic_index_in_dim(array, index, axis, keepdims=False)


def fetch_block(block, inner):
    halves = block.reshape((2, block.shape[0] // 2) + block.shape[1:])
    direct = swap_row(pick(halves, inner))
    other = swap_pair(direct)
    low = jnp.where(inner == 0, direct, other)
    high = jnp.where(inner == 0, other, direct)
    return jnp.concatenate([low, high], axis=0)


def sum_groups(block, inner, outer_index):
    parts, rows, columns = block.shape
    outer = lax.axis_size("dp") // 2
    piece = rows // (2 * outer)
    cut = block.reshape(parts, outer, 2, piece, columns)
    half = pick(cut, inner, 2).astype(F32) + swap_pair(pick(cut, 1 - inner, 2)).astype(F32)
    half = half.astype(BF)
    total = pick(half, outer_index, 1).astype(F32)
    for step in range(1, outer):
        sent = pick(half, (outer_index + step) % outer, 1)
        total = total + shift_outer(sent, step).astype(F32)
    return total


def body(
    inputs,
    segments,
    positions,
    w_query,
    w_key,
    w_value,
    b_query,
    b_key,
    b_value,
    w_out,
    gain_one,
    gain_two,
    w_gate,
    w_up,
    w_down,
    cotangent,
):
    length = inputs.shape[0]
    width = inputs.shape[1]
    heads_here = w_query.shape[1] // HD
    pairs_here = w_key.shape[1] // HD
    group_size = HQ // KVH
    query_width = w_query.shape[1]
    key_width = w_key.shape[1]
    row = lax.axis_index("row")
    col = lax.axis_index("col")
    group = lax.axis_index("dp")
    inner = group % 2
    outer_index = group // 2
    same = row == col

    def by_row(mine, other):
        return jnp.where(same, mine, other), jnp.where(same, other, mine)

    mine = turn_square(inputs)
    other = swap_col(mine)
    weights_attention = jnp.concatenate([w_query, w_key, w_value], axis=1)
    fetched_attention = fetch_block(weights_attention, inner)
    gains = jnp.stack([gain_one, gain_two])
    fetched_gains = swap_row(gains)
    gains_mine, _ = by_row(gains, fetched_gains)
    gains_mine = gains_mine.astype(F32)
    gains_all = jnp.concatenate([gains, fetched_gains], axis=1).astype(F32)

    hidden_here = w_gate.shape[1]
    blocks = hidden_here // LANES
    quarter = (blocks + 1) // 2 * LANES
    overlap = 2 * quarter - hidden_here
    start_mine = row * (hidden_here - quarter)
    start_other = (1 - row) * (hidden_here - quarter)
    own_gate = lax.dynamic_slice_in_dim(w_gate, start_mine, quarter, 1)
    own_up = lax.dynamic_slice_in_dim(w_up, start_mine, quarter, 1)
    own_down = lax.dynamic_slice_in_dim(w_down, start_mine, quarter, 0)
    fetched_gate = fetch_block(lax.dynamic_slice_in_dim(w_gate, start_other, quarter, 1), inner)
    fetched_up = fetch_block(lax.dynamic_slice_in_dim(w_up, start_other, quarter, 1), inner)
    fetched_out = fetch_block(w_out, inner)
    fetched_down = fetch_block(lax.dynamic_slice_in_dim(w_down, start_other, quarter, 0), inner)
    full_gate = jnp.concatenate([own_gate, fetched_gate], axis=0)
    full_up = jnp.concatenate([own_up, fetched_up], axis=0)
    full_down = jnp.concatenate([own_down, fetched_down], axis=1)
    counted = (jnp.arange(quarter) >= row * overlap)[None, :]

    cot_own = by_row(cotangent, swap_col(cotangent))
    cot_far = swap_row(cotangent)
    cot_far = by_row(cot_far, swap_col(cot_far))
    full_cot = jnp.concatenate(
        [jnp.concatenate([cot_own[0], cot_far[0]], axis=1),
         jnp.concatenate([cot_own[1], cot_far[1]], axis=1)], axis=0
    )
    cot_mine = jnp.where(same, cot_own[0], cot_far[0]).astype(F32)

    cosine, sine = angles(positions)
    residual = mine.astype(F32)
    both = jnp.concatenate(by_row(mine, other), axis=1).astype(F32)
    rstd_one = lax.rsqrt(jnp.mean(both * both, axis=1, keepdims=True) + EPS)
    full_one = (both * rstd_one * gains_all[0]).astype(BF)
    normed_one = residual * rstd_one
    full_attention = jnp.concatenate([weights_attention, fetched_attention], axis=0)
    projected = product(full_one, full_attention)
    bias = jnp.concatenate([b_query, b_key, b_value]).astype(F32)
    projected = projected + bias
    queries = rotate(
        projected[:, :query_width].reshape(length, heads_here, HD), cosine, sine
    ).astype(BF)
    keys_local = rotate(
        projected[:, query_width : query_width + key_width].reshape(length, pairs_here, HD),
        cosine,
        sine,
    ).astype(BF)
    values_local = (
        projected[:, query_width + key_width :].astype(BF).reshape(length, pairs_here, HD)
    )
    grouped = queries.reshape(length, pairs_here, group_size, HD)
    scores = masked_scores(grouped, keys_local, segments)
    row_max = jnp.max(scores, axis=-1, keepdims=True)
    row_sum = jnp.sum(jnp.exp(scores - row_max), axis=-1, keepdims=True)
    log_total = row_max + jnp.log(row_sum)
    weights = jnp.exp(scores - log_total).astype(BF)
    attended = jnp.einsum("kgqp,pkd->qkgd", weights, values_local, preferred_element_type=F32)
    attended = attended.reshape(length, query_width).astype(BF)
    out_keep, out_send = by_row(w_out, fetched_out)
    branch = product(attended, out_keep) + swap_col(
        product(attended, out_send).astype(BF)
    ).astype(F32)
    middle = residual + branch
    squares = jnp.sum(middle * middle, axis=1)
    rstd_two = lax.rsqrt((squares + swap_col(squares)) / D + EPS)[:, None]
    normed_two = middle * rstd_two
    low_two = (normed_two * gains_mine[1]).astype(BF)
    near = jnp.concatenate(by_row(low_two, swap_col(low_two)), axis=1)
    far_two = swap_row(low_two)
    far = jnp.concatenate(by_row(far_two, swap_col(far_two)), axis=1)
    full_two = jnp.concatenate([near, far], axis=0)

    gate = product(full_two, full_gate)
    upward = product(full_two, full_up)
    sigma = jax.nn.sigmoid(gate)
    hidden = jnp.where(counted, gate * sigma * upward, 0.0).astype(BF)
    hidden_grad = jnp.where(counted, product_right(full_cot, full_down), 0.0)
    gate_low = (hidden_grad * upward * sigma * (1.0 + gate * (1.0 - sigma))).astype(BF)
    up_low = (hidden_grad * gate * sigma).astype(BF)

    def gather_sum(partial):
        keep, send = by_row(partial[:, :width].astype(BF), partial[:, width:].astype(BF))
        half = keep.astype(F32) + swap_col(send).astype(F32)
        return half[:length] + swap_row(half[length:].astype(BF)).astype(F32)

    grad_down = product_left(full_cot, hidden).astype(BF).reshape(2, width, quarter)
    sum_down = sum_groups(grad_down, inner, outer_index)
    grad_gate = product_left(full_two, gate_low).astype(BF).reshape(2, width, quarter)
    sum_gate = sum_groups(grad_gate, inner, outer_index)
    grad_up = product_left(full_two, up_low).astype(BF).reshape(2, width, quarter)
    sum_up = sum_groups(grad_up, inner, outer_index)

    normed_grad_two = gather_sum(
        product_right(gate_low, full_gate) + product_right(up_low, full_up)
    )
    output = turn_square(
        (middle + gather_sum(product(hidden, full_down))).astype(BF)
    )
    scaled_two = normed_grad_two * gains_mine[1]
    gain_two_part = jnp.sum(normed_grad_two * normed_two, axis=0)
    dots = jnp.sum(scaled_two * normed_two, axis=1)
    mean_two = (dots + swap_col(dots)) / D
    middle_grad = cot_mine + rstd_two * (scaled_two - normed_two * mean_two[:, None])
    low_mid = middle_grad.astype(BF)
    full_mid = jnp.concatenate(by_row(low_mid, swap_col(low_mid)), axis=1)
    full_out = jnp.concatenate([w_out, fetched_out], axis=1)
    att_grad = product_right(full_mid, full_out).astype(BF)
    grad_out = product_left(full_mid, attended)

    att_grouped = att_grad.reshape(length, pairs_here, group_size, HD)
    scores = masked_scores(grouped, keys_local, segments)
    probs = jnp.exp(scores - log_total)
    weights = probs.astype(BF)
    prob_grad = jnp.einsum(
        "qkgd,pkd->kgqp", att_grouped, values_local, preferred_element_type=F32
    )
    delta = jnp.sum(probs * prob_grad, axis=-1, keepdims=True)
    score_grad = (probs * (prob_grad - delta)).astype(BF)
    query_turned = jnp.einsum(
        "kgqp,pkd->qkgd", score_grad, keys_local, preferred_element_type=F32
    ) * HD ** (-0.5)
    key_turned = jnp.einsum(
        "kgqp,qkgd->pkd", score_grad, grouped, preferred_element_type=F32
    ) * HD ** (-0.5)
    value_back = jnp.einsum(
        "kgqp,qkgd->pkd", weights, att_grouped, preferred_element_type=F32
    )
    query_low = (
        rotate(query_turned.reshape(length, heads_here, HD), cosine, -sine)
        .reshape(length, query_width)
        .astype(BF)
    )
    key_low = rotate(key_turned, cosine, -sine).reshape(length, key_width).astype(BF)
    value_low = value_back.reshape(length, key_width).astype(BF)
    back_low = jnp.concatenate([query_low, key_low, value_low], axis=1)
    bias_part = jnp.sum(back_low.astype(F32), axis=0)

    input_part = product_right(back_low, full_attention)
    keep, send = by_row(input_part[:, :width], input_part[:, width:])
    normed_grad_one = keep + swap_col(send.astype(BF)).astype(F32)
    scaled_one = normed_grad_one * gains_mine[0]
    gain_one_part = jnp.sum(normed_grad_one * normed_one, axis=0)
    dots = jnp.sum(scaled_one * normed_one, axis=1)
    mean_one = (dots + swap_col(dots)) / D
    input_grad = middle_grad + rstd_one * (scaled_one - normed_one * mean_one[:, None])
    input_grad = turn_square(input_grad.astype(BF)).astype(F32)

    grad_attention = product_left(full_one, back_low)
    grads = jnp.concatenate([grad_attention, grad_out], axis=1)
    grads = grads[:width] + swap_row(grads[width:].astype(BF)).astype(F32)
    sum_attention = sum_groups(grads.astype(BF)[None], inner, outer_index)[0]

    small = lax.psum(
        jnp.concatenate([bias_part, gain_one_part, gain_two_part]), ("dp", "row")
    )
    total_width = query_width + 2 * key_width
    gain_sums = small[total_width:].reshape(2, width)
    gain_sums, _ = by_row(gain_sums, swap_col(gain_sums))

    def joined(total):
        near = total[0]
        far = swap_row(total[1].astype(BF)).astype(F32)
        low = jnp.where(row == 0, near, far)
        high = jnp.where(row == 0, far, near)
        return jnp.concatenate([low, high[:, overlap:]], axis=1)

    return (
        output,
        input_grad,
        sum_attention[:, :query_width],
        sum_attention[:, query_width : query_width + key_width],
        sum_attention[:, query_width + key_width : total_width],
        small[:query_width],
        small[query_width : query_width + key_width],
        small[query_width + key_width : total_width],
        sum_attention[:, total_width:].T,
        gain_sums[0],
        gain_sums[1],
        joined(sum_gate),
        joined(sum_up),
        joined(sum_down).T,
    )


def solution(mesh):
    return jax.shard_map(
        body,
        mesh=mesh,
        in_specs=(
            P(("dp", "col"), "row"),
            P(("dp", "row")),
            P(("dp", "row")),
            P("row", "col"),
            P("row", "col"),
            P("row", "col"),
            P("col"),
            P("col"),
            P("col"),
            P("col", "row"),
            P("row"),
            P("row"),
            P("row", "col"),
            P("row", "col"),
            P("col", "row"),
            P(("dp", "col"), "row"),
        ),
        out_specs=(
            P(("dp", "col"), "row"),
            P(("dp", "col"), "row"),
            P(("row", "dp"), "col"),
            P(("row", "dp"), "col"),
            P(("row", "dp"), "col"),
            P("col"),
            P("col"),
            P("col"),
            P("col", ("row", "dp")),
            P("row"),
            P("row"),
            P(("row", "dp"), "col"),
            P(("row", "dp"), "col"),
            P("col", ("row", "dp")),
        ),
        check_vma=False,
    )
```

time: 3060 us -> 1120 us (0.37)
  waiting for transfers between devices: 2570 us -> 486 us
  local copies, waits for them, and re-layouts: 20.5 us -> 99.5 us
  starting transfers between devices: 2.94 us -> 67.1 us
    psum x1 -> x0, waiting for transfers between devices: 1800 us -> none  [ffn_total(): return lax.psum(values, 'row')]
    reduce_scatter x15 -> x0, waiting for transfers between devices: 708 us -> none  [the longest x1 127 us: body(): lax.psum_scatter(grad_down.astype(jnp.bfloat16), 'dp', scatter_dimension=...]
    ppermute x0 -> x52, waiting for transfers between devices: none -> 486 us  [the longest x12 177 us: shift_outer(): lax.ppermute(value, 'dp', [(i, (i + 2 * step) % size) for i in range(size)])]
    ppermute x0 -> x52, starting transfers between devices: none -> 67.1 us  [the longest x12 18.5 us: shift_outer(): lax.ppermute(value, 'dp', [(i, (i + 2 * step) % size) for i in range(size)])]
    all_gather x6 -> x0, waiting for transfers between devices: 65.3 us -> none  [the longest x2 36.3 us: row_collect(): lax.all_gather(for_sending(values), 'row', axis=0, tiled=True)]
    select_n x0 -> x20, other arithmetic: none -> 40 us  [the longest x9 18.3 us: by_row(): return (jnp.where(same, mine, other), jnp.where(same, other, mine))]
    convert_element_type x20 -> x16, other arithmetic: 65.4 us -> 28.2 us  [the longest x4 10.5 us: sum_groups(): half = half.astype(BF)]
    dynamic_slice x0 -> x9, local copies, waits for them, and re-layouts: none -> 31.7 us  [the longest x6 17.1 us: pick(): return lax.dynamic_index_in_dim(array, index, axis, keepdims=False)]
  transfers between devices with their start and end apart: 22 -> 52, of which waited for: 18 -> 17; matrix products, arithmetic and copies ran while one was open for 6% -> 25% of each run, Pallas kernels for 0% -> 0%
where the time goes in v1:
time: 1120 us; the launch traced here: 1110 us
  waiting for transfers between devices  486 us (43%)
  matrix products  258 us (23%)
  other arithmetic  117 us (10%)
  local copies, waits for them, and re-layouts  99.5 us (9%)
  blocking collectives  77 us (7%)
  starting transfers between devices  67.1 us (6%)
    ppermute x12, waiting for transfers between devices, shift_outer(): lax.ppermute(value, 'dp', [(i, (i + 2 * step) % size) for i in range(size)])  177 us
    ppermute x9, waiting for transfers between devices, swap_pair(): return lax.ppermute(value, 'dp', [(i, i ^ 1) for i in range(size)])  164 us
    ppermute x14, waiting for transfers between devices, swap_row(): return lax.ppermute(value, 'row', [(0, 1), (1, 0)])  145 us
    dot_general x5, matrix products, product_left(): lax.dot_general(left, right, (((0,), (0,)), ((), ())), preferred_element_...  96 us
    psum x1, blocking collectives, body(): lax.psum(jnp.concatenate([bias_part, gain_one_part, gain_two_part]), ('dp...  77 us
    dot_general x6, matrix products, product(): return jnp.dot(left, right, preferred_element_type=F32)  74.8 us
    dot_general x5, matrix products, product_right(): lax.dot_general(left, right, (((1,), (1,)), ((), ())), preferred_element_...  64.5 us
    unnamed x246, local copies, waits for them, and re-layouts  34 us
  transfers between devices with their start and end apart: 52, of which 17 were waited for; matrix products, arithmetic and copies ran while one was open for 25% of the time, Pallas kernels for 0%

profile of v1, /device:TPU:0, one launch (start us, length us, event | category | flops | bytes accessed | tf_op | source)
XLA Modules:
  0.0 1107.1 jit_solution(9526082877712925517)
XLA Ops:
  15.8 5.3 constant_dynamic-slice_fusion.7
  22.4 5.9 constant_dynamic-slice_fusion.11
  40.7 9.2 collective-permute-start.1
  52.5 14.1 %collective-permute-done.3 = bf16[384,1024]{1,0:T(8,128)(2,1)} collective-permute-done((bf16[384,1024]{1,0:T(8,128)(2,1)}, bf16[384,1024]{1,0:T(8,128)(2,1)}, u32[]{:S(2)}, u32[]{:S(2)}) %collective-permute-start.3) | collective-permute-done | bytes 786464 | tf_op jit(solution)/shard_map/ppermute | solution.py:20
  74.8 6.7 collective-permute-done.4
  85.3 44.5 %collective-permute-done.22 = bf16[768,768]{0,1:T(8,128)(2,1)} collective-permute-done((bf16[768,768]{0,1:T(8,128)(2,1)}, bf16[768,768]{0,1:T(8,128)(2,1)}, u32[]{:S(2)}, u32[]{:S(2)}) %collective-permute-start.22) | collective-permute-done | bytes 1179680 | tf_op jit(solution)/shard_map/ppermute | solution.py:20
  170.1 21.4 %collective-permute-done.14 = bf16[384,2304]{1,0:T(8,128)(2,1)} collective-permute-done((bf16[384,2304]{1,0:T(8,128)(2,1)}, bf16[384,2304]{1,0:T(8,128)(2,1)}, u32[]{:S(2)}, u32[]{:S(2)}) %collective-permute-start.14) | collective-permute-done | bytes 1769504 | tf_op jit(solution)/shard_map/ppermute | solution.py:20
  199.0 4.8 broadcast_select_fusion.3
  205.1 20.6 %convolution_select_fusion = f32[1536,2304]{1,0:T(8,128)} fusion(pred[2304]{0:T(1024)(128)(4,1)S(1)} %iota_compare_fusion.1, bf16[1152,768]{1,0:T(8,128)(2,1)} %get-tuple-element.80, bf16[1152,768]{1,0:T(8,128)(2,1)} %get-tuple-element.79, bf16[2304,768]{1,0:T(8,128)(2,1)} %get-tuple-element.62, bf16[768,768]{0,1:T(8,128)(2,1)} %get-tuple-element.93, ...), kind=kOutput, calls=%fused_computation | convolution fusion | flops 10915282944 | bytes 25954560 | tf_op jit(solution)/shard_map/dot_general | solution.py:52
  233.0 16.3 %collective-permute-done.15 = bf16[384,2304]{1,0:T(8,128)(2,1)} collective-permute-done((bf16[384,2304]{1,0:T(8,128)(2,1)}, bf16[384,2304]{1,0:T(8,128)(2,1)}, u32[]{:S(2)}, u32[]{:S(2)}) %collective-permute-start.15) | collective-permute-done | bytes 1769504 | tf_op jit(solution)/shard_map/ppermute | solution.py:29
  258.4 18.8 %fusion.20 = f32[1536,2304]{1,0:T(8,128)} fusion(bf16[384,2304]{1,0:T(8,128)(2,1)} %get-tuple-element.84, bf16[384,2304]{1,0:T(8,128)(2,1)} %get-tuple-element.83, bf16[768,2304]{1,0:T(8,128)(2,1)S(1)} %copy-done.35, bf16[768,768]{0,1:T(8,128)(2,1)} %get-tuple-element.97, bf16[768,768]{0,1:T(8,128)(2,1)S(1)} %get-tuple-element.96, ...), kind=kOutput, calls=%fused_computation.60 | convolution fusion | flops 10911744000 | bytes 25952256 | tf_op jit(solution)/shard_map/dot_general | solution.py:42
  277.1 30.7 %multiply_convert_fusion.1 = (bf16[1536,2304]{1,0:T(8,128)(2,1)}, bf16[1536,2304]{1,0:T(8,128)(2,1)}, bf16[1536,2304]{1,0:T(8,128)(2,1)}) fusion(f32[1536,2304]{1,0:T(8,128)} %convolution_select_fusion, f32[1536,2304]{1,0:T(8,128)} %fusion.20, pred[2304]{0:T(1024)(128)(4,1)S(1)} %iota_compare_fusion.1, bf16[384,2304]{1,0:T(8,128)(2,1)} %get-tuple-element.82, ...), kind=kOutput, calls=%fused_computation.8 | convolution fusion | flops 10971906048 | bytes 61344000 | tf_op jit(solution)/shard_map/dot_general | solution.py:42
  307.8 18.4 %fusion.19 = f32[1536,1536]{0,1:T(8,128)} fusion(bf16[1536,2304]{1,0:T(8,128)(2,1)} %get-tuple-element.55, bf16[384,2304]{1,0:T(8,128)(2,1)} %get-tuple-element.84, bf16[384,2304]{1,0:T(8,128)(2,1)} %get-tuple-element.83, bf16[768,2304]{1,0:T(8,128)(2,1)} %get-tuple-element.66), kind=kOutput, calls=%fused_computation.59 | convolution fusion | flops 10892869632 | bytes 23592960 | tf_op jit(solution)/shard_map/dot_general | solution.py:52
  326.2 31.3 %convolution_convert_fusion.1 = bf16[1536,2304]{1,0:T(8,128)(2,1)} fusion(bf16[1536,2304]{1,0:T(8,128)(2,1)} %get-tuple-element.55, bf16[768,768]{0,1:T(8,128)(2,1)S(1)} %copy-done.61, bf16[768,768]{0,1:T(8,128)(2,1)S(1)} %copy-done.59, bf16[768,768]{0,1:T(8,128)(2,1)S(1)} %copy-done.71, bf16[768,768]{0,1:T(8,128)(2,1)S(1)} %copy-done.69), kind=kOutput, calls=%fused_computation.14 | convolution fusion | flops 10894049280 | bytes 18874368 | tf_op jit(solution)/shard_map/dot_general | solution.py:46
  357.5 18.8 %convolution_convert_fusion.3 = bf16[1536,1536]{0,1:T(8,128)(2,1)} fusion(bf16[1536,2304]{1,0:T(8,128)(2,1)} %get-tuple-element.54, bf16[1152,768]{1,0:T(8,128)(2,1)} %get-tuple-element.80, bf16[1152,768]{1,0:T(8,128)(2,1)} %get-tuple-element.79, bf16[2304,768]{1,0:T(8,128)(2,1)} %get-tuple-element.62), kind=kOutput, calls=%fused_computation.20 | convolution fusion | flops 10895228928 | bytes 18874368 | tf_op jit(solution)/shard_map/dot_general | solution.py:42
  380.5 31.4 %convolution_convert_fusion.2 = bf16[1536,2304]{1,0:T(8,128)(2,1)} fusion(bf16[1536,2304]{1,0:T(8,128)(2,1)} %get-tuple-element.53, bf16[768,768]{0,1:T(8,128)(2,1)S(1)} %copy-done.62, bf16[768,768]{0,1:T(8,128)(2,1)S(1)} %copy-done.60, bf16[768,768]{0,1:T(8,128)(2,1)S(1)} %copy-done.72, bf16[768,768]{0,1:T(8,128)(2,1)S(1)} %copy-done.70), kind=kOutput, calls=%fused_computation.15 | convolution fusion | flops 10894049280 | bytes 18874368 | tf_op jit(solution)/shard_map/dot_general | solution.py:46
  411.9 18.7 %add_convert_fusion = bf16[1536,1536]{0,1:T(8,128)(2,1)} fusion(f32[1536,1536]{0,1:T(8,128)} %fusion.19, bf16[1536,2304]{1,0:T(8,128)(2,1)} %get-tuple-element.53, bf16[384,2304]{1,0:T(8,128)(2,1)} %get-tuple-element.82, bf16[384,2304]{1,0:T(8,128)(2,1)} %get-tuple-element.81, bf16[768,2304]{1,0:T(8,128)(2,1)S(1)} %copy-done.34), kind=kOutput, calls=%fused_computation.19 | convolution fusion | flops 10897588224 | bytes 28311552 | tf_op jit(solution)/shard_map/dot_general | solution.py:52
  438.3 28.6 %convolution_convert_fusion = bf16[1536,2304]{1,0:T(8,128)(2,1)} fusion(bf16[1536,2304]{1,0:T(8,128)(2,1)} %get-tuple-element.54, bf16[768,768]{0,1:T(8,128)(2,1)} %get-tuple-element.93, bf16[768,768]{0,1:T(8,128)(2,1)S(1)} %copy-done.53, bf16[768,768]{0,1:T(8,128)(2,1)S(1)} %copy-done.23, bf16[768,768]{0,1:T(8,128)(2,1)S(1)} %copy-done.21), kind=kOutput, calls=%fused_computation.13 | convolution fusion | flops 10894049280 | bytes 18874368 | tf_op jit(solution)/shard_map/dot_general | solution.py:46
  467.0 7.3 constant_dynamic-slice_fusion.1
  495.6 16.5 %collective-permute-done.25 = bf16[768,768]{0,1:T(8,128)(2,1)} collective-permute-done((bf16[768,768]{0,1:T(8,128)(2,1)}, bf16[768,768]{0,1:T(8,128)(2,1)}, u32[]{:S(2)}, u32[]{:S(2)}) %collective-permute-start.25) | collective-permute-done | bytes 1179680 | tf_op jit(solution)/shard_map/ppermute | solution.py:20
  523.2 70.0 %collective-permute-done.42 = bf16[2,4,96,2304]{3,2,0,1:T(8,128)(2,1)} collective-permute-done((bf16[2,4,96,2304]{3,2,0,1:T(8,128)(2,1)}, bf16[2,4,96,2304]{3,2,0,1:T(8,128)(2,1)}, u32[]{:S(2)}, u32[]{:S(2)}) %collective-permute-start.42) | collective-permute-done | bytes 3538976 | tf_op jit(solution)/shard_map/ppermute | solution.py:29
  599.8 68.3 %collective-permute-done.47 = bf16[2,4,96,2304]{3,2,0,1:T(8,128)(2,1)} collective-permute-done((bf16[2,4,96,2304]{3,2,0,1:T(8,128)(2,1)}, bf16[2,4,96,2304]{3,2,0,1:T(8,128)(2,1)}, u32[]{:S(2)}, u32[]{:S(2)}) %collective-permute-start.47) | collective-permute-done | bytes 3538976 | tf_op jit(solution)/shard_map/ppermute | solution.py:29
  683.6 81.9 %collective-permute-done.39 = bf16[2,96,2304]{2,1,0:T(8,128)(2,1)} collective-permute-done((bf16[2,96,2304]{2,1,0:T(8,128)(2,1)S(1)}, bf16[2,96,2304]{2,1,0:T(8,128)(2,1)}, u32[]{:S(2)}, u32[]{:S(2)}) %collective-permute-start.39) | collective-permute-done | bytes 884768 | tf_op jit(solution)/shard_map/ppermute | solution.py:34
  770.2 10.4 collective-permute-start.20
  780.6 43.2 %collective-permute-done.44 = bf16[2,96,2304]{2,1,0:T(8,128)(2,1)S(1)} collective-permute-done((bf16[2,96,2304]{2,1,0:T(8,128)(2,1)S(1)}, bf16[2,96,2304]{2,1,0:T(8,128)(2,1)S(1)}, u32[]{:S(2)}, u32[]{:S(2)}) %collective-permute-start.44) | collective-permute-done | bytes 884768 | tf_op jit(solution)/shard_map/ppermute | solution.py:34
  828.3 32.3 %collective-permute-done.49 = bf16[2,96,2304]{2,1,0:T(8,128)(2,1)S(1)} collective-permute-done((bf16[2,96,2304]{2,1,0:T(8,128)(2,1)S(1)}, bf16[2,96,2304]{2,1,0:T(8,128)(2,1)S(1)}, u32[]{:S(2)}, u32[]{:S(2)}) %collective-permute-start.49) | collective-permute-done | bytes 884768 | tf_op jit(solution)/shard_map/ppermute | solution.py:34
  872.1 7.8 fusion
  879.9 7.1 fusion.5
  931.0 45.6 %collective-permute-done.31 = bf16[768,1792]{0,1:T(8,128)(2,1)} collective-permute-done((bf16[768,1792]{0,1:T(8,128)(2,1)}, bf16[768,1792]{0,1:T(8,128)(2,1)}, u32[]{:S(2)}, u32[]{:S(2)}) %collective-permute-start.31) | collective-permute-done | bytes 2752544 | tf_op jit(solution)/shard_map/ppermute | solution.py:20
  986.5 5.1 fusion.28
  991.6 77.0 %psum.7 = f32[2560]{0:T(1024)S(1)} all-reduce(f32[2560]{0:T(1024)S(1)} %pad_maximum_fusion.24), channel_id=1, replica_groups=mesh['dp'=8,'row'=2,'col'=2] {'dp','row'}, use_global_device_ids=true, to_apply=%region_10.11 | all-reduce | flops 2560 | bytes 20480 | tf_op jit(solution)/shard_map/psum | solution.py:305
  1089.4 12.2 %collective-permute-done.35 = bf16[1,96,1792]{2,1,0:T(8,128)(2,1)S(1)} collective-permute-done((bf16[1,96,1792]{2,1,0:T(8,128)(2,1)S(1)}, bf16[1,96,1792]{2,1,0:T(8,128)(2,1)S(1)}, u32[]{:S(2)}, u32[]{:S(2)}) %collective-permute-start.35) | collective-permute-done | bytes 344096 | tf_op jit(solution)/shard_map/ppermute | solution.py:34
  (461 shorter events, 274.6 us)
Async XLA Ops:
  22.4 107.4 %collective-permute-start.16 = (bf16[1152,768]{1,0:T(8,128)(2,1)}, bf16[1152,768]{1,0:T(8,128)(2,1)}, u32[]{:S(2)}, u32[]{:S(2)}) collective-permute-start(bf16[1152,768]{1,0:T(8,128)(2,1)} %dynamic-slice_bitcast_fusion), channel_id=1, source_target_pairs={{0,2},{2,0},{1,3},{3,1},{4,6},{6,4},{5,7},{7,5},{8,10},{10,8},{9,1... | collective-permute-start | bytes 5308424 | tf_op jit(solution)/shard_map/ppermute | solution.py:20
  37.6 92.2 %collective-permute-start.22 = (bf16[768,768]{0,1:T(8,128)(2,1)}, bf16[768,768]{0,1:T(8,128)(2,1)}, u32[]{:S(2)}, u32[]{:S(2)}) collective-permute-start(bf16[768,768]{0,1:T(8,128)(2,1)} %copy.78), channel_id=1, source_target_pairs={{0,2},{2,0},{1,3},{3,1},{4,6},{6,4},{5,7},{7,5},{8,10},{10,8},{9,1... | collective-permute-start | bytes 3538952 | tf_op jit(solution)/shard_map/ppermute | solution.py:20
  40.7 89.2 %collective-permute-start.1 = (bf16[768,768]{0,1:T(8,128)(2,1)S(1)}, bf16[768,768]{0,1:T(8,128)(2,1)S(1)}, u32[]{:S(2)}, u32[]{:S(2)}) collective-permute-start(bf16[768,768]{0,1:T(8,128)(2,1)S(1)} %collective-permute-done), channel_id=1, source_target_pairs={{0,1},{1,0},{2,3},{3,2},{4,5},{5,4},{6,7},{7,6},{8,9},{9,8},{10,11... | collective-permute-start | bytes 3538952 | tf_op jit(solution)/shard_map/ppermute | solution.py:24
  72.4 93.4 %collective-permute-start.21 = (bf16[768,768]{0,1:T(8,128)(2,1)}, bf16[768,768]{0,1:T(8,128)(2,1)}, u32[]{:S(2)}, u32[]{:S(2)}) collective-permute-start(bf16[768,768]{0,1:T(8,128)(2,1)} %copy.78), channel_id=1, source_target_pairs={{0,1},{1,0},{2,3},{3,2},{4,5},{5,4},{6,7},{7,6},{8,9},{9,8},{10,11... | collective-permute-start | bytes 3538952 | tf_op jit(solution)/shard_map/ppermute | solution.py:24
  81.6 88.0 %collective-permute-start.12 = (bf16[384,2304]{1,0:T(8,128)(2,1)}, bf16[384,2304]{1,0:T(8,128)(2,1)}, u32[]{:S(2)}, u32[]{:S(2)}) collective-permute-start(bf16[384,2304]{1,0:T(8,128)(2,1)} %dynamic-slice_bitcast_fusion.2), channel_id=1, source_target_pairs={{0,2},{2,0},{1,3},{3,1},{4,6},{6,4},{5,7},{7,5},{8,10},{10,8},{9,1... | collective-permute-start | bytes 5308424 | tf_op jit(solution)/shard_map/ppermute | solution.py:20
  129.8 61.7 %collective-permute-start.14 = (bf16[384,2304]{1,0:T(8,128)(2,1)}, bf16[384,2304]{1,0:T(8,128)(2,1)}, u32[]{:S(2)}, u32[]{:S(2)}) collective-permute-start(bf16[384,2304]{1,0:T(8,128)(2,1)} %dynamic-slice_bitcast_fusion.1), channel_id=1, source_target_pairs={{0,2},{2,0},{1,3},{3,1},{4,6},{6,4},{5,7},{7,5},{8,10},{10,8},{9,1... | collective-permute-start | bytes 5308424 | tf_op jit(solution)/shard_map/ppermute | solution.py:20
  129.8 63.3 %collective-permute-start.23 = (bf16[768,768]{0,1:T(8,128)(2,1)}, bf16[768,768]{0,1:T(8,128)(2,1)}, u32[]{:S(2)}, u32[]{:S(2)}) collective-permute-start(bf16[768,768]{0,1:T(8,128)(2,1)} %collective-permute-done.22), channel_id=1, source_target_pairs={{0,1},{1,0},{2,3},{3,2},{4,5},{5,4},{6,7},{7,6},{8,9},{9,8},{10,11... | collective-permute-start | bytes 3538952 | tf_op jit(solution)/shard_map/ppermute | solution.py:24
  129.8 69.2 %collective-permute-start.17 = (bf16[1152,768]{1,0:T(8,128)(2,1)}, bf16[1152,768]{1,0:T(8,128)(2,1)}, u32[]{:S(2)}, u32[]{:S(2)}) collective-permute-start(bf16[1152,768]{1,0:T(8,128)(2,1)} %collective-permute-done.16), channel_id=1, source_target_pairs={{0,4},{4,0},{8,12},{12,8},{16,20},{20,16},{24,28},{28,24},{1,5},{5... | collective-permute-start | bytes 5308424 | tf_op jit(solution)/shard_map/ppermute | solution.py:29
  169.6 56.3 %collective-permute-start.13 = (bf16[384,2304]{1,0:T(8,128)(2,1)}, bf16[384,2304]{1,0:T(8,128)(2,1)}, u32[]{:S(2)}, u32[]{:S(2)}) collective-permute-start(bf16[384,2304]{1,0:T(8,128)(2,1)} %collective-permute-done.12), channel_id=1, source_target_pairs={{0,4},{4,0},{8,12},{12,8},{16,20},{20,16},{24,28},{28,24},{1,5},{5... | collective-permute-start | bytes 5308424 | tf_op jit(solution)/shard_map/ppermute | solution.py:29
  191.6 57.7 %collective-permute-start.15 = (bf16[384,2304]{1,0:T(8,128)(2,1)}, bf16[384,2304]{1,0:T(8,128)(2,1)}, u32[]{:S(2)}, u32[]{:S(2)}) collective-permute-start(bf16[384,2304]{1,0:T(8,128)(2,1)} %collective-permute-done.14), channel_id=1, source_target_pairs={{0,4},{4,0},{8,12},{12,8},{16,20},{20,16},{24,28},{28,24},{1,5},{5... | collective-permute-start | bytes 5308424 | tf_op jit(solution)/shard_map/ppermute | solution.py:29
  437.6 79.7 %collective-permute-start.37 = (bf16[2,4,96,2304]{3,2,0,1:T(8,128)(2,1)}, bf16[2,4,96,2304]{3,2,0,1:T(8,128)(2,1)}, u32[]{:S(2)}, u32[]{:S(2)}) collective-permute-start(bf16[2,4,96,2304]{3,2,0,1:T(8,128)(2,1)} %bitcast.208), channel_id=1, source_target_pairs={{0,4},{4,0},{8,12},{12,8},{16,20},{20,16},{24,28},{28,24},{1,5},{5... | collective-permute-start | bytes 10616840 | tf_op jit(solution)/shard_map/ppermute | solution.py:29
  476.3 116.9 %collective-permute-start.42 = (bf16[2,4,96,2304]{3,2,0,1:T(8,128)(2,1)}, bf16[2,4,96,2304]{3,2,0,1:T(8,128)(2,1)}, u32[]{:S(2)}, u32[]{:S(2)}) collective-permute-start(bf16[2,4,96,2304]{3,2,0,1:T(8,128)(2,1)} %bitcast.207), channel_id=1, source_target_pairs={{0,4},{4,0},{8,12},{12,8},{16,20},{20,16},{24,28},{28,24},{1,5},{5... | collective-permute-start | bytes 10616840 | tf_op jit(solution)/shard_map/ppermute | solution.py:29
  488.5 179.6 %collective-permute-start.47 = (bf16[2,4,96,2304]{3,2,0,1:T(8,128)(2,1)}, bf16[2,4,96,2304]{3,2,0,1:T(8,128)(2,1)}, u32[]{:S(2)}, u32[]{:S(2)}) collective-permute-start(bf16[2,4,96,2304]{3,2,0,1:T(8,128)(2,1)} %bitcast.206), channel_id=1, source_target_pairs={{0,4},{4,0},{8,12},{12,8},{16,20},{20,16},{24,28},{28,24},{1,5},{5... | collective-permute-start | bytes 10616840 | tf_op jit(solution)/shard_map/ppermute | solution.py:29
  495.0 181.3 %collective-permute-start.19 = (bf16[768,768]{0,1:T(8,128)(2,1)}, bf16[768,768]{0,1:T(8,128)(2,1)}, u32[]{:S(2)}, u32[]{:S(2)}) collective-permute-start(bf16[768,768]{0,1:T(8,128)(2,1)} %slice.332), channel_id=1, source_target_pairs={{0,2},{2,0},{1,3},{3,1},{4,6},{6,4},{5,7},{7,5},{8,10},{10,8},{9,1... | collective-permute-start | bytes 3538952 | tf_op jit(solution)/shard_map/ppermute | solution.py:20
  514.3 159.7 %collective-permute-start.26 = (f32[768]{0:T(1024)S(1)}, f32[768]{0:T(1024)}, u32[]{:S(2)}, u32[]{:S(2)}) collective-permute-start(f32[768]{0:T(1024)S(1)} %get-tuple-element.43), channel_id=1, source_target_pairs={{0,1},{1,0},{2,3},{3,2},{4,5},{5,4},{6,7},{7,6},{8,9},{9,8},{10,11... | collective-permute-start | bytes 9224 | tf_op jit(solution)/shard_map/ppermute | solution.py:24
  521.6 161.3 %collective-permute-start.38 = (bf16[2,96,2304]{2,1,0:T(8,128)(2,1)}, bf16[2,96,2304]{2,1,0:T(8,128)(2,1)S(1)}, u32[]{:S(2)}, u32[]{:S(2)}) collective-permute-start(bf16[2,96,2304]{2,1,0:T(8,128)(2,1)} %get-tuple-element.76), channel_id=1, source_target_pairs={{0,8},{4,12},{8,16},{12,20},{16,24},{20,28},{24,0},{28,4},{1,9},{5... | collective-permute-start | bytes 2654216 | tf_op jit(solution)/shard_map/ppermute | solution.py:34
  593.1 89.8 %collective-permute-start.40 = (bf16[2,96,2304]{2,1,0:T(8,128)(2,1)}, bf16[2,96,2304]{2,1,0:T(8,128)(2,1)S(1)}, u32[]{:S(2)}, u32[]{:S(2)}) collective-permute-start(bf16[2,96,2304]{2,1,0:T(8,128)(2,1)} %get-tuple-element.77), channel_id=1, source_target_pairs={{0,24},{4,28},{8,0},{12,4},{16,8},{20,12},{24,16},{28,20},{1,25},{... | collective-permute-start | bytes 2654216 | tf_op jit(solution)/shard_map/ppermute | solution.py:34
  668.1 97.3 %collective-permute-start.39 = (bf16[2,96,2304]{2,1,0:T(8,128)(2,1)S(1)}, bf16[2,96,2304]{2,1,0:T(8,128)(2,1)}, u32[]{:S(2)}, u32[]{:S(2)}) collective-permute-start(bf16[2,96,2304]{2,1,0:T(8,128)(2,1)S(1)} %get-tuple-element.78), channel_id=1, source_target_pairs={{0,16},{4,20},{8,24},{12,28},{16,0},{20,4},{24,8},{28,12},{1,17},{... | collective-permute-start | bytes 2654216 | tf_op jit(solution)/shard_map/ppermute | solution.py:34
  674.1 93.8 %collective-permute-start.43 = (bf16[2,96,2304]{2,1,0:T(8,128)(2,1)S(1)}, bf16[2,96,2304]{2,1,0:T(8,128)(2,1)S(1)}, u32[]{:S(2)}, u32[]{:S(2)}) collective-permute-start(bf16[2,96,2304]{2,1,0:T(8,128)(2,1)S(1)} %get-tuple-element.73), channel_id=1, source_target_pairs={{0,8},{4,12},{8,16},{12,20},{16,24},{20,28},{24,0},{28,4},{1,9},{5... | collective-permute-start | bytes 2654216 | tf_op jit(solution)/shard_map/ppermute | solution.py:34
  676.4 93.8 %collective-permute-start.45 = (bf16[2,96,2304]{2,1,0:T(8,128)(2,1)S(1)}, bf16[2,96,2304]{2,1,0:T(8,128)(2,1)S(1)}, u32[]{:S(2)}, u32[]{:S(2)}) collective-permute-start(bf16[2,96,2304]{2,1,0:T(8,128)(2,1)S(1)} %get-tuple-element.74), channel_id=1, source_target_pairs={{0,24},{4,28},{8,0},{12,4},{16,8},{20,12},{24,16},{28,20},{1,25},{... | collective-permute-start | bytes 2654216 | tf_op jit(solution)/shard_map/ppermute | solution.py:34
  682.9 140.9 %collective-permute-start.44 = (bf16[2,96,2304]{2,1,0:T(8,128)(2,1)S(1)}, bf16[2,96,2304]{2,1,0:T(8,128)(2,1)S(1)}, u32[]{:S(2)}, u32[]{:S(2)}) collective-permute-start(bf16[2,96,2304]{2,1,0:T(8,128)(2,1)S(1)} %get-tuple-element.75), channel_id=1, source_target_pairs={{0,16},{4,20},{8,24},{12,28},{16,0},{20,4},{24,8},{28,12},{1,17},{... | collective-permute-start | bytes 2654216 | tf_op jit(solution)/shard_map/ppermute | solution.py:34
  683.0 143.3 %collective-permute-start.48 = (bf16[2,96,2304]{2,1,0:T(8,128)(2,1)S(1)}, bf16[2,96,2304]{2,1,0:T(8,128)(2,1)S(1)}, u32[]{:S(2)}, u32[]{:S(2)}) collective-permute-start(bf16[2,96,2304]{2,1,0:T(8,128)(2,1)S(1)} %get-tuple-element.70), channel_id=1, source_target_pairs={{0,8},{4,12},{8,16},{12,20},{16,24},{20,28},{24,0},{28,4},{1,9},{5... | collective-permute-start | bytes 2654216 | tf_op jit(solution)/shard_map/ppermute | solution.py:34
  765.4 60.9 %collective-permute-start.50 = (bf16[2,96,2304]{2,1,0:T(8,128)(2,1)S(1)}, bf16[2,96,2304]{2,1,0:T(8,128)(2,1)S(1)}, u32[]{:S(2)}, u32[]{:S(2)}) collective-permute-start(bf16[2,96,2304]{2,1,0:T(8,128)(2,1)S(1)} %get-tuple-element.71), channel_id=1, source_target_pairs={{0,24},{4,28},{8,0},{12,4},{16,8},{20,12},{24,16},{28,20},{1,25},{... | collective-permute-start | bytes 2654216 | tf_op jit(solution)/shard_map/ppermute | solution.py:34
  767.9 92.7 %collective-permute-start.49 = (bf16[2,96,2304]{2,1,0:T(8,128)(2,1)S(1)}, bf16[2,96,2304]{2,1,0:T(8,128)(2,1)S(1)}, u32[]{:S(2)}, u32[]{:S(2)}) collective-permute-start(bf16[2,96,2304]{2,1,0:T(8,128)(2,1)S(1)} %get-tuple-element.72), channel_id=1, source_target_pairs={{0,16},{4,20},{8,24},{12,28},{16,0},{20,4},{24,8},{28,12},{1,17},{... | collective-permute-start | bytes 2654216 | tf_op jit(solution)/shard_map/ppermute | solution.py:34
  770.2 144.6 %collective-permute-start.20 = (bf16[768,768]{0,1:T(8,128)(2,1)}, bf16[768,768]{0,1:T(8,128)(2,1)}, u32[]{:S(2)}, u32[]{:S(2)}) collective-permute-start(bf16[768,768]{0,1:T(8,128)(2,1)} %get-tuple-element.89), channel_id=1, source_target_pairs={{0,0},{1,2},{2,1},{3,3},{4,4},{5,6},{6,5},{7,7},{8,8},{9,10},{10,9... | collective-permute-start | bytes 3538952 | tf_op jit(solution)/shard_map/ppermute | solution.py:38
  826.3 92.6 %collective-permute-start.41 = (bf16[96,2304]{1,0:T(8,128)(2,1)}, bf16[96,2304]{1,0:T(8,128)(2,1)S(1)}, u32[]{:S(2)}, u32[]{:S(2)}) collective-permute-start(bf16[96,2304]{1,0:T(8,128)(2,1)} %fusion.83), channel_id=1, source_target_pairs={{0,2},{2,0},{1,3},{3,1},{4,6},{6,4},{5,7},{7,5},{8,10},{10,8},{9,1... | collective-permute-start | bytes 1327112 | tf_op jit(solution)/shard_map/ppermute | solution.py:20
  826.3 92.8 %collective-permute-start.46 = (bf16[96,2304]{1,0:T(8,128)(2,1)}, bf16[96,2304]{1,0:T(8,128)(2,1)}, u32[]{:S(2)}, u32[]{:S(2)}) collective-permute-start(bf16[96,2304]{1,0:T(8,128)(2,1)} %fusion.84), channel_id=1, source_target_pairs={{0,2},{2,0},{1,3},{3,1},{4,6},{6,4},{5,7},{7,5},{8,10},{10,8},{9,1... | collective-permute-start | bytes 1327112 | tf_op jit(solution)/shard_map/ppermute | solution.py:20
  861.8 61.6 %collective-permute-start.51 = (bf16[96,2304]{1,0:T(8,128)(2,1)}, bf16[96,2304]{1,0:T(8,128)(2,1)}, u32[]{:S(2)}, u32[]{:S(2)}) collective-permute-start(bf16[96,2304]{1,0:T(8,128)(2,1)} %fusion.85), channel_id=1, source_target_pairs={{0,2},{2,0},{1,3},{3,1},{4,6},{6,4},{5,7},{7,5},{8,10},{10,8},{9,1... | collective-permute-start | bytes 1327112 | tf_op jit(solution)/shard_map/ppermute | solution.py:20
  912.2 74.3 %collective-permute-start.28 = (bf16[768,768]{0,1:T(8,128)(2,1)}, bf16[768,768]{0,1:T(8,128)(2,1)}, u32[]{:S(2)}, u32[]{:S(2)}) collective-permute-start(bf16[768,768]{0,1:T(8,128)(2,1)} %select_convert_fusion.1), channel_id=1, source_target_pairs={{0,1},{1,0},{2,3},{3,2},{4,5},{5,4},{6,7},{7,6},{8,9},{9,8},{10,11... | collective-permute-start | bytes 3538952 | tf_op jit(solution)/shard_map/ppermute | solution.py:24
  914.8 61.8 %collective-permute-start.31 = (bf16[768,1792]{0,1:T(8,128)(2,1)}, bf16[768,1792]{0,1:T(8,128)(2,1)}, u32[]{:S(2)}, u32[]{:S(2)}) collective-permute-start(bf16[768,1792]{0,1:T(8,128)(2,1)} %fusion.12), channel_id=1, source_target_pairs={{0,2},{2,0},{1,3},{3,1},{4,6},{6,4},{5,7},{7,5},{8,10},{10,8},{9,1... | collective-permute-start | bytes 8257544 | tf_op jit(solution)/shard_map/ppermute | solution.py:20
  984.5 89.2 %collective-permute-start.32 = (bf16[1,4,96,1792]{3,2,1,0:T(8,128)(2,1)}, bf16[1,4,96,1792]{3,2,1,0:T(8,128)(2,1)}, u32[]{:S(2)}, u32[]{:S(2)}) collective-permute-start(bf16[1,4,96,1792]{3,2,1,0:T(8,128)(2,1)} %dynamic-slice_bitcast_fusion.3), channel_id=1, source_target_pairs={{0,4},{4,0},{8,12},{12,8},{16,20},{20,16},{24,28},{28,24},{1,5},{5... | collective-permute-start | bytes 4128776 | tf_op jit(solution)/shard_map/ppermute | solution.py:29
  991.6 77.0 %collective-permute-start.29 = (f32[768]{0:T(1024)S(1)}, f32[768]{0:T(1024)S(1)}, u32[]{:S(2)}, u32[]{:S(2)}) collective-permute-start(f32[768]{0:T(1024)S(1)} %get-tuple-element.45), channel_id=1, source_target_pairs={{0,1},{1,0},{2,3},{3,2},{4,5},{5,4},{6,7},{7,6},{8,9},{9,8},{10,11... | collective-permute-start | bytes 9224 | tf_op jit(solution)/shard_map/ppermute | solution.py:24
  (138 other events, 2358.5 us)

commit v2 on v1

v2 whole, which is shorter than its diff:
```python
import functools

import jax
import jax.numpy as jnp
from jax import lax
from jax.experimental import pallas as pl
from jax.experimental.pallas import tpu as pltpu
from jax.sharding import PartitionSpec as P

D = 1536
HQ = 12
KVH = 2
HD = 128
LANES = 128
PARTS = 4
TILE = 256
WIDE_TILE = 384
MIB = 1024 * 1024
SCALE = 10.0

EPS = 1e-06
THETA = 1000000.0
BF = jnp.bfloat16
F32 = jnp.float32

SAME, INNER, START, START_FAR, SKIP, OWN, PAIR, NEAR, ACROSS, ROW = range(10)


def swap_row(value):
    return lax.ppermute(value, "row", [(0, 1), (1, 0)])


def swap_col(value):
    return lax.ppermute(value, "col", [(0, 1), (1, 0)])


def swap_bit(value, bit):
    size = lax.axis_size("dp")
    return lax.ppermute(value, "dp", [(i, i ^ (1 << bit)) for i in range(size)])


def trade_col(value):
    return lax.all_to_all(value, "col", 0, 0)


def turn_square(value):
    return lax.ppermute(value, ("row", "col"), [(0, 0), (1, 2), (2, 1), (3, 3)])


def pick(array, index, axis=0):
    return lax.dynamic_index_in_dim(array, index, axis, keepdims=False)


ANY = pl.BlockSpec(memory_space=pl.ANY)
SCALARS = pl.BlockSpec(memory_space=pltpu.SMEM)
WHOLE = pl.BlockSpec(memory_space=pltpu.VMEM)


def shape(dims, dtype):
    return jax.ShapeDtypeStruct(dims, dtype)


def cost(flops, moved=0, exps=0):
    return pl.CostEstimate(
        flops=int(flops * SCALE), bytes_accessed=int(moved * SCALE), transcendentals=int(exps * SCALE)
    )


def run(kernel, ins, outs, after=(), grid=None, out_specs=None, scratch=(), limit=56, aliases=None,
        estimate=None, name=None):
    given = len(ins)
    count = len(outs)

    def body(*refs):
        kernel(*refs[:given], *refs[given + len(after):])

    return pl.pallas_call(
        body,
        grid=grid if grid is not None else (),
        in_specs=[spec for _, spec in ins] + [ANY] * len(after),
        out_specs=out_specs if out_specs is not None else [WHOLE] * count,
        out_shape=outs,
        scratch_shapes=list(scratch),
        input_output_aliases=aliases or {},
        cost_estimate=estimate,
        name=name,
        compiler_params=pltpu.CompilerParams(vmem_limit_bytes=limit * MIB),
    )(*[array for array, _ in ins], *after)


def dot(left, right):
    return jnp.dot(left, right, preferred_element_type=F32)


def dot_right(left, right):
    return lax.dot_general(left, right, (((1,), (1,)), ((), ())), preferred_element_type=F32)


def dot_left(left, right):
    return lax.dot_general(left, right, (((0,), (0,)), ((), ())), preferred_element_type=F32)


def copies(pairs, sems):
    started = [pltpu.make_async_copy(src, dst, sems.at[i]) for i, (src, dst) in enumerate(pairs)]
    for one in started:
        one.start()
    for one in started:
        one.wait()


def rows_at(start, size):
    return pl.ds(pl.multiple_of(start, 16), size)


def lanes_at(start, size):
    return pl.ds(pl.multiple_of(start, LANES), size)


def pack_weights(scalars, arrays, part, dims, place, after=(), down=False, scale=1, chunk=0):
    def kernel(s, *refs):
        srcs, out, sems = refs[: len(arrays)], refs[len(arrays)], refs[len(arrays) + 1]
        start = (s[place] * scale + chunk) * dims[0]
        pairs = []
        at = 0
        for src in srcs:
            if down:
                pairs.append((src.at[rows_at(s[START_FAR] + start, dims[0]), :], out))
            elif part is not None:
                pairs.append((src.at[rows_at(start, dims[0]), lanes_at(s[START_FAR], part)],
                              out.at[:, at:at + part]))
                at += part
            else:
                wide = src.shape[1]
                pairs.append((src.at[rows_at(start, dims[0]), :], out.at[:, at:at + wide]))
                at += wide
        copies(pairs, sems)

    return run(kernel, [(scalars, SCALARS)] + [(a, ANY) for a in arrays], [shape(dims, BF)],
               after=after, scratch=[pltpu.SemaphoreType.DMA((len(arrays),))], limit=48,
               estimate=cost(0, 4 * dims[0] * dims[1]), name="pack")[0]


QUARTERS = 5
HALVES = 2
CHUNKED = 4


def placed(s, fetched, at, total):
    if len(fetched) in (HALVES, CHUNKED):
        chunks = len(fetched) // 2
        size = total // 2
        step = size // chunks
        rows = [rows_at(at + half * size + i * step, step)
                for i in range(chunks) for half in (s[INNER], 1 - s[INNER])]
    else:
        size = total // 4
        rows = [rows_at(at + s[place] * size, size) for place in (OWN, PAIR, NEAR)]
        rows += [rows_at(at + s[ACROSS] * size + i * (size // 2), size // 2) for i in range(2)]
    return list(zip(fetched, rows))


def project(scalars, mine, other, gain, gain_far, w_query, w_key, w_value, fetched, bias, cosine,
            sine, after=()):
    length, width = mine.shape
    qw, kw = w_query.shape[1], w_key.shape[1]
    total = qw + 2 * kw

    def kernel(s, mine, other, gain, gain_far, wq, wk, wv, *refs):
        fetched, (bias, cosine, sine, q, k, v, a, r, w) = refs[:QUARTERS], refs[QUARTERS:]
        x = mine[...].astype(F32)
        y = other[...].astype(F32)
        squares = jnp.sum(x * x, axis=1, keepdims=True) + jnp.sum(y * y, axis=1, keepdims=True)
        rstd = lax.rsqrt(squares / D + EPS)
        r[...] = rstd

        @pl.when(s[SAME] == 1)
        def _():
            a[:, :width] = (x * rstd * gain[...]).astype(BF)
            a[:, width:] = (y * rstd * gain_far[...]).astype(BF)

        @pl.when(s[SAME] == 0)
        def _():
            a[:, :width] = (y * rstd * gain[...]).astype(BF)
            a[:, width:] = (x * rstd * gain_far[...]).astype(BF)

        w[:width, :qw] = wq[...]
        w[:width, qw:qw + kw] = wk[...]
        w[:width, qw + kw:] = wv[...]
        for piece, rows in placed(s, fetched, width, width):
            w[rows, :] = piece[...]
        out = dot(a[...], w[...]) + bias[...]
        c, t = cosine[...], sine[...]
        for head in range(qw // HD):
            u = out[:, head * HD:(head + 1) * HD]
            q[:, head * HD:(head + 1) * HD] = (u * c + pltpu.roll(u, HD // 2, 1) * t).astype(BF)
        for head in range(kw // HD):
            u = out[:, qw + head * HD:qw + (head + 1) * HD]
            k[:, head * HD:(head + 1) * HD] = (u * c + pltpu.roll(u, HD // 2, 1) * t).astype(BF)
        v[...] = out[:, qw + kw:].astype(BF)

    arrays = [mine, other, gain, gain_far, w_query, w_key, w_value, *fetched, bias, cosine, sine]
    return run(kernel, [(scalars, SCALARS)] + [(a, WHOLE) for a in arrays],
               [shape((length, qw), BF), shape((length, kw), BF), shape((length, kw), BF),
                shape((length, 2 * width), BF), shape((length, 1), F32)], after=after,
               scratch=[pltpu.VMEM((2 * width, total), BF)],
               estimate=cost(2 * length * 2 * width * total, 12 * MIB), name="qkv")


def allowed_keys(seg_col, seg_row, start, size, keys):
    rows = lax.broadcasted_iota(jnp.int32, (size, keys), 0) + start
    cols = lax.broadcasted_iota(jnp.int32, (size, keys), 1)
    return (seg_col[start:start + size, :] == seg_row[:, :keys]) & (cols <= rows)


def attend(scalars, q, k, v, seg_col, seg_row, w_out, fetched, after=()):
    length, qw = q.shape
    heads, pairs = qw // HD, k.shape[1] // HD
    width = w_out.shape[1]

    def kernel(s, q, k, v, seg_col, seg_row, w_out, *refs):
        fetched, (o, lse, part, w) = refs[:QUARTERS], refs[QUARTERS:]
        for start in range(0, length, TILE):
            keys = start + TILE
            allowed = allowed_keys(seg_col, seg_row, start, TILE, keys)
            rows = slice(start, start + TILE)
            for head in range(heads):
                pair = head // (heads // pairs)
                place = slice(head * HD, (head + 1) * HD)
                mine = slice(pair * HD, (pair + 1) * HD)
                scores = dot_right(q[rows, place], k[:keys, mine]) * HD ** (-0.5)
                scores = jnp.where(allowed, scores, -1e30)
                top = jnp.max(scores, axis=1, keepdims=True)
                raised = jnp.exp(scores - top)
                total = jnp.sum(raised, axis=1, keepdims=True)
                weights = (raised * (1.0 / total)).astype(BF)
                o[rows, place] = dot(weights, v[:keys, mine]).astype(BF)
                lse[rows, head:head + 1] = top + jnp.log(total)
        w[:, :width] = w_out[...]
        for piece, rows in placed(s, fetched, 0, qw):
            w[rows, width:] = piece[...]
        value = dot(o[...], w[...]).astype(BF)
        part[0] = value
        part[1] = value

    arrays = [q, k, v, seg_col, seg_row, w_out, *fetched]
    return run(kernel, [(scalars, SCALARS)] + [(a, WHOLE) for a in arrays],
               [shape((length, qw), BF), shape((length, LANES), F32), shape((2, length, 2 * width), BF)],
               after=after,
               scratch=[pltpu.VMEM((qw, 2 * width), BF)],
               estimate=cost(4 * length * length * qw + 2 * length * qw * 2 * width, 12 * MIB,
                             heads * length * length), name="attention")


def tiled(array, tile):
    return array, pl.BlockSpec((tile, array.shape[1]), lambda i: (i, 0))


def both_tiled(array, tile):
    return array, pl.BlockSpec((2, tile, array.shape[2]), lambda i: (0, i, 0))


def fixed(array):
    return array, pl.BlockSpec(array.shape, lambda i: (0, 0))


def norm_two(scalars, mine, other, parts, gain, gain_far, after=()):
    length, width = mine.shape

    def kernel(s, mine, other, parts, gain, gain_far, h, near, far, r):
        added = parts[0].astype(F32) + parts[1].astype(F32)

        def fill(first, second):
            h[:, :width] = first[...].astype(F32) + added[:, :width]
            h[:, width:] = second[...].astype(F32) + added[:, width:]

        pl.when(s[SAME] == 1)(lambda: fill(mine, other))
        pl.when(s[SAME] == 0)(lambda: fill(other, mine))
        rstd = lax.rsqrt(jnp.sum(h[...] * h[...], axis=1, keepdims=True) / D + EPS)
        r[...] = rstd
        first = (h[:, :width] * rstd * gain[...]).astype(BF)
        second = (h[:, width:] * rstd * gain_far[...]).astype(BF)

        @pl.when(s[SAME] == 1)
        def _():
            near[...] = first
            far[...] = second

        @pl.when(s[SAME] == 0)
        def _():
            near[...] = second
            far[...] = first

    tile = TILE // 2
    outs = [shape((length, 2 * width), F32), shape((length, width), BF), shape((length, width), BF),
            shape((length, 1), F32)]
    return run(kernel, [(scalars, SCALARS)] + [tiled(mine, tile), tiled(other, tile), both_tiled(parts, tile)]
               + [fixed(gain), fixed(gain_far)], outs, after=after, grid=(length // tile,),
               out_specs=[tiled(o, tile)[1] for o in outs],
               estimate=cost(length * width * 20, 16 * MIB), name="norm_two")


def gate_up(scalars, pieces, w_gate, w_up, fetched, first, total, part, kept=None, after=()):
    width = pieces[0][0].shape[1]
    counts = [near.shape[0] // WIDE_TILE for near, _ in pieces]
    steps = sum(counts)
    offset = first // WIDE_TILE
    starts = [sum(counts[:i]) for i in range(len(counts))]

    def kernel(s, *refs):
        halves = refs[:2 * len(pieces)]
        wg, wu, *fetched = refs[2 * len(pieces):2 * len(pieces) + 2 + CHUNKED]
        b, z, up_slope, gate_slope, w, sems = refs[-6:]
        step = pl.program_id(0)

        @pl.when(step == 0)
        def _():
            load_gate_up(s, wg, wu, fetched, w, sems, part, width)

        def fill(near, far):
            @pl.when(s[SAME] == 1)
            def _():
                b[:, :width] = near[...]
                b[:, width:] = far[...]

            @pl.when(s[SAME] == 0)
            def _():
                b[:, :width] = far[...]
                b[:, width:] = near[...]

        for i in range(len(pieces)):
            pl.when((step >= starts[i]) & (step < starts[i] + counts[i]))(
                functools.partial(fill, halves[2 * i], halves[2 * i + 1])
            )

        both = dot(b[...], w[...])
        gate, upward = both[:, :part], both[:, part:]
        counted = lax.broadcasted_iota(jnp.int32, gate.shape, 1) >= s[SKIP]
        sigma = 1.0 / (1.0 + jnp.exp(-gate))
        sigma = jnp.where(counted, sigma, 0.0)
        silu = gate * sigma
        z[...] = (silu * upward).astype(BF)
        up_slope[...] = silu.astype(BF)
        gate_slope[...] = (upward * sigma * (1.0 + gate * (1.0 - sigma))).astype(BF)

    def block(start, count):
        return pl.BlockSpec((WIDE_TILE, width), lambda i: (jnp.clip(i - start, 0, count - 1), 0))

    ins = [(scalars, SCALARS)]
    for pair, start, count in zip(pieces, starts, counts):
        ins += [(array, block(start, count)) for array in pair]
    ins += [(array, ANY) for array in (w_gate, w_up, *fetched)]
    aliases = {}
    if kept is not None:
        aliases = {len(ins) + i: i for i in range(4)}
        ins += [(array, ANY) for array in kept]
    at = lambda i: (i + offset, 0)
    length = steps * WIDE_TILE
    return run(kernel, ins,
               [shape((total, 2 * width), BF)] + [shape((total, part), BF)] * 3,
               after=after, grid=(steps,),
               out_specs=[pl.BlockSpec((WIDE_TILE, 2 * width), at)]
               + [pl.BlockSpec((WIDE_TILE, part), at)] * 3,
               scratch=[pltpu.VMEM((2 * width, 2 * part), BF), pltpu.SemaphoreType.DMA((2 + CHUNKED,))],
               aliases=aliases,
               estimate=cost(8 * length * width * part, 12 * MIB + length * 12000, length * part),
               name="gate_up")


def load_gate_up(s, wg, wu, fetched, w, sems, part, width):
    lanes = lanes_at(s[START], part)
    copies([(wg.at[:, lanes], w.at[:width, :part]), (wu.at[:, lanes], w.at[:width, part:])]
           + [(piece, w.at[rows, :]) for piece, rows in placed(s, fetched, width, width)], sems)


def place_rows(scalars, pieces, after=()):
    length, width = pieces[0][0][0].shape
    flat = [array for group in pieces for pair in group for array in pair]

    def kernel(s, *refs):
        srcs, out, sems = refs[:len(flat)], refs[len(flat)], refs[len(flat) + 1]
        pairs = []
        for i, src in enumerate(srcs):
            group, side, token = i // 4, (i // 2) % 2, i % 2
            place = jnp.where(s[SAME] == 1, token, 1 - token) * length
            pairs.append((src, out.at[rows_at(2 * group * length + place, length),
                                      side * width:(side + 1) * width]))
        copies(pairs, sems)

    return run(kernel, [(scalars, SCALARS)] + [(a, ANY) for a in flat],
               [shape((2 * len(pieces) * length, 2 * width), BF)], after=after,
               scratch=[pltpu.SemaphoreType.DMA((len(flat),))], limit=48,
               estimate=cost(0, 16 * len(flat) * length * width // 4), name="place_rows")[0]


def copy_of(array, after):
    def kernel(src, out, sem):
        copies([(src, out)], sem)

    return run(kernel, [(array, ANY)], [shape(array.shape, array.dtype)], after=after,
               scratch=[pltpu.SemaphoreType.DMA((1,))], limit=48,
               estimate=cost(0, 4 * array.size), name="copy_of")[0]


def hold(array, *after):
    if not after:
        return array

    def kernel(src, out):
        pass

    return run(kernel, [(array, ANY)], [shape(array.shape, array.dtype)], after=after, out_specs=[ANY],
               aliases={0: 0}, limit=48, estimate=cost(0, 0), name="hold")[0]


def load_down(s, w_down, fetched, w, sems, part, width):
    copies([(w_down.at[rows_at(s[START], part), :], w.at[:, :width])]
           + [(piece, w.at[rows, width:]) for piece, rows in placed(s, fetched, 0, part)], sems)


def hidden_back(scalars, cot, up_slope, gate_slope, w_down, fetched, after=()):
    total, width = cot.shape[0], cot.shape[1] // 2
    part = up_slope.shape[1]

    def kernel(s, g, up_slope, gate_slope, w_down, *refs):
        fetched, (out, w, sems) = refs[:HALVES], refs[HALVES:]

        @pl.when(pl.program_id(0) == 0)
        def _():
            load_down(s, w_down, fetched, w, sems, part, width)

        back = dot_right(g[...], w[...])
        out[:, :part] = (back * gate_slope[...].astype(F32)).astype(BF)
        out[:, part:] = (back * up_slope[...].astype(F32)).astype(BF)

    at = lambda i: (i, 0)
    tile = 2 * TILE
    return run(kernel,
               [(scalars, SCALARS), (cot, pl.BlockSpec((tile, 2 * width), at)),
                (up_slope, pl.BlockSpec((tile, part), at)), (gate_slope, pl.BlockSpec((tile, part), at)),
                (w_down, ANY)] + [(piece, ANY) for piece in fetched],
               [shape((total, 2 * part), BF)], after=after, grid=(total // tile,),
               out_specs=[pl.BlockSpec((tile, 2 * part), at)],
               scratch=[pltpu.VMEM((part, 2 * width), BF), pltpu.SemaphoreType.DMA((1 + HALVES,))],
               estimate=cost(4 * total * width * part, total * 14000), name="hidden_back")[0]


def split_store(s, value, keep, send, width):
    first, second = value[:, :width].astype(BF), value[:, width:].astype(BF)

    @pl.when(s[SAME] == 1)
    def _():
        keep[...] = first
        send[...] = second

    @pl.when(s[SAME] == 0)
    def _():
        keep[...] = second
        send[...] = first


def norm_back(scalars, low, w_gate, w_up, fetched, first, length, after=(), stacked=False):
    width = w_gate.shape[0]
    part = low.shape[1] // 2
    offset = first // WIDE_TILE

    def kernel(s, low, wg, wu, *refs):
        fetched, (*outs, w, sems) = refs[:CHUNKED], refs[CHUNKED:]

        @pl.when(pl.program_id(0) == 0)
        def _():
            load_gate_up(s, wg, wu, fetched, w, sems, part, width)

        value = dot_right(low[...], w[...])
        if stacked:
            outs[0][s[ROW]] = value[:, :width].astype(BF)
            outs[0][1 - s[ROW]] = value[:, width:].astype(BF)
        else:
            split_store(s, value, *outs, width)

    tiles = [pl.BlockSpec((WIDE_TILE, width), lambda i: (i, 0))] * 2
    outs = [shape((length, width), BF)] * 2
    if stacked:
        outs = [shape((2, length, width), BF)]
        tiles = [pl.BlockSpec((2, WIDE_TILE, width), lambda i: (0, i, 0))]
    return run(kernel,
               [(scalars, SCALARS), (low, pl.BlockSpec((WIDE_TILE, 2 * part), lambda i: (i + offset, 0))),
                (w_gate, ANY), (w_up, ANY)] + [(piece, ANY) for piece in fetched],
               outs, after=after, grid=(length // WIDE_TILE,), out_specs=tiles,
               scratch=[pltpu.VMEM((2 * width, 2 * part), BF), pltpu.SemaphoreType.DMA((2 + CHUNKED,))],
               estimate=cost(8 * length * width * part, 8 * MIB + length * 8000), name="norm_back")


def down_project(scalars, hidden, w_down, fetched, after=()):
    total, part = hidden.shape
    width = w_down.shape[1]

    def kernel(s, z, w_down, *refs):
        fetched, (keep, send, w, sems) = refs[:HALVES], refs[HALVES:]

        @pl.when(pl.program_id(0) == 0)
        def _():
            load_down(s, w_down, fetched, w, sems, part, width)

        split_store(s, dot(z[...], w[...]), keep, send, width)

    at = lambda i: (i, 0)
    tile = 2 * TILE
    return run(kernel,
               [(scalars, SCALARS), (hidden, pl.BlockSpec((tile, part), at)), (w_down, ANY)]
               + [(piece, ANY) for piece in fetched],
               [shape((total, width), BF)] * 2, after=after, grid=(total // tile,),
               out_specs=[pl.BlockSpec((tile, width), at)] * 2,
               scratch=[pltpu.VMEM((part, 2 * width), BF), pltpu.SemaphoreType.DMA((1 + HALVES,))],
               estimate=cost(4 * total * width * part, total * 8000), name="down_project")


def weight_grad(scalars, left, right, piece, columns, place=0, after=()):
    tokens, width = left.shape[0], left.shape[1] // 2
    groups = width // (2 * piece)

    def kernel(s, left, right, keep, send):
        value = dot_left(left[...], right[...]).astype(BF).reshape(groups, 2, piece, columns)

        @pl.when(s[INNER] == 0)
        def _():
            keep[0] = value[:, 0]
            send[0] = value[:, 1]

        @pl.when(s[INNER] == 1)
        def _():
            keep[0] = value[:, 1]
            send[0] = value[:, 0]

    block = pl.BlockSpec((1, groups, piece, columns), lambda i: (i, 0, 0, 0))
    return run(kernel,
               [(scalars, SCALARS), (left, pl.BlockSpec((tokens, width), lambda i: (0, i))),
                (right, pl.BlockSpec((tokens, columns), lambda i: (0, place)))],
               [shape((2, groups, piece, columns), BF)] * 2, after=after, grid=(2,),
               out_specs=[block, block],
               estimate=cost(4 * tokens * width * columns, tokens * (4 * width + 4 * columns)),
               name="weight_grad")


def small_grad(left, right, after=()):
    tokens, width = left.shape[0], left.shape[1] // 2
    columns = right.shape[1]

    def kernel(left, right, keep, send):
        send[...] = dot_left(left[:, width:], right[...]).astype(BF)
        keep[...] = dot_left(left[:, :width], right[...]).astype(BF)

    return run(kernel, [(left, WHOLE), (right, WHOLE)], [shape((width, columns), BF)] * 2, after=after,
               estimate=cost(4 * tokens * width * columns, 8 * MIB), name="small_grad")


def middle_back(scalars, both, h, r, gain, gain_far, cot, after=()):
    _, length, width = both.shape

    def kernel(s, both, h, r, gain, gain_far, g, dh, low, gain_part, db):
        def fill(first, second):
            db[:, :width] = first.astype(F32)
            db[:, width:] = second.astype(F32)

        pl.when(s[ROW] == 0)(lambda: fill(both[0], both[1]))
        pl.when(s[ROW] == 1)(lambda: fill(both[1], both[0]))
        rstd = r[...]
        normed = h[...] * rstd
        gains = jnp.concatenate([gain[...], gain_far[...]], axis=1)

        @pl.when(pl.program_id(0) == 0)
        def _():
            gain_part[...] = jnp.zeros_like(gain_part)

        gain_part[...] += jnp.sum(db[...] * normed, axis=0, keepdims=True)
        scaled = db[...] * gains
        mean = jnp.sum(scaled * normed, axis=1, keepdims=True) / D
        value = g[...].astype(F32) + rstd * (scaled - normed * mean)
        dh[...] = value
        low[...] = value.astype(BF)

    tile = TILE // 2
    outs = [shape((length, 2 * width), F32), shape((length, 2 * width), BF), shape((1, 2 * width), F32)]
    return run(kernel, [(scalars, SCALARS)] + [both_tiled(both, tile), tiled(h, tile), tiled(r, tile)]
               + [fixed(gain), fixed(gain_far), tiled(cot, tile)], outs, after=after,
               grid=(length // tile,),
               out_specs=[tiled(o, tile)[1] for o in outs[:2]] + [fixed(outs[2])[1]],
               scratch=[pltpu.VMEM((tile, 2 * width), F32)],
               estimate=cost(length * width * 30, 20 * MIB), name="middle_back")


def attend_back(scalars, low, q, k, v, lse, seg_col, seg_row, w_out, out_fetched, w_query, w_key, w_value,
                qkv_fetched, cosine, sine, after=()):
    length, qw = q.shape
    kw = k.shape[1]
    heads, pairs = qw // HD, kw // HD
    width = w_out.shape[1]
    total = qw + 2 * kw

    def kernel(s, low, q, k, v, lse, seg_col, seg_row, w_out, *refs):
        out_fetched, (wq, wk, wv), refs = refs[:QUARTERS], refs[QUARTERS:QUARTERS + 3], refs[QUARTERS + 3:]
        fetched, (cosine, sine, back, part, bias, wo, w, do, dk, dv) = refs[:QUARTERS], refs[QUARTERS:]
        wo[:, :width] = w_out[...]
        for piece, rows in placed(s, out_fetched, 0, qw):
            wo[rows, width:] = piece[...]
        do[...] = dot_right(low[...], wo[...]).astype(BF)
        dk[...] = jnp.zeros_like(dk)
        dv[...] = jnp.zeros_like(dv)
        for start in range(0, length, TILE):
            keys = start + TILE
            allowed = allowed_keys(seg_col, seg_row, start, TILE, keys)
            rows = slice(start, start + TILE)
            c, t = cosine[rows, :], sine[rows, :]
            for head in range(heads):
                pair = head // (heads // pairs)
                place = slice(head * HD, (head + 1) * HD)
                mine = slice(pair * HD, (pair + 1) * HD)
                scores = dot_right(q[rows, place], k[:keys, mine]) * HD ** (-0.5)
                probs = jnp.where(allowed, jnp.exp(scores - lse[rows, head:head + 1]), 0.0)
                grads = dot_right(do[rows, place], v[:keys, mine])
                delta = jnp.sum(probs * grads, axis=1, keepdims=True)
                score_grad = (probs * (grads - delta)).astype(BF)
                dv[:keys, mine] += dot_left(probs.astype(BF), do[rows, place])
                dk[:keys, mine] += dot_left(score_grad, q[rows, place])
                u = dot(score_grad, k[:keys, mine]) * HD ** (-0.5)
                back[rows, place] = (u * c - pltpu.roll(u, HD // 2, 1) * t).astype(BF)
        for pair in range(pairs):
            u = dk[:, pair * HD:(pair + 1) * HD] * HD ** (-0.5)
            u = u * cosine[...] - pltpu.roll(u, HD // 2, 1) * sine[...]
            back[:, qw + pair * HD:qw + (pair + 1) * HD] = u.astype(BF)
        back[:, qw + kw:] = dv[...].astype(BF)
        w[:width, :qw] = wq[...]
        w[:width, qw:qw + kw] = wk[...]
        w[:width, qw + kw:] = wv[...]
        for piece, rows in placed(s, fetched, width, width):
            w[rows, :] = piece[...]
        value = dot_right(back[...], w[...]).astype(BF)
        part[0] = value
        part[1] = value
        bias[...] = jnp.sum(back[...].astype(F32), axis=0, keepdims=True)

    arrays = [low, q, k, v, lse, seg_col, seg_row, w_out, *out_fetched, w_query, w_key, w_value,
              *qkv_fetched, cosine, sine]
    return run(kernel, [(scalars, SCALARS)] + [(a, WHOLE) for a in arrays],
               [shape((length, total), BF), shape((2, length, 2 * width), BF), shape((1, total), F32)],
               after=after,
               scratch=[pltpu.VMEM((qw, 2 * width), BF), pltpu.VMEM((2 * width, total), BF),
                        pltpu.VMEM((length, qw), BF), pltpu.VMEM((length, kw), F32),
                        pltpu.VMEM((length, kw), F32)],
               estimate=cost(10 * length * length * qw + 2 * length * 2 * width * (qw + total), 20 * MIB,
                             heads * length * length), name="attention_back")


def input_back(scalars, parts, mine, other, r, gain, gain_far, dh, after=()):
    length, width = mine.shape

    def kernel(s, parts, mine, other, r, dh, gain, gain_far, out, gain_part, n):
        def fill(first, second):
            n[:, :width] = first[...].astype(F32) * r[...]
            n[:, width:] = second[...].astype(F32) * r[...]

        pl.when(s[SAME] == 1)(lambda: fill(mine, other))
        pl.when(s[SAME] == 0)(lambda: fill(other, mine))
        da = parts[0].astype(F32) + parts[1].astype(F32)
        normed = n[...]

        @pl.when(pl.program_id(0) == 0)
        def _():
            gain_part[...] = jnp.zeros_like(gain_part)

        gain_part[...] += jnp.sum(da * normed, axis=0, keepdims=True)
        scaled = da * jnp.concatenate([gain[...], gain_far[...]], axis=1)
        mean = jnp.sum(scaled * normed, axis=1, keepdims=True) / D
        value = (dh[...] + r[...] * (scaled - normed * mean)).astype(BF)

        @pl.when(s[SAME] == 1)
        def _():
            out[...] = value[:, :width]

        @pl.when(s[SAME] == 0)
        def _():
            out[...] = value[:, width:]

    tile = TILE // 2
    outs = [shape((length, width), BF), shape((1, 2 * width), F32)]
    return run(kernel, [(scalars, SCALARS)] + [both_tiled(parts, tile)] + [tiled(a, tile) for a in (mine, other, r, dh)]
               + [fixed(gain), fixed(gain_far)], outs, after=after, grid=(length // tile,),
               out_specs=[tiled(outs[0], tile)[1], fixed(outs[1])[1]],
               scratch=[pltpu.VMEM((tile, 2 * width), F32)],
               estimate=cost(length * width * 30, 16 * MIB), name="input_back")


def body(
    inputs,
    segments,
    positions,
    w_query,
    w_key,
    w_value,
    b_query,
    b_key,
    b_value,
    w_out,
    gain_one,
    gain_two,
    w_gate,
    w_up,
    w_down,
    cotangent,
):
    length, width = inputs.shape
    query_width = w_query.shape[1]
    key_width = w_key.shape[1]
    total_width = query_width + 2 * key_width
    row = lax.axis_index("row")
    col = lax.axis_index("col")
    group = lax.axis_index("dp")
    groups = lax.axis_size("dp")
    inner = group % 2
    near_bit = (group // 2) % 2
    same = row == col

    hidden_here = w_gate.shape[1]
    blocks = hidden_here // LANES
    wide = -(-blocks // PARTS)
    part = wide * LANES
    overlap = PARTS * part - hidden_here

    def start_of(index):
        return jnp.minimum(index * wide, blocks - wide) * LANES

    mine_part = near_bit * 2 + row
    place_of = lambda low, high: 2 * low + high
    scalars = jnp.stack(
        [same.astype(jnp.int32), inner, start_of(mine_part), start_of(near_bit * 2 + 1 - row),
         jnp.where(mine_part == PARTS - 1, overlap, 0), place_of(inner, near_bit),
         place_of(1 - inner, near_bit), place_of(inner, 1 - near_bit), place_of(1 - inner, 1 - near_bit), row]
    ).astype(jnp.int32)

    def by_row(mine, other):
        return jnp.where(same, mine, other), jnp.where(same, other, mine)

    half = width // 2
    gains = jnp.stack([gain_one, gain_two])
    fetched_gains = swap_row(gains)
    mine = turn_square(inputs)
    sent_qkv = pack_weights(scalars, [w_query, w_key, w_value], None, (width // 4, total_width), OWN)
    qkv_direct = swap_row(sent_qkv)
    cot_near = swap_bit(cotangent, 1)
    mine = hold(mine, sent_qkv)
    other = swap_col(mine)
    sent_out = pack_weights(
        scalars, [w_out], None, (query_width // 4, width), OWN, after=[qkv_direct]
    )
    out_direct = swap_row(sent_out)
    sent_gu = []
    for chunk in range(2):
        sent_gu.append(pack_weights(
            scalars, [w_gate, w_up], part, (width // 4, 2 * part), INNER, scale=2, chunk=chunk,
            after=[out_direct, fetched_gains] + sent_gu,
        ))
    gu_direct = [swap_row(sent) for sent in sent_gu]
    fetched_gains = fetched_gains.astype(F32)
    gains = gains.astype(F32)

    def relay_far(direct, pair, near, *after):
        pair, near = hold(pair, *after), hold(near, *after)
        cut = direct.shape[0] // 2
        return direct, pair, near, swap_bit(pair[:cut], 1), swap_bit(near[cut:], 0)

    def relay_near(direct):
        return direct, swap_bit(direct, 0), swap_bit(direct, 1)

    cot_near = hold(cot_near, sent_gu[1])
    qkv_fetched = relay_far(*relay_near(qkv_direct), sent_gu[1])
    out_fetched = relay_far(*relay_near(out_direct), sent_gu[1])

    indices = jnp.arange(HD // 2, dtype=F32)
    inverse = jnp.exp(indices * (-2.0 / HD) * jnp.log(F32(THETA)))
    turned = positions.astype(F32)[:, None] * inverse[None, :]
    cosine, sine = jnp.cos(turned), jnp.sin(turned)
    cosine = jnp.concatenate([cosine, cosine], axis=1)
    sine = jnp.concatenate([-sine, sine], axis=1)
    bias = jnp.concatenate([b_query, b_key, b_value]).astype(F32)[None, :]
    seg_col, seg_row = segments[:, None], segments[None, :]

    q, k, v, low_one, r_one = project(
        scalars, mine, other, gains[:1], fetched_gains[:1], w_query, w_key, w_value, qkv_fetched,
        bias, cosine, sine, after=sent_gu[1:] + [cot_near],
    )

    gu_first = hold(gu_direct[0], k)
    gu_fetched = [gu_first, swap_bit(gu_first, 0)]
    cot = copy_of(cotangent, after=[k])
    cot_row = swap_row(cot)
    attended, lse, out_part = attend(scalars, q, k, v, seg_col, seg_row, w_out, out_fetched, after=[gu_first, cot])
    gu_second = hold(gu_direct[1], lse)
    gu_fetched += [gu_second, swap_bit(gu_second, 0)]
    h, low_near, low_far, r_two = norm_two(
        scalars, mine, other, trade_col(hold(out_part, gu_second)), gains[1:], fetched_gains[1:],
        after=[gu_fetched[1]],
    )

    b_row = swap_row(low_near)
    b_near = swap_bit(low_near, 1)
    cot_row = hold(cot_row, low_near)
    cot_low = swap_bit(cot_row[:half], 1)
    tokens = 4 * length
    ffn = functools.partial(
        gate_up, scalars, w_gate=w_gate, w_up=w_up, fetched=gu_fetched, total=tokens, part=part,
    )
    kept = ffn([(low_near, low_far)], first=0, after=[cot_row])
    b_row, b_near = hold(b_row, kept[1]), hold(b_near, kept[1])
    b_row_other, b_near_other = swap_col(b_row), swap_col(b_near)
    b_low = swap_bit(b_row[:half], 1)
    b_high = swap_row(b_near[half:])
    cot_near = hold(cot_near, b_near_other)
    cot_high = swap_row(cot_near[half:])
    sent_down = pack_weights(
        scalars, [w_down], None, (part // 2, width), INNER, after=[cot_near], down=True
    )
    down_direct = swap_row(sent_down)
    kept = ffn([(b_row, b_row_other), (b_near, b_near_other)], first=length, kept=kept, after=[sent_down])
    b_low, b_high, cot_low, cot_high, down_direct = (
        hold(array, kept[1]) for array in (b_low, b_high, cot_low, cot_high, down_direct)
    )
    down_fetched = down_direct, swap_bit(down_direct, 0)
    cot_far = jnp.concatenate([cot_low, cot_high], axis=0)
    cot_pieces = [[(one, swap_col(one)) for one in pair] for pair in ((cot, cot_row), (cot_near, cot_far))]
    kept = ffn([(b_low, swap_col(b_low)), (b_high, swap_col(b_high))], first=3 * length, kept=kept)
    full_two, hidden, up_slope, gate_slope = kept
    full_cot = place_rows(scalars, cot_pieces, after=[hidden])

    piece = width // groups
    down_keep, down_send = weight_grad(scalars, full_cot, hidden, piece, part)
    low_back = hidden_back(
        scalars, full_cot, up_slope, gate_slope, w_down, down_fetched, after=[down_send]
    )
    back = functools.partial(
        norm_back, scalars, low_back, w_gate, w_up, gu_fetched
    )

    def sum_far(keep, send):
        across = (keep.astype(F32) + send.astype(F32)).astype(BF)
        return across[:half], across[half:]

    def sum_near(keep, send, via_row, via_near):
        to_row = keep[:length].astype(F32) + send[:length].astype(F32)
        to_near = keep[length:].astype(F32) + send[length:].astype(F32)
        to_row = jnp.concatenate([to_row[:half], to_row[half:] + via_near.astype(F32)], axis=0)
        to_near = jnp.concatenate([to_near[:half] + via_row.astype(F32), to_near[half:]], axis=0)
        return to_row.astype(BF), to_near.astype(BF)

    def sum_own(keep, send, via_row, via_near):
        return (keep.astype(F32) + send.astype(F32)) + (via_row.astype(F32) + via_near.astype(F32))

    far_both = trade_col(back(3 * length, length, stacked=True)[0])
    to_row, to_near = sum_far(far_both[0], far_both[1])
    own_keep, own_send = back(0, length, after=[to_row, to_near])
    two_keep, two_send = back(length, 2 * length, after=[own_send])
    via_row, via_near = swap_row(to_row), swap_bit(to_near, 1)
    gate_keep, gate_send = weight_grad(scalars, full_two, low_back, piece, part, 0, after=[two_send])
    two_got = hold(swap_col(two_send), gate_send)
    via_row, via_near = hold(via_row, gate_send), hold(via_near, gate_send)
    to_row, to_near = sum_near(two_keep, two_got, via_row, via_near)
    via_row, via_near = swap_row(to_row), swap_bit(to_near, 1)
    own_got = swap_col(own_send)
    out_keep, out_send = down_project(scalars, hidden, w_down, down_fetched, after=[to_row, to_near])
    up_keep, up_send = weight_grad(scalars, full_two, low_back, piece, part, 1, after=[out_send])
    via_row, via_near = hold(via_row, up_send), hold(via_near, up_send)
    normed_grad = sum_own(own_keep, own_got, via_row, via_near).astype(BF)
    dh, low_mid, gain_two_part = middle_back(
        scalars, trade_col(jnp.stack([normed_grad, normed_grad])), h, r_two, gains[1:], fetched_gains[1:],
        full_cot,
    )
    out_grad_keep, out_grad_send = small_grad(low_mid, attended)
    first = 3 * length
    out_got = hold(swap_col(out_send), out_grad_send)
    to_row, to_near = sum_far(out_keep[first:], out_got[first:])
    back_low, in_part, bias_part = attend_back(
        scalars, low_mid, q, k, v, lse, seg_col, seg_row, w_out, out_fetched, w_query, w_key,
        w_value, qkv_fetched, cosine, sine, after=[out_grad_send, to_row, to_near],
    )
    via_row, via_near = hold(swap_row(to_row), back_low), hold(swap_bit(to_near, 1), back_low)
    qkv_grad_keep, qkv_grad_send = small_grad(low_one, back_low)
    to_row, to_near = sum_near(out_keep[length:first], out_got[length:first], via_row, via_near)
    input_grad, gain_one_part = input_back(
        scalars, trade_col(hold(in_part, qkv_grad_send)), mine, other, r_one, gains[:1], fetched_gains[:1], dh,
        after=[qkv_grad_send, to_row, to_near],
    )
    via_row, via_near = swap_row(to_row), swap_bit(to_near, 1)
    branch = sum_own(out_keep[:length], out_got[:length], via_row, via_near)
    h_mine, _ = by_row(h[:, :width], h[:, width:])
    output = turn_square((h_mine + branch).astype(BF))
    input_grad_low = input_grad
    input_grad = turn_square(input_grad).astype(F32)

    def add_bits(kept, sent, low_bits, after=()):
        value = kept.astype(F32) + sent.astype(F32)
        bits = (groups >> low_bits).bit_length() - 1
        for index in range(bits):
            bit = (group >> (low_bits + index)) % 2
            cut = value.reshape((value.shape[0], value.shape[1] // 2, 2) + value.shape[2:])
            recv = swap_bit(pick(cut, 1 - bit, 2).astype(BF), low_bits + index)
            if after:
                recv = hold(recv, *after)
            value = pick(cut, bit, 2) + recv.astype(F32)
        return value

    def ffn_sum(keep, send, steps):
        steps = [[step] if step is not None else [] for step in steps]
        recv = hold(swap_bit(send, 0), *steps[0])
        parts = (2, keep.shape[1] // 2, 2 * piece, keep.shape[3])
        value = add_bits(keep.reshape(parts), recv.reshape(parts), 2, after=steps[1])[:, 0]
        near, far = value[0], hold(swap_row(value[1].astype(BF)), *steps[2]).astype(F32)
        near, far = near.reshape(2, piece, -1), far.reshape(2, piece, -1)
        pair = jnp.stack([jnp.where(row == 0, near, far), jnp.where(row == 0, far, near)], axis=1)
        own = pick(pair, near_bit)
        across = hold(swap_bit(pick(pair, 1 - near_bit).astype(BF), 1), *steps[3]).astype(F32)
        four = jnp.concatenate(
            [jnp.where(near_bit == 0, own, across), jnp.where(near_bit == 0, across, own)], axis=0
        )
        last = four[PARTS - 1][:, overlap:]
        return jnp.concatenate([four[i] for i in range(PARTS - 1)] + [last], axis=1)

    down_grad = ffn_sum(down_keep, down_send, [two_send, up_send, low_mid, back_low]).T
    gate_grad = ffn_sum(gate_keep, gate_send, [low_mid, back_low, qkv_grad_send, None])
    up_grad = ffn_sum(up_keep, up_send, [back_low, input_grad_low, None, None])

    out_grads = out_grad_keep.astype(F32) + hold(swap_row(out_grad_send), qkv_grad_send).astype(F32)
    qkv_grads = qkv_grad_keep.astype(F32) + swap_row(qkv_grad_send).astype(F32)
    grads = jnp.concatenate([qkv_grads, out_grads], axis=1)
    cut = grads.reshape(groups // 2, 2, piece, -1)
    recv = swap_bit(pick(cut, 1 - inner, 1).astype(BF), 0)
    sum_attention = add_bits(pick(cut, inner, 1)[None], recv[None], 1)[0, 0]

    def canonical(value):
        first, second = value[:, :width], value[:, width:]
        return jnp.where(row == 0, value, jnp.concatenate([second, first], axis=1))[0]

    small = jnp.concatenate([bias_part[0], canonical(gain_one_part), canonical(gain_two_part)])
    small = small + swap_row(small)
    for bit in range(groups.bit_length() - 1):
        small = small + swap_bit(small, bit)
    gain_sums = pick(small[total_width:].reshape(2, 2, width), row, 1)

    return (
        output,
        input_grad,
        sum_attention[:, :query_width],
        sum_attention[:, query_width : query_width + key_width],
        sum_attention[:, query_width + key_width : total_width],
        small[:query_width],
        small[query_width : query_width + key_width],
        small[query_width + key_width : total_width],
        sum_attention[:, total_width:].T,
        gain_sums[0],
        gain_sums[1],
        gate_grad,
        up_grad,
        down_grad,
    )


def solution(mesh):
    return jax.shard_map(
        body,
        mesh=mesh,
        in_specs=(
            P(("dp", "col"), "row"),
            P(("dp", "row")),
            P(("dp", "row")),
            P("row", "col"),
            P("row", "col"),
            P("row", "col"),
            P("col"),
            P("col"),
            P("col"),
            P("col", "row"),
            P("row"),
            P("row"),
            P("row", "col"),
            P("row", "col"),
            P("col", "row"),
            P(("dp", "col"), "row"),
        ),
        out_specs=(
            P(("dp", "col"), "row"),
            P(("dp", "col"), "row"),
            P(("row", "dp"), "col"),
            P(("row", "dp"), "col"),
            P(("row", "dp"), "col"),
            P("col"),
            P("col"),
            P("col"),
            P("col", ("row", "dp")),
            P("row"),
            P("row"),
            P(("row", "dp"), "col"),
            P(("row", "dp"), "col"),
            P("col", ("row", "dp")),
        ),
        check_vma=False,
    )
```

time: 1120 us -> 641 us (0.57)
  waiting for transfers between devices: 486 us -> 126 us
  Pallas kernels: 0 us -> 279 us
  matrix products: 258 us -> 0 us
  other arithmetic: 117 us -> 53.2 us
  blocking collectives: 77 us -> 22.8 us
  local copies, waits for them, and re-layouts: 99.5 us -> 56.3 us
  starting transfers between devices: 67.1 us -> 90 us
    ppermute x21 -> x34, waiting for transfers between devices: 341 us -> 50.8 us  [swap_bit(): return lax.ppermute(value, 'dp', [(i, i ^ 1 << bit) for i in range(size)])]
    pallas_call x0 -> x63, Pallas kernels: none -> 279 us  [run(): pl.pallas_call(body, grid=grid if grid is not None else (), in_specs=[spe...]
    dot_general x22 -> x0, matrix products: 258 us -> none  [the longest x5 96 us: product_left(): lax.dot_general(left, right, (((0,), (0,)), ((), ())), preferred_element_...]
    psum x1 -> x0, blocking collectives: 77 us -> none  [body(): lax.psum(jnp.concatenate([bias_part, gain_one_part, gain_two_part]), ('dp...]
    ppermute x14 -> x20, waiting for transfers between devices: 145 us -> 75.5 us  [swap_row(): return lax.ppermute(value, 'row', [(0, 1), (1, 0)])]
    select_n x20 -> x8, other arithmetic: 40 us -> 3.41 us  [the longest x3 1.37 us: ffn_sum(): jnp.where(row == 0, near, far)]
    dynamic_slice x9 -> x0, local copies, waits for them, and re-layouts: 31.7 us -> none  [the longest x6 17.1 us: pick(): return lax.dynamic_index_in_dim(array, index, axis, keepdims=False)]
    all_to_all x0 -> x3, blocking collectives: none -> 22.8 us  [trade_col(): return lax.all_to_all(value, 'col', 0, 0)]
  transfers between devices with their start and end apart: 52 -> 70, of which waited for: 17 -> 18; matrix products, arithmetic and copies ran while one was open for 25% -> 11% of each run, Pallas kernels for 0% -> 44%
where the time goes in v2:
time: 641 us; the launch traced here: 630 us
  Pallas kernels  279 us (44%)
  waiting for transfers between devices  126 us (20%)
  starting transfers between devices  90 us (14%)
  local copies, waits for them, and re-layouts  56.3 us (9%)
  other arithmetic  53.2 us (8%)
  blocking collectives  22.8 us (4%)
    pallas_call x63, Pallas kernels, run(): pl.pallas_call(body, grid=grid if grid is not None else (), in_specs=[spe...  279 us
    ppermute x20, waiting for transfers between devices, swap_row(): return lax.ppermute(value, 'row', [(0, 1), (1, 0)])  75.5 us
    ppermute x34, waiting for transfers between devices, swap_bit(): return lax.ppermute(value, 'dp', [(i, i ^ 1 << bit) for i in range(size)])  50.8 us
    ppermute x34, starting transfers between devices, swap_bit(): return lax.ppermute(value, 'dp', [(i, i ^ 1 << bit) for i in range(size)])  44.7 us
    unnamed x175, local copies, waits for them, and re-layouts  36.9 us
    all_to_all x3, blocking collectives, trade_col(): return lax.all_to_all(value, 'col', 0, 0)  22.8 us
    ppermute x20, starting transfers between devices, swap_row(): return lax.ppermute(value, 'row', [(0, 1), (1, 0)])  19.6 us
    ppermute x12, starting transfers between devices, swap_col(): return lax.ppermute(value, 'col', [(0, 1), (1, 0)])  15.8 us
  transfers between devices with their start and end apart: 70, of which 18 were waited for; matrix products, arithmetic and copies ran while one was open for 11% of the time, Pallas kernels for 44%

profile of v2, /device:TPU:0, one launch (start us, length us, event | category | flops | bytes accessed | tf_op | source)
XLA Modules:
  0.0 629.7 jit_solution(17024061517601385604)
XLA Ops:
  11.3 13.1 %collective-permute-start.1 = (bf16[768,768]{1,0:T(8,128)(2,1)S(1)}, bf16[768,768]{1,0:T(8,128)(2,1)S(1)}, u32[]{:S(2)}, u32[]{:S(2)}) collective-permute-start(bf16[768,768]{1,0:T(8,128)(2,1)S(1)} %hold.37.refs_1_.refs_2_), channel_id=1, source_target_pairs={{0,1},{1,0},{2,3},{3,2},{4,5},{5,4},{6,7},{7,6},{8,9},{9,8},{10,11... | collective-permute-start | bytes 3538952 | tf_op jit(solution)/shard_map/ppermute | solution.py:34
  61.1 8.2 %qkv.1 = (bf16[768,768]{1,0:T(8,128)(2,1)}, bf16[768,128]{1,0:T(8,128)(2,1)}, bf16[768,128]{1,0:T(8,128)(2,1)}, bf16[768,1536]{1,0:T(8,128)(2,1)}, f32[768,1]{1,0:T(8,128)}) custom-call(s32[10]{0:T(128)} %copy-done.40, bf16[768,768]{1,0:T(8,128)(2,1)} %copy-done.12, bf16[768,768]{1,0:T(8,128)(2,1)} %copy-done.59, ...), custom_call_target="tpu_custom_call" | custom-call | flops 24159191040 | bytes 125829120 | tf_op jit(solution)/shard_map/qkv/pallas_call | solution.py:77
  70.6 5.3 collective-permute-done.14.refs_0_
  77.5 13.6 %attention.1 = (bf16[768,768]{1,0:T(8,128)(2,1)}, f32[768,128]{1,0:T(8,128)}, bf16[2,768,1536]{2,1,0:T(8,128)(2,1)}) custom-call(s32[10]{0:T(128)} %copy-done.40, bf16[768,768]{1,0:T(8,128)(2,1)} %get-tuple-element.62.refs_1_.refs_2_, bf16[768,128]{1,0:T(8,128)(2,1)} %get-tuple-element.63.refs_1_.refs_2_.refs_3_, ...), custom_call_target="tpu_custom_call" | custom-call | flops 36238786560 | bytes 125829120 | tf_op jit(solution)/shard_map/attention/pallas_call | solution.py:77
  99.7 9.1 %all_to_all.20.refs_3_ = bf16[2,768,1536]{2,1,0:T(8,128)(2,1)} all-to-all(bf16[2,768,1536]{2,1,0:T(8,128)(2,1)S(1)} %hold.45), channel_id=1, replica_groups=mesh['dp'=8,'row'=2,'col'=2] {'col'}, dimensions={0} | all-to-all | bytes 9437184 | tf_op jit(solution)/shard_map/all_to_all | solution.py:43
  109.8 8.6 %norm_two.1 = (f32[768,1536]{1,0:T(8,128)}, bf16[768,768]{1,0:T(8,128)(2,1)}, bf16[768,768]{1,0:T(8,128)(2,1)}, f32[768,1]{1,0:T(8,128)}) custom-call(s32[10]{0:T(128)} %copy-done.40, bf16[768,768]{1,0:T(8,128)(2,1)} %copy-done.12, bf16[768,768]{1,0:T(8,128)(2,1)} %copy-done.59, bf16[2,768,1536]{2,1,0:T(8,128)(2,1)} %all_to_all.20.refs_3_, ...), custom_call_target="tpu_custom_call" | custom-call | flops 117964800 | bytes 167772160 | tf_op jit(solution)/shard_map/norm_two/pallas_call | solution.py:77
  123.4 12.3 %gate_up.3 = (bf16[3072,1536]{1,0:T(8,128)(2,1)}, bf16[3072,1152]{1,0:T(8,128)(2,1)}, bf16[3072,1152]{1,0:T(8,128)(2,1)}, bf16[3072,1152]{1,0:T(8,128)(2,1)}) custom-call(s32[10]{0:T(128)} %copy-done.40, bf16[768,768]{1,0:T(8,128)(2,1)} %get-tuple-element.68.refs_1_, bf16[768,768]{1,0:T(8,128)(2,1)} %get-tuple-element.69.refs_2_, ...), custom_call_target="tpu_custom_call" | custom-call | flops 54358179840 | bytes 217989120 | tf_op jit(solution)/shard_map/gate_up/pallas_call | solution.py:77
  135.7 11.0 %collective-permute-done.22.refs_0_ = bf16[768,768]{1,0:T(8,128)(2,1)S(1)} collective-permute-done((bf16[768,768]{1,0:T(8,128)(2,1)}, bf16[768,768]{1,0:T(8,128)(2,1)S(1)}, u32[]{:S(2)}, u32[]{:S(2)}) %collective-permute-start.22) | collective-permute-done | bytes 1179680 | tf_op jit(solution)/shard_map/ppermute | solution.py:39
  160.2 19.1 %gate_up.4 = (bf16[3072,1536]{1,0:T(8,128)(2,1)}, bf16[3072,1152]{1,0:T(8,128)(2,1)}, bf16[3072,1152]{1,0:T(8,128)(2,1)}, bf16[3072,1152]{1,0:T(8,128)(2,1)}) custom-call(s32[10]{0:T(128)} %copy-done.40, bf16[768,768]{1,0:T(8,128)(2,1)} %copy-done.19, ...), custom_call_target="tpu_custom_call", output_to_operand_aliasing={{0}: (11, {}), {1}: (12, {}), {2}: (13, {}), {3}: (14, {})} | custom-call | flops 108716359680 | bytes 310149120 | tf_op jit(solution)/shard_map/gate_up/pallas_call | solution.py:77
  182.5 14.5 %collective-permute-done.27.refs_0_ = bf16[576,768]{1,0:T(8,128)(2,1)} collective-permute-done((bf16[576,768]{1,0:T(8,128)(2,1)}, bf16[576,768]{1,0:T(8,128)(2,1)}, u32[]{:S(2)}, u32[]{:S(2)}) %collective-permute-start.27) | collective-permute-done | bytes 884768 | tf_op jit(solution)/shard_map/ppermute | solution.py:30
  198.0 12.6 %gate_up.5 = (bf16[3072,1536]{1,0:T(8,128)(2,1)}, bf16[3072,1152]{1,0:T(8,128)(2,1)}, bf16[3072,1152]{1,0:T(8,128)(2,1)}, bf16[3072,1152]{1,0:T(8,128)(2,1)}) custom-call(s32[10]{0:T(128)} %copy-done.40, bf16[384,768]{1,0:T(8,128)(2,1)} %hold.50.refs_1_, ...), custom_call_target="tpu_custom_call", output_to_operand_aliasing={{0}: (11, {}), {1}: (12, {}), {2}: (13, {}), {3}: (14, {})} | custom-call | flops 54358179840 | bytes 217989120 | tf_op jit(solution)/shard_map/gate_up/pallas_call | solution.py:77
  210.6 6.7 %place_rows.1.refs_1_.refs_6_ = bf16[3072,1536]{1,0:T(8,128)(2,1)} custom-call(s32[10]{0:T(128)S(1)} %copy-done.42, bf16[768,768]{1,0:T(8,128)(2,1)S(1)} %copy-done.17, bf16[768,768]{1,0:T(8,128)(2,1)S(1)} %collective-permute-done.29.refs_2_, bf16[768,768]{1,0:T(8,128)(2,1)S(1)} %copy-done.15, bf16[768,768]{1,0:T(8,128)(2,1)S(1)} %collective-permute-done.30.refs_4_, ...), custom_call_target="tpu_custom_call" | custom-call | bytes 188743680 | tf_op jit(solution)/shard_map/place_rows/pallas_call | solution.py:77
  217.3 18.8 %weight_grad.3 = (bf16[2,4,96,1152]{3,2,1,0:T(8,128)(2,1)}, bf16[2,4,96,1152]{3,2,1,0:T(8,128)(2,1)}) custom-call(s32[10]{0:T(128)} %copy-done.40, bf16[3072,1536]{1,0:T(8,128)(2,1)} %place_rows.1.refs_1_.refs_6_, bf16[3072,1152]{1,0:T(8,128)(2,1)} %get-tuple-element.78.refs_9_.refs_2_.refs_1_), custom_call_target="tpu_custom_call" | custom-call | flops 108716359680 | bytes 235929600 | tf_op jit(solution)/shard_map/weight_grad/pallas_call | solution.py:77
  237.7 21.3 %hidden_back.1.refs_1_.refs_2_ = bf16[3072,2304]{1,0:T(8,128)(2,1)} custom-call(s32[10]{0:T(128)} %copy-done.40, bf16[3072,1536]{1,0:T(8,128)(2,1)} %place_rows.1.refs_1_.refs_6_, bf16[3072,1152]{1,0:T(8,128)(2,1)} %get-tuple-element.79.refs_2_, bf16[3072,1152]{1,0:T(8,128)(2,1)} %get-tuple-element.80.refs_3_, bf16[4480,768]{1,0:T(8,128)(2,1)} %refs_2_.13, ...), custom_call_target="tpu_custom_call" | custom-call | flops 108716359680 | bytes 430080000 | tf_op jit(solution)/shard_map/hidden_back/pallas_call | solution.py:77
  259.0 11.7 %norm_back.3 = bf16[2,768,768]{2,1,0:T(8,128)(2,1)} custom-call(s32[10]{0:T(128)} %copy-done.40, bf16[3072,2304]{1,0:T(8,128)(2,1)} %hidden_back.1.refs_1_.refs_2_, bf16[768,4480]{1,0:T(8,128)(2,1)} %refs_2_.12, bf16[768,4480]{1,0:T(8,128)(2,1)} %refs_3_.9, bf16[192,2304]{1,0:T(8,128)(2,1)} %copy-done.32, bf16[192,2304]{1,0:T(8,128)(2,1)} %copy-done.71, ...), custom_call_target="tpu_custom_call" | custom-call | flops 54358179840 | bytes 145326080 | tf_op jit(solution)/shard_map/norm_back/pallas_call | solution.py:77
  270.7 7.1 %all_to_all.21 = bf16[2,768,768]{2,1,0:T(8,128)(2,1)S(1)} all-to-all(bf16[2,768,768]{2,1,0:T(8,128)(2,1)} %norm_back.3), channel_id=1, replica_groups=mesh['dp'=8,'row'=2,'col'=2] {'col'}, dimensions={0} | all-to-all | bytes 4718592 | tf_op jit(solution)/shard_map/all_to_all | solution.py:43
  280.9 11.8 %norm_back.4 = (bf16[768,768]{1,0:T(8,128)(2,1)}, bf16[768,768]{1,0:T(8,128)(2,1)}) custom-call(s32[10]{0:T(128)} %copy-done.40, bf16[3072,2304]{1,0:T(8,128)(2,1)} %hidden_back.1.refs_1_.refs_2_, bf16[768,4480]{1,0:T(8,128)(2,1)} %refs_2_.12, bf16[768,4480]{1,0:T(8,128)(2,1)} %refs_3_.9, bf16[192,2304]{1,0:T(8,128)(2,1)} %copy-done.32, ...), custom_call_target="tpu_custom_call" | custom-call | flops 54358179840 | bytes 145326080 | tf_op jit(solution)/shard_map/norm_back/pallas_call | solution.py:77
  292.8 18.1 %norm_back.5 = (bf16[1536,768]{1,0:T(8,128)(2,1)}, bf16[1536,768]{1,0:T(8,128)(2,1)}) custom-call(s32[10]{0:T(128)} %copy-done.40, bf16[3072,2304]{1,0:T(8,128)(2,1)} %hidden_back.1.refs_1_.refs_2_, bf16[768,4480]{1,0:T(8,128)(2,1)} %refs_2_.12, bf16[768,4480]{1,0:T(8,128)(2,1)} %refs_3_.9, bf16[192,2304]{1,0:T(8,128)(2,1)} %copy-done.32, ...), custom_call_target="tpu_custom_call" | custom-call | flops 108716359680 | bytes 206766080 | tf_op jit(solution)/shard_map/norm_back/pallas_call | solution.py:77
  311.5 18.6 %weight_grad.4 = (bf16[2,4,96,1152]{3,2,1,0:T(8,128)(2,1)}, bf16[2,4,96,1152]{3,2,1,0:T(8,128)(2,1)}) custom-call(s32[10]{0:T(128)} %copy-done.40, bf16[3072,1536]{1,0:T(8,128)(2,1)} %get-tuple-element.85.refs_1_, bf16[3072,2304]{1,0:T(8,128)(2,1)} %hidden_back.1.refs_1_.refs_2_, bf16[1536,768]{1,0:T(8,128)(2,1)} %get-tuple-element.84.refs_3_.refs_1_), custom_call_target="tpu_custom_call" | custom-call | flops 108716359680 | bytes 235929600 | tf_op jit(solution)/shard_map/weight_grad/pallas_call | solution.py:77
  347.4 19.3 %down_project.1 = (bf16[3072,768]{1,0:T(8,128)(2,1)}, bf16[3072,768]{1,0:T(8,128)(2,1)}) custom-call(s32[10]{0:T(128)} %copy-done.40, bf16[3072,1152]{1,0:T(8,128)(2,1)} %get-tuple-element.78.refs_9_.refs_2_.refs_1_, bf16[4480,768]{1,0:T(8,128)(2,1)} %refs_2_.13, bf16[576,768]{1,0:T(8,128)(2,1)} %hold.52.refs_5_.refs_3_, ...), custom_call_target="tpu_custom_call" | custom-call | flops 108716359680 | bytes 245760000 | tf_op jit(solution)/shard_map/down_project/pallas_call | solution.py:77
  366.7 18.7 %weight_grad.5 = (bf16[2,4,96,1152]{3,2,1,0:T(8,128)(2,1)}, bf16[2,4,96,1152]{3,2,1,0:T(8,128)(2,1)}) custom-call(s32[10]{0:T(128)} %copy-done.40, bf16[3072,1536]{1,0:T(8,128)(2,1)} %get-tuple-element.85.refs_1_, bf16[3072,2304]{1,0:T(8,128)(2,1)} %hidden_back.1.refs_1_.refs_2_, bf16[3072,768]{1,0:T(8,128)(2,1)} %get-tuple-element.88.refs_3_), custom_call_target="tpu_custom_call" | custom-call | flops 108716359680 | bytes 235929600 | tf_op jit(solution)/shard_map/weight_grad/pallas_call | solution.py:77
  395.5 6.6 %all_to_all.22.refs_1_ = bf16[2,768,768]{2,1,0:T(8,128)(2,1)} all-to-all(bf16[2,768,768]{2,1,0:T(8,128)(2,1)S(1)} %pad_maximum_fusion.1), channel_id=1, replica_groups=mesh['dp'=8,'row'=2,'col'=2] {'col'}, dimensions={0} | all-to-all | bytes 4718592 | tf_op jit(solution)/shard_map/all_to_all | solution.py:43
  402.1 9.7 %middle_back.1 = (f32[768,1536]{1,0:T(8,128)}, bf16[768,1536]{1,0:T(8,128)(2,1)}, f32[1,1536]{1,0:T(1,128)}) custom-call(s32[10]{0:T(128)} %copy-done.40, bf16[2,768,768]{2,1,0:T(8,128)(2,1)} %all_to_all.22.refs_1_, f32[768,1536]{1,0:T(8,128)} %get-tuple-element.67.refs_2_, f32[768,1]{1,0:T(8,128)} %get-tuple-element.91.refs_3_, ...), custom_call_target="tpu_custom_call" | custom-call | flops 176947200 | bytes 209715200 | tf_op jit(solution)/shard_map/middle_back/pallas_call | solution.py:77
  430.6 6.6 %convert_add_fusion.6 = (f32[768,768]{1,0:T(8,128)}, f32[768,768]{1,0:T(8,128)}, bf16[768,768]{1,0:T(8,128)(2,1)S(1)}) fusion(bf16[3072,768]{1,0:T(8,128)(2,1)S(1)} %hold.60, bf16[3072,768]{1,0:T(8,128)(2,1)} %get-tuple-element.87), kind=kLoop, calls=%fused_computation.12 | loop fusion | flops 5898240 | bytes 12976128 | tf_op jit(solution)/shard_map/add | solution.py:847
  439.7 22.5 %attention_back.1 = (bf16[768,1024]{1,0:T(8,128)(2,1)}, bf16[2,768,1536]{2,1,0:T(8,128)(2,1)}, f32[1,1024]{1,0:T(1,128)}) custom-call(s32[10]{0:T(128)} %copy-done.40, bf16[768,1536]{1,0:T(8,128)(2,1)} %get-tuple-element.92.refs_0_.refs_1_, bf16[768,768]{1,0:T(8,128)(2,1)} %get-tuple-element.62.refs_1_.refs_2_, ...), custom_call_target="tpu_custom_call" | custom-call | flops 87577067520 | bytes 209715200 | tf_op jit(solution)/shard_map/attention_back/pallas_call | solution.py:77
  467.0 5.9 small_grad.3
  474.3 6.1 all-to-all-start.3
  496.1 8.6 %input_back.1 = (bf16[768,768]{1,0:T(8,128)(2,1)}, f32[1,1536]{1,0:T(1,128)}) custom-call(s32[10]{0:T(128)} %copy-done.40, bf16[2,768,1536]{2,1,0:T(8,128)(2,1)} %all-to-all-done.3.refs_1_, bf16[768,768]{1,0:T(8,128)(2,1)} %copy-done.12, bf16[768,768]{1,0:T(8,128)(2,1)} %copy-done.59, f32[768,1]{1,0:T(8,128)} %get-tuple-element.99.refs_4_, ...), custom_call_target="tpu_custom_call" | custom-call | flops 176947200 | bytes 167772160 | tf_op jit(solution)/shard_map/input_back/pallas_call | solution.py:77
  508.4 18.6 %collective-permute-done.53 = f32[4096]{0:T(1024)S(1)} collective-permute-done((f32[4096]{0:T(1024)S(1)}, f32[4096]{0:T(1024)S(1)}, u32[]{:S(2)}, u32[]{:S(2)}) %collective-permute-start.53) | collective-permute-done | bytes 16416 | tf_op jit(solution)/shard_map/ppermute | solution.py:30
  556.3 29.5 %collective-permute-done.63 = bf16[192,1152]{1,0:T(8,128)(2,1)S(1)} collective-permute-done((bf16[192,1152]{1,0:T(8,128)(2,1)S(1)}, bf16[192,1152]{1,0:T(8,128)(2,1)S(1)}, u32[]{:S(2)}, u32[]{:S(2)}) %collective-permute-start.63) | collective-permute-done | bytes 442400 | tf_op jit(solution)/shard_map/ppermute | solution.py:30
  598.5 13.3 %collective-permute-done.51 = bf16[1,2,96,1792]{3,2,1,0:T(8,128)(2,1)S(1)} collective-permute-done((bf16[1,2,96,1792]{3,2,1,0:T(8,128)(2,1)S(1)}, bf16[1,2,96,1792]{3,2,1,0:T(8,128)(2,1)S(1)}, u32[]{:S(2)}, u32[]{:S(2)}) %collective-permute-start.51) | collective-permute-done | bytes 688160 | tf_op jit(solution)/shard_map/ppermute | solution.py:39
  616.2 10.7 %collective-permute-done.52 = bf16[1,1,96,1792]{3,2,1,0:T(8,128)(2,1)S(1)} collective-permute-done((bf16[1,1,96,1792]{3,2,1,0:T(8,128)(2,1)S(1)}, bf16[1,1,96,1792]{3,2,1,0:T(8,128)(2,1)S(1)}, u32[]{:S(2)}, u32[]{:S(2)}) %collective-permute-start.52) | collective-permute-done | bytes 344096 | tf_op jit(solution)/shard_map/ppermute | solution.py:39
  (458 shorter events, 209.8 us)
Async XLA Ops:
  9.7 44.3 %collective-permute-start.9 = (bf16[768,768]{1,0:T(8,128)(2,1)S(1)}, bf16[768,768]{1,0:T(8,128)(2,1)S(1)}, u32[]{:S(2)}, u32[]{:S(2)}) collective-permute-start(bf16[768,768]{1,0:T(8,128)(2,1)S(1)} %copy-done.24), channel_id=1, source_target_pairs={{0,8},{4,12},{8,0},{12,4},{16,24},{20,28},{24,16},{28,20},{1,9},{5... | collective-permute-start | bytes 3538952 | tf_op jit(solution)/shard_map/ppermute | solution.py:39
  11.3 48.8 %collective-permute-start.1 = (bf16[768,768]{1,0:T(8,128)(2,1)S(1)}, bf16[768,768]{1,0:T(8,128)(2,1)S(1)}, u32[]{:S(2)}, u32[]{:S(2)}) collective-permute-start(bf16[768,768]{1,0:T(8,128)(2,1)S(1)} %hold.37.refs_1_.refs_2_), channel_id=1, source_target_pairs={{0,1},{1,0},{2,3},{3,2},{4,5},{5,4},{6,7},{7,6},{8,9},{9,8},{10,11... | collective-permute-start | bytes 3538952 | tf_op jit(solution)/shard_map/ppermute | solution.py:34
  54.0 40.8 %collective-permute-start.15 = (bf16[192,2304]{1,0:T(8,128)(2,1)S(1)}, bf16[192,2304]{1,0:T(8,128)(2,1)S(1)}, u32[]{:S(2)}, u32[]{:S(2)}) collective-permute-start(bf16[192,2304]{1,0:T(8,128)(2,1)S(1)} %pack.8.refs_1_.refs_16_), channel_id=1, source_target_pairs={{0,2},{2,0},{1,3},{3,1},{4,6},{6,4},{5,7},{7,5},{8,10},{10,8},{9,1... | collective-permute-start | bytes 2654216 | tf_op jit(solution)/shard_map/ppermute | solution.py:30
  75.8 33.0 %collective-permute-start.16 = (bf16[192,2304]{1,0:T(8,128)(2,1)S(1)}, bf16[192,2304]{1,0:T(8,128)(2,1)S(1)}, u32[]{:S(2)}, u32[]{:S(2)}) collective-permute-start(bf16[192,2304]{1,0:T(8,128)(2,1)S(1)} %hold.43.refs_12_.refs_5_.refs_7_.refs_4_), channel_id=1, source_target_pairs={{0,4},{4,0},{8,12},{12,8},{16,20},{20,16},{24,28},{28,24},{1,5},{5... | collective-permute-start | bytes 2654216 | tf_op jit(solution)/shard_map/ppermute | solution.py:39
  77.4 42.8 %collective-permute-start.19 = (bf16[768,768]{1,0:T(8,128)(2,1)S(1)}, bf16[768,768]{1,0:T(8,128)(2,1)S(1)}, u32[]{:S(2)}, u32[]{:S(2)}) collective-permute-start(bf16[768,768]{1,0:T(8,128)(2,1)S(1)} %copy_of.1.refs_13_.refs_1_), channel_id=1, source_target_pairs={{0,2},{2,0},{1,3},{3,1},{4,6},{6,4},{5,7},{7,5},{8,10},{10,8},{9,1... | collective-permute-start | bytes 3538952 | tf_op jit(solution)/shard_map/ppermute | solution.py:30
  149.7 30.2 %collective-permute-start.32 = (bf16[384,768]{1,0:T(8,128)(2,1)}, bf16[384,768]{1,0:T(8,128)(2,1)}, u32[]{:S(2)}, u32[]{:S(2)}) collective-permute-start(bf16[384,768]{1,0:T(8,128)(2,1)} %slice.343), channel_id=1, source_target_pairs={{0,8},{4,12},{8,0},{12,4},{16,24},{20,28},{24,16},{28,20},{1,9},{5... | collective-permute-start | bytes 1769480 | tf_op jit(solution)/shard_map/ppermute | solution.py:39
  158.5 38.4 %collective-permute-start.27 = (bf16[576,768]{1,0:T(8,128)(2,1)}, bf16[576,768]{1,0:T(8,128)(2,1)}, u32[]{:S(2)}, u32[]{:S(2)}) collective-permute-start(bf16[576,768]{1,0:T(8,128)(2,1)} %pack.9.refs_15_), channel_id=1, source_target_pairs={{0,2},{2,0},{1,3},{3,1},{4,6},{6,4},{5,7},{7,5},{8,10},{10,8},{9,1... | collective-permute-start | bytes 2654216 | tf_op jit(solution)/shard_map/ppermute | solution.py:30
  180.6 30.0 %collective-permute-start.30 = (bf16[768,768]{1,0:T(8,128)(2,1)S(1)}, bf16[768,768]{1,0:T(8,128)(2,1)S(1)}, u32[]{:S(2)}, u32[]{:S(2)}) collective-permute-start(bf16[768,768]{1,0:T(8,128)(2,1)S(1)} %copy-done.15), channel_id=1, source_target_pairs={{0,1},{1,0},{2,3},{3,2},{4,5},{5,4},{6,7},{7,6},{8,9},{9,8},{10,11... | collective-permute-start | bytes 3538952 | tf_op jit(solution)/shard_map/ppermute | solution.py:34
  197.5 40.2 %collective-permute-start.28 = (bf16[576,768]{1,0:T(8,128)(2,1)}, bf16[576,768]{1,0:T(8,128)(2,1)}, u32[]{:S(2)}, u32[]{:S(2)}) collective-permute-start(bf16[576,768]{1,0:T(8,128)(2,1)} %hold.52.refs_5_.refs_3_), channel_id=1, source_target_pairs={{0,4},{4,0},{8,12},{12,8},{16,20},{20,16},{24,28},{28,24},{1,5},{5... | collective-permute-start | bytes 2654216 | tf_op jit(solution)/shard_map/ppermute | solution.py:39
  236.1 96.0 %collective-permute-start.65 = (bf16[2,4,96,1152]{3,2,1,0:T(8,128)(2,1)}, bf16[2,4,96,1152]{3,2,1,0:T(8,128)(2,1)}, u32[]{:S(2)}, u32[]{:S(2)}) collective-permute-start(bf16[2,4,96,1152]{3,2,1,0:T(8,128)(2,1)} %get-tuple-element.81.refs_7_), channel_id=1, source_target_pairs={{0,4},{4,0},{8,12},{12,8},{16,20},{20,16},{24,28},{28,24},{1,5},{5... | collective-permute-start | bytes 5308424 | tf_op jit(solution)/shard_map/ppermute | solution.py:39
  279.1 51.0 %collective-permute-start.37 = (bf16[384,768]{1,0:T(8,128)(2,1)}, bf16[384,768]{1,0:T(8,128)(2,1)}, u32[]{:S(2)}, u32[]{:S(2)}) collective-permute-start(bf16[384,768]{1,0:T(8,128)(2,1)} %get-tuple-element.132.refs_8_), channel_id=1, source_target_pairs={{0,2},{2,0},{1,3},{3,1},{4,6},{6,4},{5,7},{7,5},{8,10},{10,8},{9,1... | collective-permute-start | bytes 1769480 | tf_op jit(solution)/shard_map/ppermute | solution.py:30
  280.5 51.6 %collective-permute-start.36 = (bf16[384,768]{1,0:T(8,128)(2,1)}, bf16[384,768]{1,0:T(8,128)(2,1)}, u32[]{:S(2)}, u32[]{:S(2)}) collective-permute-start(bf16[384,768]{1,0:T(8,128)(2,1)} %get-tuple-element.131.refs_9_), channel_id=1, source_target_pairs={{0,8},{4,12},{8,0},{12,4},{16,24},{20,28},{24,16},{28,20},{1,9},{5... | collective-permute-start | bytes 1769480 | tf_op jit(solution)/shard_map/ppermute | solution.py:39
  292.8 100.0 %collective-permute-start.39 = (bf16[768,768]{1,0:T(8,128)(2,1)}, bf16[768,768]{1,0:T(8,128)(2,1)}, u32[]{:S(2)}, u32[]{:S(2)}) collective-permute-start(bf16[768,768]{1,0:T(8,128)(2,1)} %get-tuple-element.82.refs_8_), channel_id=1, source_target_pairs={{0,1},{1,0},{2,3},{3,2},{4,5},{5,4},{6,7},{7,6},{8,9},{9,8},{10,11... | collective-permute-start | bytes 3538952 | tf_op jit(solution)/shard_map/ppermute | solution.py:34
  330.1 83.7 %collective-permute-start.57 = (bf16[2,4,96,1152]{3,2,1,0:T(8,128)(2,1)}, bf16[2,4,96,1152]{3,2,1,0:T(8,128)(2,1)}, u32[]{:S(2)}, u32[]{:S(2)}) collective-permute-start(bf16[2,4,96,1152]{3,2,1,0:T(8,128)(2,1)} %get-tuple-element.86.refs_1_), channel_id=1, source_target_pairs={{0,4},{4,0},{8,12},{12,8},{16,20},{20,16},{24,28},{28,24},{1,5},{5... | collective-permute-start | bytes 5308424 | tf_op jit(solution)/shard_map/ppermute | solution.py:39
  337.2 48.1 %collective-permute-start.66 = (bf16[2,1,192,1152]{3,2,1,0:T(8,128)(2,1)}, bf16[2,1,192,1152]{3,2,1,0:T(8,128)(2,1)}, u32[]{:S(2)}, u32[]{:S(2)}) collective-permute-start(bf16[2,1,192,1152]{3,2,1,0:T(8,128)(2,1)} %dynamic-slice_convert_fusion), channel_id=1, source_target_pairs={{0,16},{4,20},{8,24},{12,28},{16,0},{20,4},{24,8},{28,12},{1,17},{... | collective-permute-start | bytes 2654216 | tf_op jit(solution)/shard_map/ppermute | solution.py:39
  344.1 44.7 %collective-permute-start.40 = (bf16[768,768]{1,0:T(8,128)(2,1)}, bf16[768,768]{1,0:T(8,128)(2,1)}, u32[]{:S(2)}, u32[]{:S(2)}) collective-permute-start(bf16[768,768]{1,0:T(8,128)(2,1)} %pad_maximum_fusion.5.refs_5_), channel_id=1, source_target_pairs={{0,2},{2,0},{1,3},{3,1},{4,6},{6,4},{5,7},{7,5},{8,10},{10,8},{9,1... | collective-permute-start | bytes 3538952 | tf_op jit(solution)/shard_map/ppermute | solution.py:30
  345.9 45.5 %collective-permute-start.41 = (bf16[768,768]{1,0:T(8,128)(2,1)}, bf16[768,768]{1,0:T(8,128)(2,1)}, u32[]{:S(2)}, u32[]{:S(2)}) collective-permute-start(bf16[768,768]{1,0:T(8,128)(2,1)} %pad_maximum_fusion.6.refs_6_), channel_id=1, source_target_pairs={{0,8},{4,12},{8,0},{12,4},{16,24},{20,28},{24,16},{28,20},{1,9},{5... | collective-permute-start | bytes 3538952 | tf_op jit(solution)/shard_map/ppermute | solution.py:39
  385.3 43.9 %collective-permute-start.38 = (bf16[3072,768]{1,0:T(8,128)(2,1)}, bf16[3072,768]{1,0:T(8,128)(2,1)S(1)}, u32[]{:S(2)}, u32[]{:S(2)}) collective-permute-start(bf16[3072,768]{1,0:T(8,128)(2,1)} %get-tuple-element.88.refs_3_), channel_id=1, source_target_pairs={{0,1},{1,0},{2,3},{3,2},{4,5},{5,4},{6,7},{7,6},{8,9},{9,8},{10,11... | collective-permute-start | bytes 14155784 | tf_op jit(solution)/shard_map/ppermute | solution.py:34
  388.7 91.7 %collective-permute-start.61 = (bf16[2,4,96,1152]{3,2,1,0:T(8,128)(2,1)}, bf16[2,4,96,1152]{3,2,1,0:T(8,128)(2,1)}, u32[]{:S(2)}, u32[]{:S(2)}) collective-permute-start(bf16[2,4,96,1152]{3,2,1,0:T(8,128)(2,1)} %get-tuple-element.90.refs_1_), channel_id=1, source_target_pairs={{0,4},{4,0},{8,12},{12,8},{16,20},{20,16},{24,28},{28,24},{1,5},{5... | collective-permute-start | bytes 5308424 | tf_op jit(solution)/shard_map/ppermute | solution.py:39
  413.7 48.5 %collective-permute-start.68 = (bf16[2,96,1152]{2,1,0:T(8,128)(2,1)S(1)}, bf16[2,96,1152]{2,1,0:T(8,128)(2,1)S(1)}, u32[]{:S(2)}, u32[]{:S(2)}) collective-permute-start(bf16[2,96,1152]{2,1,0:T(8,128)(2,1)S(1)} %fusion.24), channel_id=1, source_target_pairs={{0,8},{4,12},{8,0},{12,4},{16,24},{20,28},{24,16},{28,20},{1,9},{5... | collective-permute-start | bytes 1327112 | tf_op jit(solution)/shard_map/ppermute | solution.py:39
  419.8 66.7 %collective-permute-start.58 = (bf16[2,1,192,1152]{3,2,1,0:T(8,128)(2,1)}, bf16[2,1,192,1152]{3,2,1,0:T(8,128)(2,1)}, u32[]{:S(2)}, u32[]{:S(2)}) collective-permute-start(bf16[2,1,192,1152]{3,2,1,0:T(8,128)(2,1)} %dynamic-slice_convert_fusion.2), channel_id=1, source_target_pairs={{0,16},{4,20},{8,24},{12,28},{16,0},{20,4},{24,8},{28,12},{1,17},{... | collective-permute-start | bytes 2654216 | tf_op jit(solution)/shard_map/ppermute | solution.py:39
  428.6 79.8 %collective-permute-start.49 = (bf16[768,768]{1,0:T(8,128)(2,1)}, bf16[768,768]{1,0:T(8,128)(2,1)}, u32[]{:S(2)}, u32[]{:S(2)}) collective-permute-start(bf16[768,768]{1,0:T(8,128)(2,1)} %get-tuple-element.94.refs_1_.refs_24_), channel_id=1, source_target_pairs={{0,2},{2,0},{1,3},{3,1},{4,6},{6,4},{5,7},{7,5},{8,10},{10,8},{9,1... | collective-permute-start | bytes 3538952 | tf_op jit(solution)/shard_map/ppermute | solution.py:30
  438.3 52.5 %collective-permute-start.42 = (bf16[384,768]{1,0:T(8,128)(2,1)}, bf16[384,768]{1,0:T(8,128)(2,1)}, u32[]{:S(2)}, u32[]{:S(2)}) collective-permute-start(bf16[384,768]{1,0:T(8,128)(2,1)} %get-tuple-element.129.refs_26_), channel_id=1, source_target_pairs={{0,8},{4,12},{8,0},{12,4},{16,24},{20,28},{24,16},{28,20},{1,9},{5... | collective-permute-start | bytes 1769480 | tf_op jit(solution)/shard_map/ppermute | solution.py:39
  462.2 30.5 %collective-permute-start.44 = (bf16[384,768]{1,0:T(8,128)(2,1)}, bf16[384,768]{1,0:T(8,128)(2,1)}, u32[]{:S(2)}, u32[]{:S(2)}) collective-permute-start(bf16[384,768]{1,0:T(8,128)(2,1)} %get-tuple-element.130.refs_25_), channel_id=1, source_target_pairs={{0,2},{2,0},{1,3},{3,1},{4,6},{6,4},{5,7},{7,5},{8,10},{10,8},{9,1... | collective-permute-start | bytes 1769480 | tf_op jit(solution)/shard_map/ppermute | solution.py:30
  480.4 71.6 %collective-permute-start.48 = (bf16[768,1024]{1,0:T(8,128)(2,1)S(1)}, bf16[768,1024]{1,0:T(8,128)(2,1)}, u32[]{:S(2)}, u32[]{:S(2)}) collective-permute-start(bf16[768,1024]{1,0:T(8,128)(2,1)S(1)} %copy-done.4), channel_id=1, source_target_pairs={{0,2},{2,0},{1,3},{3,1},{4,6},{6,4},{5,7},{7,5},{8,10},{10,8},{9,1... | collective-permute-start | bytes 4718600 | tf_op jit(solution)/shard_map/ppermute | solution.py:30
  486.5 56.1 %collective-permute-start.62 = (bf16[2,1,192,1152]{3,2,1,0:T(8,128)(2,1)}, bf16[2,1,192,1152]{3,2,1,0:T(8,128)(2,1)}, u32[]{:S(2)}, u32[]{:S(2)}) collective-permute-start(bf16[2,1,192,1152]{3,2,1,0:T(8,128)(2,1)} %dynamic-slice_convert_fusion.1), channel_id=1, source_target_pairs={{0,16},{4,20},{8,24},{12,28},{16,0},{20,4},{24,8},{28,12},{1,17},{... | collective-permute-start | bytes 2654216 | tf_op jit(solution)/shard_map/ppermute | solution.py:39
  490.8 40.8 %collective-permute-start.59 = (bf16[192,1152]{1,0:T(8,128)(2,1)}, bf16[192,1152]{1,0:T(8,128)(2,1)}, u32[]{:S(2)}, u32[]{:S(2)}) collective-permute-start(bf16[192,1152]{1,0:T(8,128)(2,1)} %fusion.19), channel_id=1, source_target_pairs={{0,2},{2,0},{1,3},{3,1},{4,6},{6,4},{5,7},{7,5},{8,10},{10,8},{9,1... | collective-permute-start | bytes 1327112 | tf_op jit(solution)/shard_map/ppermute | solution.py:30
  537.0 50.5 %collective-permute-start.43 = (bf16[768,768]{1,0:T(8,128)(2,1)}, bf16[768,768]{1,0:T(8,128)(2,1)}, u32[]{:S(2)}, u32[]{:S(2)}) collective-permute-start(bf16[768,768]{1,0:T(8,128)(2,1)} %pad_maximum_fusion.7.refs_9_), channel_id=1, source_target_pairs={{0,2},{2,0},{1,3},{3,1},{4,6},{6,4},{5,7},{7,5},{8,10},{10,8},{9,1... | collective-permute-start | bytes 3538952 | tf_op jit(solution)/shard_map/ppermute | solution.py:30
  540.3 47.1 %collective-permute-start.45 = (bf16[768,768]{1,0:T(8,128)(2,1)}, bf16[768,768]{1,0:T(8,128)(2,1)}, u32[]{:S(2)}, u32[]{:S(2)}) collective-permute-start(bf16[768,768]{1,0:T(8,128)(2,1)} %pad_maximum_fusion.8.refs_10_), channel_id=1, source_target_pairs={{0,8},{4,12},{8,0},{12,4},{16,24},{20,28},{24,16},{28,20},{1,9},{5... | collective-permute-start | bytes 3538952 | tf_op jit(solution)/shard_map/ppermute | solution.py:39
  542.6 48.9 %collective-permute-start.47 = (bf16[768,768]{1,0:T(8,128)(2,1)S(1)}, bf16[768,768]{1,0:T(8,128)(2,1)S(1)}, u32[]{:S(2)}, u32[]{:S(2)}) collective-permute-start(bf16[768,768]{1,0:T(8,128)(2,1)S(1)} %copy-done.27), channel_id=1, source_target_pairs={{0,0},{1,2},{2,1},{3,3},{4,4},{5,6},{6,5},{7,7},{8,8},{9,10},{10,9... | collective-permute-start | bytes 3538952 | tf_op jit(solution)/shard_map/ppermute | solution.py:47
  549.7 36.0 %collective-permute-start.63 = (bf16[192,1152]{1,0:T(8,128)(2,1)S(1)}, bf16[192,1152]{1,0:T(8,128)(2,1)S(1)}, u32[]{:S(2)}, u32[]{:S(2)}) collective-permute-start(bf16[192,1152]{1,0:T(8,128)(2,1)S(1)} %fusion.20), channel_id=1, source_target_pairs={{0,2},{2,0},{1,3},{3,1},{4,6},{6,4},{5,7},{7,5},{8,10},{10,8},{9,1... | collective-permute-start | bytes 1327112 | tf_op jit(solution)/shard_map/ppermute | solution.py:30
  555.5 41.0 %collective-permute-start.50 = (bf16[4,96,1792]{2,1,0:T(8,128)(2,1)S(1)}, bf16[4,96,1792]{2,1,0:T(8,128)(2,1)S(1)}, u32[]{:S(2)}, u32[]{:S(2)}) collective-permute-start(bf16[4,96,1792]{2,1,0:T(8,128)(2,1)S(1)} %fusion), channel_id=1, source_target_pairs={{0,4},{4,0},{8,12},{12,8},{16,20},{20,16},{24,28},{28,24},{1,5},{5... | collective-permute-start | bytes 4128776 | tf_op jit(solution)/shard_map/ppermute | solution.py:39
  (128 other events, 1235.4 us)

commit v3 on v2

--- a/solution.py
+++ b/solution.py
@@ -17,13 +17,14 @@
 WIDE_TILE = 384
 MIB = 1024 * 1024
 SCALE = 10.0
+GLUE = 1e9
 
 EPS = 1e-06
 THETA = 1000000.0
 BF = jnp.bfloat16
 F32 = jnp.float32
 
-SAME, INNER, START, START_FAR, SKIP, OWN, PAIR, NEAR, ACROSS, ROW = range(10)
+SAME, INNER, START, START_FAR, SKIP, OWN, PAIR, NEAR, ACROSS, ROW, BITS = range(11)
 
 
 def swap_row(value):
@@ -66,15 +67,19 @@
     )
 
 
+LAST = []
+
+
 def run(kernel, ins, outs, after=(), grid=None, out_specs=None, scratch=(), limit=56, aliases=None,
         estimate=None, name=None):
     given = len(ins)
     count = len(outs)
+    after = [*after, *LAST]
 
     def body(*refs):
         kernel(*refs[:given], *refs[given + len(after):])
 
-    return pl.pallas_call(
+    results = pl.pallas_call(
         body,
         grid=grid if grid is not None else (),
         in_specs=[spec for _, spec in ins] + [ANY] * len(after),
@@ -86,6 +91,8 @@
         name=name,
         compiler_params=pltpu.CompilerParams(vmem_limit_bytes=limit * MIB),
     )(*[array for array, _ in ins], *after)
+    LAST[:] = [results[-1]]
+    return results
 
 
 def dot(left, right):
@@ -299,16 +306,16 @@
                estimate=cost(length * width * 20, 16 * MIB), name="norm_two")
 
 
-def gate_up(scalars, pieces, w_gate, w_up, fetched, first, total, part, kept=None, after=()):
-    width = pieces[0][0].shape[1]
-    counts = [near.shape[0] // WIDE_TILE for near, _ in pieces]
+def gate_up(scalars, pieces, w_gate, w_up, fetched, first, total, part, kept=None, after=(), share=1):
+    width = pieces[0][0].shape[-1]
+    counts = [piece[0].shape[-2] // WIDE_TILE for piece in pieces]
     steps = sum(counts)
     offset = first // WIDE_TILE
     starts = [sum(counts[:i]) for i in range(len(counts))]
 
     def kernel(s, *refs):
-        halves = refs[:2 * len(pieces)]
-        wg, wu, *fetched = refs[2 * len(pieces):2 * len(pieces) + 2 + CHUNKED]
+        halves, refs = refs[:given], refs[given:]
+        wg, wu, *fetched = refs[:2 + CHUNKED]
         b, z, up_slope, gate_slope, w, sems = refs[-6:]
         step = pl.program_id(0)
 
@@ -316,21 +323,28 @@
         def _():
             load_gate_up(s, wg, wu, fetched, w, sems, part, width)
 
-        def fill(near, far):
-            @pl.when(s[SAME] == 1)
+        def fill(*piece):
+            if len(piece) == 1:
+                near, far, straight = piece[0].at[0], piece[0].at[1], s[ROW] == 0
+            else:
+                near, far, straight = *piece, s[SAME] == 1
+
+            @pl.when(straight)
             def _():
                 b[:, :width] = near[...]
                 b[:, width:] = far[...]
 
-            @pl.when(s[SAME] == 0)
+            @pl.when(jnp.logical_not(straight))
             def _():
                 b[:, :width] = far[...]
                 b[:, width:] = near[...]
 
-        for i in range(len(pieces)):
-            pl.when((step >= starts[i]) & (step < starts[i] + counts[i]))(
-                functools.partial(fill, halves[2 * i], halves[2 * i + 1])
+        at = 0
+        for piece, start, count in zip(pieces, starts, counts):
+            pl.when((step >= start) & (step < start + count))(
+                functools.partial(fill, *halves[at:at + len(piece)])
             )
+            at += len(piece)
 
         both = dot(b[...], w[...])
         gate, upward = both[:, :part], both[:, part:]
@@ -342,12 +356,15 @@
         up_slope[...] = silu.astype(BF)
         gate_slope[...] = (upward * sigma * (1.0 + gate * (1.0 - sigma))).astype(BF)
 
-    def block(start, count):
+    def block(array, start, count):
+        if len(array.shape) == 3:
+            return pl.BlockSpec((2, WIDE_TILE, width), lambda i: (0, jnp.clip(i - start, 0, count - 1), 0))
         return pl.BlockSpec((WIDE_TILE, width), lambda i: (jnp.clip(i - start, 0, count - 1), 0))
 
     ins = [(scalars, SCALARS)]
-    for pair, start, count in zip(pieces, starts, counts):
-        ins += [(array, block(start, count)) for array in pair]
+    for piece, start, count in zip(pieces, starts, counts):
+        ins += [(array, block(array, start, count)) for array in piece]
+    given = len(ins) - 1
     ins += [(array, ANY) for array in (w_gate, w_up, *fetched)]
     aliases = {}
     if kept is not None:
@@ -362,7 +379,7 @@
                + [pl.BlockSpec((WIDE_TILE, part), at)] * 3,
                scratch=[pltpu.VMEM((2 * width, 2 * part), BF), pltpu.SemaphoreType.DMA((2 + CHUNKED,))],
                aliases=aliases,
-               estimate=cost(8 * length * width * part, 12 * MIB + length * 12000, length * part),
+               estimate=cost(share * 8 * length * width * part, share * 12 * MIB, share * length * part),
                name="gate_up")
 
 
@@ -382,6 +399,10 @@
         for i, src in enumerate(srcs):
             group, side, token = i // 4, (i // 2) % 2, i % 2
             place = jnp.where(s[SAME] == 1, token, 1 - token) * length
+            if i == len(srcs) - 1:
+                place = (1 - s[ROW]) * length
+            elif i == len(srcs) - 2:
+                place = s[ROW] * length
             pairs.append((src, out.at[rows_at(2 * group * length + place, length),
                                       side * width:(side + 1) * width]))
         copies(pairs, sems)
@@ -402,9 +423,6 @@
 
 
 def hold(array, *after):
-    if not after:
-        return array
-
     def kernel(src, out):
         pass
 
@@ -598,7 +616,7 @@
 
     def kernel(s, low, q, k, v, lse, seg_col, seg_row, w_out, *refs):
         out_fetched, (wq, wk, wv), refs = refs[:QUARTERS], refs[QUARTERS:QUARTERS + 3], refs[QUARTERS + 3:]
-        fetched, (cosine, sine, back, part, bias, wo, w, do, dk, dv) = refs[:QUARTERS], refs[QUARTERS:]
+        fetched, (cosine, sine, back, bias, part, wo, w, do, dk, dv) = refs[:QUARTERS], refs[QUARTERS:]
         wo[:, :width] = w_out[...]
         for piece, rows in placed(s, out_fetched, 0, qw):
             wo[rows, width:] = piece[...]
@@ -641,7 +659,7 @@
     arrays = [low, q, k, v, lse, seg_col, seg_row, w_out, *out_fetched, w_query, w_key, w_value,
               *qkv_fetched, cosine, sine]
     return run(kernel, [(scalars, SCALARS)] + [(a, WHOLE) for a in arrays],
-               [shape((length, total), BF), shape((2, length, 2 * width), BF), shape((1, total), F32)],
+               [shape((length, total), BF), shape((1, total), F32), shape((2, length, 2 * width), BF)],
                after=after,
                scratch=[pltpu.VMEM((qw, 2 * width), BF), pltpu.VMEM((2 * width, total), BF),
                         pltpu.VMEM((length, qw), BF), pltpu.VMEM((length, kw), F32),
@@ -687,6 +705,162 @@
                out_specs=[tiled(outs[0], tile)[1], fixed(outs[1])[1]],
                scratch=[pltpu.VMEM((tile, 2 * width), F32)],
                estimate=cost(length * width * 30, 16 * MIB), name="input_back")
+
+
+def halve(scalars, keep, recv, bit, after=()):
+    parts, many, _, rows, columns = keep.shape
+
+    def kernel(s, keep, recv, kept, sent):
+        total = (keep[0, 0].astype(F32) + recv[0, 0].astype(F32)).astype(BF)
+
+        @pl.when(s[BITS + bit] == 0)
+        def _():
+            kept[0, 0] = total[0]
+            sent[0, 0] = total[1]
+
+        @pl.when(s[BITS + bit] == 1)
+        def _():
+            kept[0, 0] = total[1]
+            sent[0, 0] = total[0]
+
+    wide = pl.BlockSpec((1, 1, 2, rows, columns), lambda i, j: (i, j, 0, 0, 0))
+    narrow = pl.BlockSpec((1, 1, rows, columns), lambda i, j: (i, j, 0, 0))
+    return run(kernel, [(scalars, SCALARS), (keep, wide), (recv, wide)],
+               [shape((parts, many, rows, columns), BF)] * 2, after=after, grid=(parts, many),
+               out_specs=[narrow] * 2, estimate=cost(GLUE), name="halve")
+
+
+def sum_rows(keep, recv, after=()):
+    _, pieces, rows, columns = keep.shape
+
+    def kernel(keep, recv, near, sent):
+        near[0] = (keep[0, 0].astype(F32) + recv[0, 0].astype(F32)).astype(BF)
+        sent[0] = (keep[1, 0].astype(F32) + recv[1, 0].astype(F32)).astype(BF)
+
+    wide = pl.BlockSpec((2, 1, rows, columns), lambda i: (0, i, 0, 0))
+    narrow = pl.BlockSpec((1, rows, columns), lambda i: (i, 0, 0))
+    return run(kernel, [(keep, wide), (recv, wide)], [shape((pieces, rows, columns), BF)] * 2, after=after,
+               grid=(pieces,), out_specs=[narrow] * 2, estimate=cost(GLUE),
+               name="sum_rows")
+
+
+def deal_near(scalars, near, far, after=()):
+    def kernel(s, near, far, own, sent):
+        for bit, out in ((s[BITS + 1], own), (1 - s[BITS + 1], sent)):
+            out[s[ROW]] = near[bit]
+            out[1 - s[ROW]] = far[bit]
+
+    return run(kernel, [(scalars, SCALARS), (near, WHOLE), (far, WHOLE)], [shape(near.shape, BF)] * 2,
+               after=after, estimate=cost(GLUE), name="deal_near")
+
+
+def lay_columns(scalars, own, across, overlap, after=()):
+    _, rows, part = own.shape
+    total = PARTS * part - overlap
+
+    def kernel(s, own, across, out):
+        def fill(first, second):
+            for i, piece in enumerate((first[0], first[1], second[0])):
+                out[:, i * part:(i + 1) * part] = piece.astype(F32)
+            out[:, 3 * part:] = second[1][:, overlap:].astype(F32)
+
+        pl.when(s[BITS + 1] == 0)(lambda: fill(own, across))
+        pl.when(s[BITS + 1] == 1)(lambda: fill(across, own))
+
+    return run(kernel, [(scalars, SCALARS), (own, WHOLE), (across, WHOLE)], [shape((rows, total), F32)],
+               after=after, estimate=cost(GLUE), name="lay_columns")[0]
+
+
+def sum_plain(keep, recv, after=()):
+    def kernel(keep, recv, out):
+        out[...] = keep[...].astype(F32) + recv[...].astype(F32)
+
+    return run(kernel, [(keep, WHOLE), (recv, WHOLE)], [shape(keep.shape, F32)], after=after,
+               estimate=cost(GLUE), name="sum_plain")[0]
+
+
+def sum_split(keep, recv, widths, after=()):
+    rows = keep.shape[1]
+
+    def kernel(keep, recv, *outs):
+        at = 0
+        for out, width in zip(outs, widths):
+            part = slice(at, at + width)
+            out[...] = keep[0, :, part].astype(F32) + recv[0, :, part].astype(F32)
+            at += width
+
+    return run(kernel, [(keep, WHOLE), (recv, WHOLE)], [shape((rows, width), F32) for width in widths],
+               after=after, estimate=cost(GLUE), name="sum_split")
+
+
+def sum_far(keep, send, first, after=()):
+    width = keep.shape[1]
+    half = width // 2
+    offset = first // half
+
+    def kernel(keep, send, to_row, to_near):
+        value = (keep[...].astype(F32) + send[...].astype(F32)).astype(BF)
+        pl.when(pl.program_id(0) == 0)(lambda: to_row.__setitem__(..., value))
+        pl.when(pl.program_id(0) == 1)(lambda: to_near.__setitem__(..., value))
+
+    block = pl.BlockSpec((half, width), lambda i: (offset + i, 0))
+    return run(kernel, [(keep, block), (send, block)], [shape((half, width), BF)] * 2, after=after, grid=(2,),
+               out_specs=[pl.BlockSpec((half, width), lambda i: (0, 0))] * 2,
+               estimate=cost(GLUE), name="sum_far")
+
+
+def sum_near(keep, send, via_row, via_near, first, after=()):
+    half, width = via_row.shape
+    length = 2 * half
+    offset = first // length
+
+    def kernel(keep, send, via_row, via_near, to_row, to_near):
+        step = pl.program_id(0)
+
+        def put(out, plain, more, via):
+            out[plain, :] = (keep[plain, :].astype(F32) + send[plain, :].astype(F32)).astype(BF)
+            out[more, :] = (keep[more, :].astype(F32) + send[more, :].astype(F32)
+                            + via[...].astype(F32)).astype(BF)
+
+        low, high = slice(0, half), slice(half, length)
+        pl.when(step == 0)(lambda: put(to_row, low, high, via_near))
+        pl.when(step == 1)(lambda: put(to_near, high, low, via_row))
+
+    block = pl.BlockSpec((length, width), lambda i: (offset + i, 0))
+    whole = pl.BlockSpec((length, width), lambda i: (0, 0))
+    return run(kernel, [(keep, block), (send, block), fixed(via_row), fixed(via_near)],
+               [shape((length, width), BF)] * 2, after=after, grid=(2,), out_specs=[whole, whole],
+               estimate=cost(GLUE), name="sum_near")
+
+
+def sum_own(keep, send, via_row, via_near, after=()):
+    length, width = via_row.shape
+
+    def kernel(keep, send, via_row, via_near, out):
+        value = (keep[...].astype(F32) + send[...].astype(F32)) + (
+            via_row[...].astype(F32) + via_near[...].astype(F32))
+        out[0] = value.astype(BF)
+        out[1] = value.astype(BF)
+
+    outs = [shape((2, length, width), BF)]
+    return run(kernel, [tiled(a, TILE) for a in (keep, send, via_row, via_near)], outs, after=after,
+               grid=(length // TILE,), out_specs=[both_tiled(outs[0], TILE)[1]],
+               estimate=cost(GLUE), name="sum_own")[0]
+
+
+def sum_output(scalars, keep, send, via_row, via_near, h, after=()):
+    length, width = via_row.shape
+
+    def kernel(s, keep, send, via_row, via_near, h, out):
+        value = (keep[...].astype(F32) + send[...].astype(F32)) + (
+            via_row[...].astype(F32) + via_near[...].astype(F32))
+        pl.when(s[SAME] == 1)(lambda: out.__setitem__(..., (h[:, :width] + value).astype(BF)))
+        pl.when(s[SAME] == 0)(lambda: out.__setitem__(..., (h[:, width:] + value).astype(BF)))
+
+    outs = [shape((length, width), BF)]
+    return run(kernel, [(scalars, SCALARS)] + [tiled(a, TILE) for a in (keep, send, via_row, via_near, h)],
+               outs, after=after, grid=(length // TILE,), out_specs=[tiled(outs[0], TILE)[1]],
+               estimate=cost(GLUE), name="sum_output")[0]
 
 
 def body(
@@ -734,45 +908,39 @@
         [same.astype(jnp.int32), inner, start_of(mine_part), start_of(near_bit * 2 + 1 - row),
          jnp.where(mine_part == PARTS - 1, overlap, 0), place_of(inner, near_bit),
          place_of(1 - inner, near_bit), place_of(inner, 1 - near_bit), place_of(1 - inner, 1 - near_bit), row]
+        + [(group >> bit) % 2 for bit in range(groups.bit_length() - 1)]
     ).astype(jnp.int32)
 
     def by_row(mine, other):
         return jnp.where(same, mine, other), jnp.where(same, other, mine)
 
+    LAST.clear()
     half = width // 2
     gains = jnp.stack([gain_one, gain_two])
     fetched_gains = swap_row(gains)
     mine = turn_square(inputs)
-    sent_qkv = pack_weights(scalars, [w_query, w_key, w_value], None, (width // 4, total_width), OWN)
-    qkv_direct = swap_row(sent_qkv)
-    cot_near = swap_bit(cotangent, 1)
-    mine = hold(mine, sent_qkv)
     other = swap_col(mine)
-    sent_out = pack_weights(
-        scalars, [w_out], None, (query_width // 4, width), OWN, after=[qkv_direct]
-    )
-    out_direct = swap_row(sent_out)
-    sent_gu = []
-    for chunk in range(2):
-        sent_gu.append(pack_weights(
-            scalars, [w_gate, w_up], part, (width // 4, 2 * part), INNER, scale=2, chunk=chunk,
-            after=[out_direct, fetched_gains] + sent_gu,
+    def pack_gate_up(chunk):
+        return swap_row(pack_weights(
+            scalars, [w_gate, w_up], part, (width // 4, 2 * part), INNER, scale=2, chunk=chunk
         ))
-    gu_direct = [swap_row(sent) for sent in sent_gu]
-    fetched_gains = fetched_gains.astype(F32)
-    gains = gains.astype(F32)
-
-    def relay_far(direct, pair, near, *after):
-        pair, near = hold(pair, *after), hold(near, *after)
+
+    def relay(direct):
+        pair, near = swap_bit(direct, 0), swap_bit(direct, 1)
         cut = direct.shape[0] // 2
         return direct, pair, near, swap_bit(pair[:cut], 1), swap_bit(near[cut:], 0)
 
-    def relay_near(direct):
-        return direct, swap_bit(direct, 0), swap_bit(direct, 1)
-
-    cot_near = hold(cot_near, sent_gu[1])
-    qkv_fetched = relay_far(*relay_near(qkv_direct), sent_gu[1])
-    out_fetched = relay_far(*relay_near(out_direct), sent_gu[1])
+    qkv_fetched = relay(swap_row(
+        pack_weights(scalars, [w_query, w_key, w_value], None, (width // 4, total_width), OWN)
+    ))
+    out_fetched = relay(swap_row(
+        pack_weights(scalars, [w_out], None, (query_width // 4, width), OWN)
+    ))
+    fetched_gains = hold(fetched_gains).astype(F32)
+    gains = gains.astype(F32)
+    gu_direct = [pack_gate_up(0), pack_gate_up(1)]
+    gu_first = hold(gu_direct[0])
+    gu_fetched = [gu_first, swap_bit(gu_first, 0)]
 
     indices = jnp.arange(HD // 2, dtype=F32)
     inverse = jnp.exp(indices * (-2.0 / HD) * jnp.log(F32(THETA)))
@@ -785,174 +953,186 @@
 
     q, k, v, low_one, r_one = project(
         scalars, mine, other, gains[:1], fetched_gains[:1], w_query, w_key, w_value, qkv_fetched,
-        bias, cosine, sine, after=sent_gu[1:] + [cot_near],
+        bias, cosine, sine,
     )
-
-    gu_first = hold(gu_direct[0], k)
-    gu_fetched = [gu_first, swap_bit(gu_first, 0)]
-    cot = copy_of(cotangent, after=[k])
+    cot = copy_of(cotangent, [])
     cot_row = swap_row(cot)
-    attended, lse, out_part = attend(scalars, q, k, v, seg_col, seg_row, w_out, out_fetched, after=[gu_first, cot])
-    gu_second = hold(gu_direct[1], lse)
+    cot_near = swap_bit(cot, 1)
+    attended, lse, out_part = attend(scalars, q, k, v, seg_col, seg_row, w_out, out_fetched)
+    gu_second = hold(gu_direct[1])
     gu_fetched += [gu_second, swap_bit(gu_second, 0)]
+    cot_other = swap_col(cot)
+    gu_fetched[1] = hold(gu_fetched[1])
+    cot_other = hold(cot_other)
+    cot_near = hold(cot_near)
     h, low_near, low_far, r_two = norm_two(
-        scalars, mine, other, trade_col(hold(out_part, gu_second)), gains[1:], fetched_gains[1:],
-        after=[gu_fetched[1]],
+        scalars, mine, other, trade_col(out_part), gains[1:], fetched_gains[1:]
     )
 
     b_row = swap_row(low_near)
     b_near = swap_bit(low_near, 1)
-    cot_row = hold(cot_row, low_near)
+    cot_row = hold(cot_row)
     cot_low = swap_bit(cot_row[:half], 1)
     tokens = 4 * length
     ffn = functools.partial(
         gate_up, scalars, w_gate=w_gate, w_up=w_up, fetched=gu_fetched, total=tokens, part=part,
     )
-    kept = ffn([(low_near, low_far)], first=0, after=[cot_row])
-    b_row, b_near = hold(b_row, kept[1]), hold(b_near, kept[1])
-    b_row_other, b_near_other = swap_col(b_row), swap_col(b_near)
+    kept = ffn([(low_near, low_far)], first=0)
+    b_row = hold(b_row)
+    b_row_other = swap_col(b_row)
     b_low = swap_bit(b_row[:half], 1)
+    b_near = hold(b_near)
+    b_near_other = swap_col(b_near)
     b_high = swap_row(b_near[half:])
-    cot_near = hold(cot_near, b_near_other)
-    cot_high = swap_row(cot_near[half:])
-    sent_down = pack_weights(
-        scalars, [w_down], None, (part // 2, width), INNER, after=[cot_near], down=True
+    b_row_other, b_near_other = hold(b_row_other), hold(b_near_other)
+    cot_high = swap_row(hold(cot_near[half:]))
+    sent_down = pack_weights(scalars, [w_down], None, (part // 2, width), INNER, down=True)
+    down_direct = swap_row(sent_down)
+    kept = ffn([(b_row, b_row_other), (b_near, b_near_other)], first=length, kept=kept)
+    b_far = jnp.concatenate([hold(b_low), hold(b_high)], axis=0)
+    b_far = trade_col(jnp.stack([b_far, b_far]))
+    cot_row_other, cot_near_other = swap_col(cot_row), swap_col(cot_near)
+    kept = ffn([(b_far,)], first=3 * length, kept=kept, after=[sent_down], share=0)
+    full_two, hidden, up_slope, gate_slope = kept
+    cot_row_other, cot_near_other = hold(cot_row_other), hold(cot_near_other)
+    cot_far = jnp.concatenate([hold(cot_low), hold(cot_high)], axis=0)
+    cot_far = trade_col(jnp.stack([cot_far, cot_far]))
+    down_direct = hold(down_direct)
+    down_fetched = down_direct, swap_bit(down_direct, 0)
+    full_cot = place_rows(
+        scalars, [[(cot, cot_other), (cot_row, cot_row_other)],
+                  [(cot_near, cot_near_other), (cot_far[0], cot_far[1])]],
     )
-    down_direct = swap_row(sent_down)
-    kept = ffn([(b_row, b_row_other), (b_near, b_near_other)], first=length, kept=kept, after=[sent_down])
-    b_low, b_high, cot_low, cot_high, down_direct = (
-        hold(array, kept[1]) for array in (b_low, b_high, cot_low, cot_high, down_direct)
-    )
-    down_fetched = down_direct, swap_bit(down_direct, 0)
-    cot_far = jnp.concatenate([cot_low, cot_high], axis=0)
-    cot_pieces = [[(one, swap_col(one)) for one in pair] for pair in ((cot, cot_row), (cot_near, cot_far))]
-    kept = ffn([(b_low, swap_col(b_low)), (b_high, swap_col(b_high))], first=3 * length, kept=kept)
-    full_two, hidden, up_slope, gate_slope = kept
-    full_cot = place_rows(scalars, cot_pieces, after=[hidden])
 
     piece = width // groups
     down_keep, down_send = weight_grad(scalars, full_cot, hidden, piece, part)
-    low_back = hidden_back(
-        scalars, full_cot, up_slope, gate_slope, w_down, down_fetched, after=[down_send]
-    )
+    down_recv = swap_bit(down_send, 0)
+    low_back = hidden_back(scalars, full_cot, up_slope, gate_slope, w_down, down_fetched)
     back = functools.partial(
         norm_back, scalars, low_back, w_gate, w_up, gu_fetched
     )
-
-    def sum_far(keep, send):
-        across = (keep.astype(F32) + send.astype(F32)).astype(BF)
-        return across[:half], across[half:]
-
-    def sum_near(keep, send, via_row, via_near):
-        to_row = keep[:length].astype(F32) + send[:length].astype(F32)
-        to_near = keep[length:].astype(F32) + send[length:].astype(F32)
-        to_row = jnp.concatenate([to_row[:half], to_row[half:] + via_near.astype(F32)], axis=0)
-        to_near = jnp.concatenate([to_near[:half] + via_row.astype(F32), to_near[half:]], axis=0)
-        return to_row.astype(BF), to_near.astype(BF)
-
-    def sum_own(keep, send, via_row, via_near):
-        return (keep.astype(F32) + send.astype(F32)) + (via_row.astype(F32) + via_near.astype(F32))
-
     far_both = trade_col(back(3 * length, length, stacked=True)[0])
-    to_row, to_near = sum_far(far_both[0], far_both[1])
-    own_keep, own_send = back(0, length, after=[to_row, to_near])
-    two_keep, two_send = back(length, 2 * length, after=[own_send])
+    across = (far_both[0].astype(F32) + far_both[1].astype(F32)).astype(BF)
+    to_row, to_near = across[:half], across[half:]
+    rest_keep, rest_send = back(0, 3 * length, after=[to_row, to_near])
     via_row, via_near = swap_row(to_row), swap_bit(to_near, 1)
-    gate_keep, gate_send = weight_grad(scalars, full_two, low_back, piece, part, 0, after=[two_send])
-    two_got = hold(swap_col(two_send), gate_send)
-    via_row, via_near = hold(via_row, gate_send), hold(via_near, gate_send)
-    to_row, to_near = sum_near(two_keep, two_got, via_row, via_near)
+    gate_keep, gate_send = weight_grad(scalars, full_two, low_back, piece, part, 0)
+    gate_recv = swap_bit(gate_send, 0)
+    rest_got = swap_col(rest_send)
+    to_row, to_near = sum_near(rest_keep, rest_got, via_row, via_near, length)
     via_row, via_near = swap_row(to_row), swap_bit(to_near, 1)
-    own_got = swap_col(own_send)
-    out_keep, out_send = down_project(scalars, hidden, w_down, down_fetched, after=[to_row, to_near])
-    up_keep, up_send = weight_grad(scalars, full_two, low_back, piece, part, 1, after=[out_send])
-    via_row, via_near = hold(via_row, up_send), hold(via_near, up_send)
-    normed_grad = sum_own(own_keep, own_got, via_row, via_near).astype(BF)
+
+    high_bits = range(2, groups.bit_length() - 1)
+
+    def grad_high(keep, recv):
+        for bit in high_bits:
+            cut = (2, keep.size // (4 * 2 * piece * part), 2, 2 * piece, part)
+            keep, send = halve(scalars, keep.reshape(cut), recv.reshape(cut), bit)
+            recv = swap_bit(send, bit)
+        return keep, recv
+
+    def grad_row(keep, recv):
+        cut = (2, 2, piece, part)
+        near, send = sum_rows(keep.reshape(cut), recv.reshape(cut))
+        return near, swap_row(send)
+
+    def grad_near(near, far):
+        own, send = deal_near(scalars, near, far)
+        return own, swap_bit(send, 1)
+
+    def square_first(left, right):
+        keep, send = weight_grad(scalars, left, right, piece, right.shape[1])
+        return keep, swap_bit(send, 0)
+
+    def square_next(keep, recv, bit):
+        cut = (2, groups >> (bit + 1), 2, piece, keep.shape[-1])
+        keep, send = halve(scalars, keep.reshape(cut), recv.reshape(cut), bit)
+        return keep, swap_bit(send, bit)
+
+    def square_row(keep, recv):
+        near, send = sum_rows(keep, recv)
+        return near, swap_row(send)
+
+    def square_last(near, far):
+        return sum_plain(near, far).reshape(piece, -1)
+
+    last_bits = range(2, groups.bit_length() - 1)
+
+    down = grad_high(down_keep, down_recv)
+    out_keep, out_send = down_project(scalars, hidden, w_down, down_fetched)
+    out_got = swap_col(out_send)
+    up_keep, up_send = weight_grad(scalars, full_two, low_back, piece, part, 1)
+    up_recv = swap_bit(up_send, 0)
+    normed_grad = sum_own(rest_keep, rest_got, via_row, via_near)
+    first = 3 * length
+    to_row, to_near = sum_far(out_keep, out_got, first)
+    via_row, via_near = swap_row(to_row), swap_bit(to_near, 1)
     dh, low_mid, gain_two_part = middle_back(
-        scalars, trade_col(jnp.stack([normed_grad, normed_grad])), h, r_two, gains[1:], fetched_gains[1:],
-        full_cot,
+        scalars, trade_col(normed_grad), h, r_two, gains[1:], fetched_gains[1:], full_cot,
     )
-    out_grad_keep, out_grad_send = small_grad(low_mid, attended)
-    first = 3 * length
-    out_got = hold(swap_col(out_send), out_grad_send)
-    to_row, to_near = sum_far(out_keep[first:], out_got[first:])
-    back_low, in_part, bias_part = attend_back(
+    gate = grad_high(gate_keep, gate_recv)
+    to_row, to_near = sum_near(out_keep, out_got, via_row, via_near, length)
+    via_row, via_near = swap_row(to_row), swap_bit(to_near, 1)
+    up_recv = hold(up_recv)
+    out_sum = square_first(low_mid, attended)
+    down = grad_row(*down)
+    back_low, bias_part, in_part = attend_back(
         scalars, low_mid, q, k, v, lse, seg_col, seg_row, w_out, out_fetched, w_query, w_key,
-        w_value, qkv_fetched, cosine, sine, after=[out_grad_send, to_row, to_near],
+        w_value, qkv_fetched, cosine, sine,
     )
-    via_row, via_near = hold(swap_row(to_row), back_low), hold(swap_bit(to_near, 1), back_low)
-    qkv_grad_keep, qkv_grad_send = small_grad(low_one, back_low)
-    to_row, to_near = sum_near(out_keep[length:first], out_got[length:first], via_row, via_near)
+    down = down[0], hold(down[1])
+    qkv_sum = square_first(low_one, back_low)
+    via_row, via_near = hold(via_row), hold(via_near)
+    up = grad_high(up_keep, up_recv)
     input_grad, gain_one_part = input_back(
-        scalars, trade_col(hold(in_part, qkv_grad_send)), mine, other, r_one, gains[:1], fetched_gains[:1], dh,
-        after=[qkv_grad_send, to_row, to_near],
+        scalars, trade_col(in_part), mine, other, r_one, gains[:1], fetched_gains[:1], dh
     )
-    via_row, via_near = swap_row(to_row), swap_bit(to_near, 1)
-    branch = sum_own(out_keep[:length], out_got[:length], via_row, via_near)
-    h_mine, _ = by_row(h[:, :width], h[:, width:])
-    output = turn_square((h_mine + branch).astype(BF))
-    input_grad_low = input_grad
-    input_grad = turn_square(input_grad).astype(F32)
-
-    def add_bits(kept, sent, low_bits, after=()):
-        value = kept.astype(F32) + sent.astype(F32)
-        bits = (groups >> low_bits).bit_length() - 1
-        for index in range(bits):
-            bit = (group >> (low_bits + index)) % 2
-            cut = value.reshape((value.shape[0], value.shape[1] // 2, 2) + value.shape[2:])
-            recv = swap_bit(pick(cut, 1 - bit, 2).astype(BF), low_bits + index)
-            if after:
-                recv = hold(recv, *after)
-            value = pick(cut, bit, 2) + recv.astype(F32)
-        return value
-
-    def ffn_sum(keep, send, steps):
-        steps = [[step] if step is not None else [] for step in steps]
-        recv = hold(swap_bit(send, 0), *steps[0])
-        parts = (2, keep.shape[1] // 2, 2 * piece, keep.shape[3])
-        value = add_bits(keep.reshape(parts), recv.reshape(parts), 2, after=steps[1])[:, 0]
-        near, far = value[0], hold(swap_row(value[1].astype(BF)), *steps[2]).astype(F32)
-        near, far = near.reshape(2, piece, -1), far.reshape(2, piece, -1)
-        pair = jnp.stack([jnp.where(row == 0, near, far), jnp.where(row == 0, far, near)], axis=1)
-        own = pick(pair, near_bit)
-        across = hold(swap_bit(pick(pair, 1 - near_bit).astype(BF), 1), *steps[3]).astype(F32)
-        four = jnp.concatenate(
-            [jnp.where(near_bit == 0, own, across), jnp.where(near_bit == 0, across, own)], axis=0
-        )
-        last = four[PARTS - 1][:, overlap:]
-        return jnp.concatenate([four[i] for i in range(PARTS - 1)] + [last], axis=1)
-
-    down_grad = ffn_sum(down_keep, down_send, [two_send, up_send, low_mid, back_low]).T
-    gate_grad = ffn_sum(gate_keep, gate_send, [low_mid, back_low, qkv_grad_send, None])
-    up_grad = ffn_sum(up_keep, up_send, [back_low, input_grad_low, None, None])
-
-    out_grads = out_grad_keep.astype(F32) + hold(swap_row(out_grad_send), qkv_grad_send).astype(F32)
-    qkv_grads = qkv_grad_keep.astype(F32) + swap_row(qkv_grad_send).astype(F32)
-    grads = jnp.concatenate([qkv_grads, out_grads], axis=1)
-    cut = grads.reshape(groups // 2, 2, piece, -1)
-    recv = swap_bit(pick(cut, 1 - inner, 1).astype(BF), 0)
-    sum_attention = add_bits(pick(cut, inner, 1)[None], recv[None], 1)[0, 0]
+    input_grad = turn_square(input_grad)
 
     def canonical(value):
         first, second = value[:, :width], value[:, width:]
         return jnp.where(row == 0, value, jnp.concatenate([second, first], axis=1))[0]
 
     small = jnp.concatenate([bias_part[0], canonical(gain_one_part), canonical(gain_two_part)])
-    small = small + swap_row(small)
-    for bit in range(groups.bit_length() - 1):
-        small = small + swap_bit(small, bit)
+
+    def small_step(value, swap):
+        return value + hold(swap(value))
+
+    gate = grad_row(*gate)
+    out_sum = square_next(*out_sum, 1)
+    qkv_sum = square_next(*qkv_sum, 1)
+    input_grad = hold(input_grad).astype(F32)
+    output = turn_square(sum_output(scalars, out_keep, out_got, via_row, via_near, h))
+    up = grad_row(*up)
+    for bit in last_bits:
+        out_sum = square_next(*out_sum, bit)
+    gate = grad_near(*gate)
+    down = grad_near(*down)
+    for bit in last_bits:
+        qkv_sum = square_next(*qkv_sum, bit)
+    output = hold(output)
+    small = small_step(small, lambda value: swap_bit(value, 0))
+    gate_grad = lay_columns(scalars, *gate, overlap)
+    out_sum = square_row(*out_sum)
+    up = grad_near(*up)
+    down_grad = lay_columns(scalars, *down, overlap).T
+    for bit in range(1, groups.bit_length() - 1):
+        small = small_step(small, lambda value, bit=bit: swap_bit(value, bit))
+    qkv_sum = square_row(*qkv_sum)
+    out_grad = square_last(*out_sum).T
+    small = small_step(small, swap_row)
+    up_grad = lay_columns(scalars, *up, overlap)
+    qkv_grads = sum_split(*qkv_sum, (query_width, key_width, key_width))
     gain_sums = pick(small[total_width:].reshape(2, 2, width), row, 1)
 
     return (
         output,
         input_grad,
-        sum_attention[:, :query_width],
-        sum_attention[:, query_width : query_width + key_width],
-        sum_attention[:, query_width + key_width : total_width],
+        *qkv_grads,
         small[:query_width],
         small[query_width : query_width + key_width],
         small[query_width + key_width : total_width],
-        sum_attention[:, total_width:].T,
+        out_grad,
         gain_sums[0],
         gain_sums[1],
         gate_grad,

time: 641 us -> 621 us (0.969)
  Pallas kernels: 279 us -> 347 us
  other arithmetic: 53.2 us -> 7.06 us
  waiting for transfers between devices: 126 us -> 91.8 us
  starting transfers between devices: 90 us -> 96.5 us
    pallas_call x63 -> x79, Pallas kernels: 279 us -> 347 us  [run(): pl.pallas_call(body, grid=grid if grid is not None else (), in_specs=[spe...]
    ppermute x20, waiting for transfers between devices: 75.5 us -> 15.2 us  [swap_row(): return lax.ppermute(value, 'row', [(0, 1), (1, 0)])]
    ppermute x34 -> x37, waiting for transfers between devices: 50.8 us -> 76.5 us  [swap_bit(): return lax.ppermute(value, 'dp', [(i, i ^ 1 << bit) for i in range(size)])]
    add x16 -> x4, other arithmetic: 22.8 us -> 0.02 us  [small_step(): return value + hold(swap(value))]
    all_to_all x1 -> x3, starting transfers between devices: 6.07 us -> 16.7 us  [trade_col(): return lax.all_to_all(value, 'col', 0, 0)]
    concatenate x8 -> x0, other arithmetic: 8.77 us -> none  [the longest x2 2.61 us: ffn_sum(): return jnp.concatenate([four[i] for i in range(PARTS - 1)] + [last], axis=1)]
    ppermute x34 -> x37, starting transfers between devices: 44.7 us -> 36.7 us  [swap_bit(): return lax.ppermute(value, 'dp', [(i, i ^ 1 << bit) for i in range(size)])]
    another operation x6 -> x4, other arithmetic: 7.48 us -> 0.56 us  [the longest x2 0.28 us: body(): b_far = trade_col(jnp.stack([b_far, b_far]))]
  transfers between devices with their start and end apart: 70 -> 71, of which waited for: 18 -> 17; matrix products, arithmetic and copies ran while one was open for 11% -> 3% of each run, Pallas kernels for 44% -> 56%
where the time goes in v3:
time: 621 us; the launch traced here: 615 us
  Pallas kernels  347 us (56%)
  starting transfers between devices  96.5 us (16%)
  waiting for transfers between devices  91.8 us (15%)
  local copies, waits for them, and re-layouts  50.6 us (8%)
  blocking collectives  19.6 us (3%)
  other arithmetic  7.06 us (1%)
    pallas_call x79, Pallas kernels, run(): pl.pallas_call(body, grid=grid if grid is not None else (), in_specs=[spe...  347 us
    ppermute x37, waiting for transfers between devices, swap_bit(): return lax.ppermute(value, 'dp', [(i, i ^ 1 << bit) for i in range(size)])  76.5 us
    unnamed x145, local copies, waits for them, and re-layouts  37.7 us
    ppermute x37, starting transfers between devices, swap_bit(): return lax.ppermute(value, 'dp', [(i, i ^ 1 << bit) for i in range(size)])  36.7 us
    ppermute x20, starting transfers between devices, swap_row(): return lax.ppermute(value, 'row', [(0, 1), (1, 0)])  22 us
    all_to_all x3, blocking collectives, trade_col(): return lax.all_to_all(value, 'col', 0, 0)  19.6 us
    all_to_all x3, starting transfers between devices, trade_col(): return lax.all_to_all(value, 'col', 0, 0)  16.7 us
    ppermute x20, waiting for transfers between devices, swap_row(): return lax.ppermute(value, 'row', [(0, 1), (1, 0)])  15.2 us
  transfers between devices with their start and end apart: 71, of which 17 were waited for; matrix products, arithmetic and copies ran while one was open for 3% of the time, Pallas kernels for 56%

profile of v3, /device:TPU:0, one launch (start us, length us, event | category | flops | bytes accessed | tf_op | source)
XLA Modules:
  0.0 614.5 jit_solution(9721280615138138329)
XLA Ops:
  9.7 14.4 %collective-permute-start.1 = (bf16[768,768]{1,0:T(8,128)(2,1)S(1)}, bf16[768,768]{1,0:T(8,128)(2,1)S(1)}, u32[]{:S(2)}, u32[]{:S(2)}) collective-permute-start(bf16[768,768]{1,0:T(8,128)(2,1)S(1)} %collective-permute-done.refs_1_.refs_2_), channel_id=1, source_target_pairs={{0,1},{1,0},{2,3},{3,2},{4,5},{5,4},{6,7},{7,6},{8,9},{9,8},{10,11... | collective-permute-start | bytes 3538952 | tf_op jit(solution)/shard_map/ppermute | solution.py:35
  60.1 8.2 %qkv.1 = (bf16[768,768]{1,0:T(8,128)(2,1)}, bf16[768,128]{1,0:T(8,128)(2,1)}, bf16[768,128]{1,0:T(8,128)(2,1)}, bf16[768,1536]{1,0:T(8,128)(2,1)}, f32[768,1]{1,0:T(8,128)}) custom-call(s32[13]{0:T(128)} %copy-done.27, bf16[768,768]{1,0:T(8,128)(2,1)} %copy-done.30, bf16[768,768]{1,0:T(8,128)(2,1)} %copy-done.31, ...), custom_call_target="tpu_custom_call" | custom-call | flops 24159191040 | bytes 125829120 | tf_op jit(solution)/shard_map/qkv/pallas_call | solution.py:82
  71.9 13.6 %attention.1 = (bf16[768,768]{1,0:T(8,128)(2,1)}, f32[768,128]{1,0:T(8,128)}, bf16[2,768,1536]{2,1,0:T(8,128)(2,1)}) custom-call(s32[13]{0:T(128)} %copy-done.27, bf16[768,768]{1,0:T(8,128)(2,1)} %get-tuple-element.99.refs_1_.refs_2_, bf16[768,128]{1,0:T(8,128)(2,1)} %get-tuple-element.100.refs_2_.refs_3_, ...), custom_call_target="tpu_custom_call" | custom-call | flops 36238786560 | bytes 125829120 | tf_op jit(solution)/shard_map/attention/pallas_call | solution.py:82
  89.4 6.0 all-to-all-start
  100.4 8.7 %norm_two.1 = (f32[768,1536]{1,0:T(8,128)}, bf16[768,768]{1,0:T(8,128)(2,1)}, bf16[768,768]{1,0:T(8,128)(2,1)}, f32[768,1]{1,0:T(8,128)}) custom-call(s32[13]{0:T(128)} %copy-done.27, bf16[768,768]{1,0:T(8,128)(2,1)} %copy-done.30, bf16[768,768]{1,0:T(8,128)(2,1)} %copy-done.31, bf16[2,768,1536]{2,1,0:T(8,128)(2,1)} %all-to-all-done.refs_3_, ...), custom_call_target="tpu_custom_call" | custom-call | flops 117964800 | bytes 167772160 | tf_op jit(solution)/shard_map/norm_two/pallas_call | solution.py:82
  113.0 12.3 %gate_up.3 = (bf16[3072,1536]{1,0:T(8,128)(2,1)}, bf16[3072,1152]{1,0:T(8,128)(2,1)}, bf16[3072,1152]{1,0:T(8,128)(2,1)}, bf16[3072,1152]{1,0:T(8,128)(2,1)}) custom-call(s32[13]{0:T(128)} %copy-done.27, bf16[768,768]{1,0:T(8,128)(2,1)} %get-tuple-element.104.refs_1_, bf16[768,768]{1,0:T(8,128)(2,1)} %get-tuple-element.105.refs_2_, ...), custom_call_target="tpu_custom_call" | custom-call | flops 54358179840 | bytes 125829120 | tf_op jit(solution)/shard_map/gate_up/pallas_call | solution.py:82
  125.2 12.1 %collective-permute-done.18.refs_0_ = bf16[768,768]{1,0:T(8,128)(2,1)} collective-permute-done((bf16[768,768]{1,0:T(8,128)(2,1)}, bf16[768,768]{1,0:T(8,128)(2,1)}, u32[]{:S(2)}, u32[]{:S(2)}) %collective-permute-start.18) | collective-permute-done | bytes 1179680 | tf_op jit(solution)/shard_map/ppermute | solution.py:31
  150.1 6.6 %collective-permute-done.21.refs_0_ = bf16[384,768]{1,0:T(8,128)(2,1)S(1)} collective-permute-done((bf16[384,768]{1,0:T(8,128)(2,1)}, bf16[384,768]{1,0:T(8,128)(2,1)S(1)}, u32[]{:S(2)}, u32[]{:S(2)}) %collective-permute-start.21) | collective-permute-done | bytes 589856 | tf_op jit(solution)/shard_map/ppermute | solution.py:40
  157.5 19.1 %gate_up.4 = (bf16[3072,1536]{1,0:T(8,128)(2,1)}, bf16[3072,1152]{1,0:T(8,128)(2,1)}, bf16[3072,1152]{1,0:T(8,128)(2,1)}, bf16[3072,1152]{1,0:T(8,128)(2,1)}) custom-call(s32[13]{0:T(128)} %copy-done.27, bf16[768,768]{1,0:T(8,128)(2,1)} %hold.36.refs_1_, ...), custom_call_target="tpu_custom_call", output_to_operand_aliasing={{0}: (11, {}), {1}: (12, {}), {2}: (13, {}), {3}: (14, {})} | custom-call | flops 108716359680 | bytes 125829120 | tf_op jit(solution)/shard_map/gate_up/pallas_call | solution.py:82
  178.8 6.5 %all_to_all.30.refs_1_ = bf16[2,768,768]{2,1,0:T(8,128)(2,1)} all-to-all(bf16[2,768,768]{2,1,0:T(8,128)(2,1)S(1)} %pad_maximum_fusion), channel_id=1, replica_groups=mesh['dp'=8,'row'=2,'col'=2] {'col'}, dimensions={0} | all-to-all | bytes 4718592 | tf_op jit(solution)/shard_map/all_to_all | solution.py:44
  185.3 12.3 %gate_up.5 = (bf16[3072,1536]{1,0:T(8,128)(2,1)}, bf16[3072,1152]{1,0:T(8,128)(2,1)}, bf16[3072,1152]{1,0:T(8,128)(2,1)}, bf16[3072,1152]{1,0:T(8,128)(2,1)}) custom-call(s32[13]{0:T(128)} %copy-done.27, bf16[2,768,768]{2,1,0:T(8,128)(2,1)} %all_to_all.30.refs_1_, ...), custom_call_target="tpu_custom_call", output_to_operand_aliasing={{0}: (8, {}), {1}: (9, {}), {2}: (10, {}), {3}: (11, {})} | custom-call | tf_op jit(solution)/shard_map/gate_up/pallas_call | solution.py:82
  198.9 6.1 all_to_all.31
  207.2 7.4 %place_rows.1.refs_1_.refs_3_.refs_6_ = bf16[3072,1536]{1,0:T(8,128)(2,1)} custom-call(s32[13]{0:T(128)S(1)} %copy-done.29, bf16[768,768]{1,0:T(8,128)(2,1)} %copy_of.1.refs_12_.refs_1_, bf16[768,768]{1,0:T(8,128)(2,1)S(1)} %hold.33.refs_1_.refs_2_, bf16[768,768]{1,0:T(8,128)(2,1)} %hold.35.refs_9_.refs_3_, bf16[768,768]{1,0:T(8,128)(2,1)S(1)} %hold.43.refs_1_.refs_4_, ...), custom_call_target="tpu_custom_call" | custom-call | bytes 188743680 | tf_op jit(solution)/shard_map/place_rows/pallas_call | solution.py:82
  214.6 18.7 %weight_grad.5 = (bf16[2,4,96,1152]{3,2,1,0:T(8,128)(2,1)}, bf16[2,4,96,1152]{3,2,1,0:T(8,128)(2,1)}) custom-call(s32[13]{0:T(128)} %copy-done.27, bf16[3072,1536]{1,0:T(8,128)(2,1)} %place_rows.1.refs_1_.refs_3_.refs_6_, bf16[3072,1152]{1,0:T(8,128)(2,1)} %get-tuple-element.115.refs_2_.refs_1_, bf16[3072,1536]{1,0:T(8,128)(2,1)} %place_rows.1.refs_1_.refs_3_.refs_6_), custom_call_target="tpu_custom_call" | custom-call | flops 108716359680 | bytes 235929600 | tf_op jit(solution)/shard_map/weight_grad/pallas_call | solution.py:82
  235.6 21.3 %hidden_back.1.refs_1_.refs_8_.refs_2_ = bf16[3072,2304]{1,0:T(8,128)(2,1)} custom-call(s32[13]{0:T(128)} %copy-done.27, bf16[3072,1536]{1,0:T(8,128)(2,1)} %place_rows.1.refs_1_.refs_3_.refs_6_, bf16[3072,1152]{1,0:T(8,128)(2,1)} %get-tuple-element.119.refs_2_, bf16[3072,1152]{1,0:T(8,128)(2,1)} %get-tuple-element.116.refs_1_.refs_3_, ...), custom_call_target="tpu_custom_call" | custom-call | flops 108716359680 | bytes 430080000 | tf_op jit(solution)/shard_map/hidden_back/pallas_call | solution.py:82
  256.9 11.7 %norm_back.2.refs_10_ = bf16[2,768,768]{2,1,0:T(8,128)(2,1)} custom-call(s32[13]{0:T(128)} %copy-done.27, bf16[3072,2304]{1,0:T(8,128)(2,1)} %hidden_back.1.refs_1_.refs_8_.refs_2_, bf16[768,4480]{1,0:T(8,128)(2,1)} %refs_2_.12, bf16[768,4480]{1,0:T(8,128)(2,1)} %refs_3_.9, bf16[192,2304]{1,0:T(8,128)(2,1)} %hold.30.refs_16_.refs_5_.refs_7_.refs_4_, ...), custom_call_target="tpu_custom_call" | custom-call | flops 54358179840 | bytes 145326080 | tf_op jit(solution)/shard_map/norm_back/pallas_call | solution.py:82
  268.6 7.0 %all_to_all.32 = bf16[2,768,768]{2,1,0:T(8,128)(2,1)S(1)} all-to-all(bf16[2,768,768]{2,1,0:T(8,128)(2,1)} %norm_back.2.refs_10_), channel_id=1, replica_groups=mesh['dp'=8,'row'=2,'col'=2] {'col'}, dimensions={0} | all-to-all | bytes 4718592 | tf_op jit(solution)/shard_map/all_to_all | solution.py:44
  279.4 24.3 %norm_back.3 = (bf16[2304,768]{1,0:T(8,128)(2,1)}, bf16[2304,768]{1,0:T(8,128)(2,1)}) custom-call(s32[13]{0:T(128)} %copy-done.27, bf16[3072,2304]{1,0:T(8,128)(2,1)} %hidden_back.1.refs_1_.refs_8_.refs_2_, bf16[768,4480]{1,0:T(8,128)(2,1)} %refs_2_.12, bf16[768,4480]{1,0:T(8,128)(2,1)} %refs_3_.9, bf16[192,2304]{1,0:T(8,128)(2,1)} %hold.30.refs_16_.refs_5_.refs_7_.refs_4_, ...), custom_call_target="tpu_custom_call" | custom-call | flops 163074539520 | bytes 268206080 | tf_op jit(solution)/shard_map/norm_back/pallas_call | solution.py:82
  303.8 18.7 %weight_grad.6 = (bf16[2,4,96,1152]{3,2,1,0:T(8,128)(2,1)}, bf16[2,4,96,1152]{3,2,1,0:T(8,128)(2,1)}) custom-call(s32[13]{0:T(128)} %copy-done.27, bf16[3072,1536]{1,0:T(8,128)(2,1)} %get-tuple-element.122.refs_1_, bf16[3072,2304]{1,0:T(8,128)(2,1)} %hidden_back.1.refs_1_.refs_8_.refs_2_, bf16[2304,768]{1,0:T(8,128)(2,1)} %get-tuple-element.121.refs_3_), custom_call_target="tpu_custom_call" | custom-call | flops 108716359680 | bytes 235929600 | tf_op jit(solution)/shard_map/weight_grad/pallas_call | solution.py:82
  334.4 18.9 %down_project.1 = (bf16[3072,768]{1,0:T(8,128)(2,1)}, bf16[3072,768]{1,0:T(8,128)(2,1)}) custom-call(s32[13]{0:T(128)} %copy-done.27, bf16[3072,1152]{1,0:T(8,128)(2,1)} %get-tuple-element.115.refs_2_.refs_1_, bf16[4480,768]{1,0:T(8,128)(2,1)} %refs_2_.13, bf16[576,768]{1,0:T(8,128)(2,1)} %hold.47.refs_9_.refs_5_.refs_3_, bf16[576,768]{1,0:T(8,128)(2,1)} %copy-done.48, ...), custom_call_target="tpu_custom_call" | custom-call | flops 108716359680 | bytes 245760000 | tf_op jit(solution)/shard_map/down_project/pallas_call | solution.py:82
  353.5 18.9 %weight_grad.7 = (bf16[2,4,96,1152]{3,2,1,0:T(8,128)(2,1)}, bf16[2,4,96,1152]{3,2,1,0:T(8,128)(2,1)}) custom-call(s32[13]{0:T(128)} %copy-done.27, bf16[3072,1536]{1,0:T(8,128)(2,1)} %get-tuple-element.122.refs_1_, bf16[3072,2304]{1,0:T(8,128)(2,1)} %hidden_back.1.refs_1_.refs_8_.refs_2_, bf16[3072,768]{1,0:T(8,128)(2,1)} %get-tuple-element.127.refs_3_), custom_call_target="tpu_custom_call" | custom-call | flops 108716359680 | bytes 235929600 | tf_op jit(solution)/shard_map/weight_grad/pallas_call | solution.py:82
  391.2 9.5 %middle_back.1 = (f32[768,1536]{1,0:T(8,128)}, bf16[768,1536]{1,0:T(8,128)(2,1)}, f32[1,1536]{1,0:T(1,128)}) custom-call(s32[13]{0:T(128)} %copy-done.27, bf16[2,768,768]{2,1,0:T(8,128)(2,1)} %all-to-all-done.4.refs_1_, f32[768,1536]{1,0:T(8,128)} %get-tuple-element.133.refs_2_.refs_5_, f32[768,1]{1,0:T(8,128)} %get-tuple-element.106.refs_1_.refs_3_, ...), custom_call_target="tpu_custom_call" | custom-call | flops 176947200 | bytes 209715200 | tf_op jit(solution)/shard_map/middle_back/pallas_call | solution.py:82
  405.0 12.9 %collective-permute-done.40.refs_3_ = bf16[384,768]{1,0:T(8,128)(2,1)S(1)} collective-permute-done((bf16[384,768]{1,0:T(8,128)(2,1)}, bf16[384,768]{1,0:T(8,128)(2,1)S(1)}, u32[]{:S(2)}, u32[]{:S(2)}) %collective-permute-start.40) | collective-permute-done | bytes 589856 | tf_op jit(solution)/shard_map/ppermute | solution.py:40
  438.8 22.2 %attention_back.1 = (bf16[768,1024]{1,0:T(8,128)(2,1)}, f32[1,1024]{1,0:T(1,128)}, bf16[2,768,1536]{2,1,0:T(8,128)(2,1)}) custom-call(s32[13]{0:T(128)} %copy-done.27, bf16[768,1536]{1,0:T(8,128)(2,1)} %get-tuple-element.138.refs_1_, bf16[768,768]{1,0:T(8,128)(2,1)} %get-tuple-element.99.refs_1_.refs_2_, ...), custom_call_target="tpu_custom_call" | custom-call | flops 87577067520 | bytes 209715200 | tf_op jit(solution)/shard_map/attention_back/pallas_call | solution.py:82
  461.1 5.8 all-to-all-start.5
  470.0 6.1 weight_grad.9
  483.2 8.5 %input_back.1 = (bf16[768,768]{1,0:T(8,128)(2,1)}, f32[1,1536]{1,0:T(1,128)}) custom-call(s32[13]{0:T(128)} %copy-done.27, bf16[2,768,1536]{2,1,0:T(8,128)(2,1)} %all-to-all-done.5.refs_1_, bf16[768,768]{1,0:T(8,128)(2,1)} %copy-done.30, bf16[768,768]{1,0:T(8,128)(2,1)} %copy-done.31, f32[768,1]{1,0:T(8,128)} %get-tuple-element.102.refs_1_.refs_4_, ...), custom_call_target="tpu_custom_call" | custom-call | flops 176947200 | bytes 167772160 | tf_op jit(solution)/shard_map/input_back/pallas_call | solution.py:82
  503.6 9.6 %collective-permute-done.48 = bf16[2,4,96,1024]{3,2,1,0:T(8,128)(2,1)S(1)} collective-permute-done((bf16[2,4,96,1024]{3,2,1,0:T(8,128)(2,1)}, bf16[2,4,96,1024]{3,2,1,0:T(8,128)(2,1)S(1)}, u32[]{:S(2)}, u32[]{:S(2)}) %collective-permute-start.48) | collective-permute-done | bytes 1572896 | tf_op jit(solution)/shard_map/ppermute | solution.py:40
  521.7 5.8 sum_output.1.refs_2_
  531.6 6.2 %collective-permute-done.54 = bf16[2,2,96,768]{3,2,1,0:T(8,128)(2,1)S(1)} collective-permute-done((bf16[2,2,96,768]{3,2,1,0:T(8,128)(2,1)}, bf16[2,2,96,768]{3,2,1,0:T(8,128)(2,1)S(1)}, u32[]{:S(2)}, u32[]{:S(2)}) %collective-permute-start.54) | collective-permute-done | bytes 589856 | tf_op jit(solution)/shard_map/ppermute | solution.py:40
  547.5 13.4 %collective-permute-done.52 = bf16[2,2,96,1024]{3,2,1,0:T(8,128)(2,1)S(1)} collective-permute-done((bf16[2,2,96,1024]{3,2,1,0:T(8,128)(2,1)}, bf16[2,2,96,1024]{3,2,1,0:T(8,128)(2,1)S(1)}, u32[]{:S(2)}, u32[]{:S(2)}) %collective-permute-start.52) | collective-permute-done | bytes 786464 | tf_op jit(solution)/shard_map/ppermute | solution.py:40
  566.0 12.2 %collective-permute-done.62.refs_2_ = bf16[2,96,1152]{2,1,0:T(8,128)(2,1)S(1)} collective-permute-done((bf16[2,96,1152]{2,1,0:T(8,128)(2,1)}, bf16[2,96,1152]{2,1,0:T(8,128)(2,1)S(1)}, u32[]{:S(2)}, u32[]{:S(2)}) %collective-permute-start.62) | collective-permute-done | bytes 442400 | tf_op jit(solution)/shard_map/ppermute | solution.py:40
  (381 shorter events, 228.0 us)
Async XLA Ops:
  9.7 49.4 %collective-permute-start.1 = (bf16[768,768]{1,0:T(8,128)(2,1)S(1)}, bf16[768,768]{1,0:T(8,128)(2,1)S(1)}, u32[]{:S(2)}, u32[]{:S(2)}) collective-permute-start(bf16[768,768]{1,0:T(8,128)(2,1)S(1)} %collective-permute-done.refs_1_.refs_2_), channel_id=1, source_target_pairs={{0,1},{1,0},{2,3},{3,2},{4,5},{5,4},{6,7},{7,6},{8,9},{9,8},{10,11... | collective-permute-start | bytes 3538952 | tf_op jit(solution)/shard_map/ppermute | solution.py:35
  53.3 32.3 %collective-permute-start.17 = (bf16[192,2304]{1,0:T(8,128)(2,1)S(1)}, bf16[192,2304]{1,0:T(8,128)(2,1)S(1)}, u32[]{:S(2)}, u32[]{:S(2)}) collective-permute-start(bf16[192,2304]{1,0:T(8,128)(2,1)S(1)} %pack.8.refs_1_), channel_id=1, source_target_pairs={{0,2},{2,0},{1,3},{3,1},{4,6},{6,4},{5,7},{7,5},{8,10},{10,8},{9,1... | collective-permute-start | bytes 2654216 | tf_op jit(solution)/shard_map/ppermute | solution.py:31
  58.6 36.9 %collective-permute-start.16 = (bf16[192,2304]{1,0:T(8,128)(2,1)}, bf16[192,2304]{1,0:T(8,128)(2,1)}, u32[]{:S(2)}, u32[]{:S(2)}) collective-permute-start(bf16[192,2304]{1,0:T(8,128)(2,1)} %hold.30.refs_16_.refs_5_.refs_7_.refs_4_), channel_id=1, source_target_pairs={{0,4},{4,0},{8,12},{12,8},{16,20},{20,16},{24,28},{28,24},{1,5},{5... | collective-permute-start | bytes 2654216 | tf_op jit(solution)/shard_map/ppermute | solution.py:40
  71.3 40.7 %collective-permute-start.20 = (bf16[768,768]{1,0:T(8,128)(2,1)}, bf16[768,768]{1,0:T(8,128)(2,1)}, u32[]{:S(2)}, u32[]{:S(2)}) collective-permute-start(bf16[768,768]{1,0:T(8,128)(2,1)} %copy_of.1.refs_12_.refs_1_), channel_id=1, source_target_pairs={{0,2},{2,0},{1,3},{3,1},{4,6},{6,4},{5,7},{7,5},{8,10},{10,8},{9,1... | collective-permute-start | bytes 3538952 | tf_op jit(solution)/shard_map/ppermute | solution.py:31
  142.0 55.5 %collective-permute-start.30 = (bf16[768,768]{1,0:T(8,128)(2,1)}, bf16[768,768]{1,0:T(8,128)(2,1)S(1)}, u32[]{:S(2)}, u32[]{:S(2)}) collective-permute-start(bf16[768,768]{1,0:T(8,128)(2,1)} %hold.35.refs_9_.refs_3_), channel_id=1, source_target_pairs={{0,1},{1,0},{2,3},{3,2},{4,5},{5,4},{6,7},{7,6},{8,9},{9,8},{10,11... | collective-permute-start | bytes 3538952 | tf_op jit(solution)/shard_map/ppermute | solution.py:35
  142.3 55.3 %collective-permute-start.29 = (bf16[768,768]{1,0:T(8,128)(2,1)S(1)}, bf16[768,768]{1,0:T(8,128)(2,1)S(1)}, u32[]{:S(2)}, u32[]{:S(2)}) collective-permute-start(bf16[768,768]{1,0:T(8,128)(2,1)S(1)} %copy-done.3), channel_id=1, source_target_pairs={{0,1},{1,0},{2,3},{3,2},{4,5},{5,4},{6,7},{7,6},{8,9},{9,8},{10,11... | collective-permute-start | bytes 3538952 | tf_op jit(solution)/shard_map/ppermute | solution.py:35
  145.6 52.0 %collective-permute-start.28 = (bf16[384,768]{1,0:T(8,128)(2,1)S(1)}, bf16[384,768]{1,0:T(8,128)(2,1)S(1)}, u32[]{:S(2)}, u32[]{:S(2)}) collective-permute-start(bf16[384,768]{1,0:T(8,128)(2,1)S(1)} %slice.137), channel_id=1, source_target_pairs={{0,8},{4,12},{8,0},{12,4},{16,24},{20,28},{24,16},{28,20},{1,9},{5... | collective-permute-start | bytes 1769480 | tf_op jit(solution)/shard_map/ppermute | solution.py:40
  146.1 30.6 %collective-permute-start.25 = (bf16[384,768]{1,0:T(8,128)(2,1)}, bf16[384,768]{1,0:T(8,128)(2,1)S(1)}, u32[]{:S(2)}, u32[]{:S(2)}) collective-permute-start(bf16[384,768]{1,0:T(8,128)(2,1)} %slice.136), channel_id=1, source_target_pairs={{0,2},{2,0},{1,3},{3,1},{4,6},{6,4},{5,7},{7,5},{8,10},{10,8},{9,1... | collective-permute-start | bytes 1769480 | tf_op jit(solution)/shard_map/ppermute | solution.py:31
  156.7 40.9 %collective-permute-start.27 = (bf16[384,768]{1,0:T(8,128)(2,1)S(1)}, bf16[384,768]{1,0:T(8,128)(2,1)S(1)}, u32[]{:S(2)}, u32[]{:S(2)}) collective-permute-start(bf16[384,768]{1,0:T(8,128)(2,1)S(1)} %hold.40.refs_2_), channel_id=1, source_target_pairs={{0,2},{2,0},{1,3},{3,1},{4,6},{6,4},{5,7},{7,5},{8,10},{10,8},{9,1... | collective-permute-start | bytes 1769480 | tf_op jit(solution)/shard_map/ppermute | solution.py:31
  233.3 97.8 %collective-permute-start.32 = (bf16[2,4,96,1152]{3,2,1,0:T(8,128)(2,1)}, bf16[2,4,96,1152]{3,2,1,0:T(8,128)(2,1)}, u32[]{:S(2)}, u32[]{:S(2)}) collective-permute-start(bf16[2,4,96,1152]{3,2,1,0:T(8,128)(2,1)} %get-tuple-element.118.refs_7_), channel_id=1, source_target_pairs={{0,4},{4,0},{8,12},{12,8},{16,20},{20,16},{24,28},{28,24},{1,5},{5... | collective-permute-start | bytes 5308424 | tf_op jit(solution)/shard_map/ppermute | solution.py:40
  277.0 46.1 %collective-permute-start.34 = (bf16[384,768]{1,0:T(8,128)(2,1)}, bf16[384,768]{1,0:T(8,128)(2,1)}, u32[]{:S(2)}, u32[]{:S(2)}) collective-permute-start(bf16[384,768]{1,0:T(8,128)(2,1)} %get-tuple-element.189.refs_8_), channel_id=1, source_target_pairs={{0,2},{2,0},{1,3},{3,1},{4,6},{6,4},{5,7},{7,5},{8,10},{10,8},{9,1... | collective-permute-start | bytes 1769480 | tf_op jit(solution)/shard_map/ppermute | solution.py:31
  277.8 45.3 %collective-permute-start.35 = (bf16[384,768]{1,0:T(8,128)(2,1)}, bf16[384,768]{1,0:T(8,128)(2,1)}, u32[]{:S(2)}, u32[]{:S(2)}) collective-permute-start(bf16[384,768]{1,0:T(8,128)(2,1)} %get-tuple-element.188.refs_9_), channel_id=1, source_target_pairs={{0,8},{4,12},{8,0},{12,4},{16,24},{20,28},{24,16},{28,20},{1,9},{5... | collective-permute-start | bytes 1769480 | tf_op jit(solution)/shard_map/ppermute | solution.py:40
  322.5 78.2 %collective-permute-start.41 = (bf16[2,4,96,1152]{3,2,1,0:T(8,128)(2,1)}, bf16[2,4,96,1152]{3,2,1,0:T(8,128)(2,1)}, u32[]{:S(2)}, u32[]{:S(2)}) collective-permute-start(bf16[2,4,96,1152]{3,2,1,0:T(8,128)(2,1)} %get-tuple-element.123.refs_4_), channel_id=1, source_target_pairs={{0,4},{4,0},{8,12},{12,8},{16,20},{20,16},{24,28},{28,24},{1,5},{5... | collective-permute-start | bytes 5308424 | tf_op jit(solution)/shard_map/ppermute | solution.py:40
  329.4 45.5 %collective-permute-start.37 = (bf16[768,768]{1,0:T(8,128)(2,1)}, bf16[768,768]{1,0:T(8,128)(2,1)}, u32[]{:S(2)}, u32[]{:S(2)}) collective-permute-start(bf16[768,768]{1,0:T(8,128)(2,1)} %get-tuple-element.128), channel_id=1, source_target_pairs={{0,2},{2,0},{1,3},{3,1},{4,6},{6,4},{5,7},{7,5},{8,10},{10,8},{9,1... | collective-permute-start | bytes 3538952 | tf_op jit(solution)/shard_map/ppermute | solution.py:31
  330.6 45.7 %collective-permute-start.38 = (bf16[768,768]{1,0:T(8,128)(2,1)}, bf16[768,768]{1,0:T(8,128)(2,1)}, u32[]{:S(2)}, u32[]{:S(2)}) collective-permute-start(bf16[768,768]{1,0:T(8,128)(2,1)} %get-tuple-element.124.refs_3_), channel_id=1, source_target_pairs={{0,8},{4,12},{8,0},{12,4},{16,24},{20,28},{24,16},{28,20},{1,9},{5... | collective-permute-start | bytes 3538952 | tf_op jit(solution)/shard_map/ppermute | solution.py:40
  353.4 32.5 %collective-permute-start.36 = (bf16[3072,768]{1,0:T(8,128)(2,1)}, bf16[3072,768]{1,0:T(8,128)(2,1)}, u32[]{:S(2)}, u32[]{:S(2)}) collective-permute-start(bf16[3072,768]{1,0:T(8,128)(2,1)} %get-tuple-element.127.refs_3_), channel_id=1, source_target_pairs={{0,1},{1,0},{2,3},{3,2},{4,5},{5,4},{6,7},{7,6},{8,9},{9,8},{10,11... | collective-permute-start | bytes 14155784 | tf_op jit(solution)/shard_map/ppermute | solution.py:35
  372.4 61.7 %collective-permute-start.43 = (bf16[2,1,192,1152]{3,2,1,0:T(8,128)(2,1)}, bf16[2,1,192,1152]{3,2,1,0:T(8,128)(2,1)}, u32[]{:S(2)}, u32[]{:S(2)}) collective-permute-start(bf16[2,1,192,1152]{3,2,1,0:T(8,128)(2,1)} %get-tuple-element.125.refs_5_), channel_id=1, source_target_pairs={{0,16},{4,20},{8,24},{12,28},{16,0},{20,4},{24,8},{28,12},{1,17},{... | collective-permute-start | bytes 2654216 | tf_op jit(solution)/shard_map/ppermute | solution.py:40
  375.0 48.3 %collective-permute-start.44 = (bf16[2,4,96,1152]{3,2,1,0:T(8,128)(2,1)}, bf16[2,4,96,1152]{3,2,1,0:T(8,128)(2,1)S(1)}, u32[]{:S(2)}, u32[]{:S(2)}) collective-permute-start(bf16[2,4,96,1152]{3,2,1,0:T(8,128)(2,1)} %get-tuple-element.129.refs_4_), channel_id=1, source_target_pairs={{0,4},{4,0},{8,12},{12,8},{16,20},{20,16},{24,28},{28,24},{1,5},{5... | collective-permute-start | bytes 5308424 | tf_op jit(solution)/shard_map/ppermute | solution.py:40
  404.1 89.9 %collective-permute-start.50 = (bf16[2,1,192,1152]{3,2,1,0:T(8,128)(2,1)}, bf16[2,1,192,1152]{3,2,1,0:T(8,128)(2,1)}, u32[]{:S(2)}, u32[]{:S(2)}) collective-permute-start(bf16[2,1,192,1152]{3,2,1,0:T(8,128)(2,1)} %get-tuple-element.135.refs_4_), channel_id=1, source_target_pairs={{0,16},{4,20},{8,24},{12,28},{16,0},{20,4},{24,8},{28,12},{1,17},{... | collective-permute-start | bytes 2654216 | tf_op jit(solution)/shard_map/ppermute | solution.py:40
  423.2 55.6 %collective-permute-start.46 = (bf16[768,768]{1,0:T(8,128)(2,1)}, bf16[768,768]{1,0:T(8,128)(2,1)}, u32[]{:S(2)}, u32[]{:S(2)}) collective-permute-start(bf16[768,768]{1,0:T(8,128)(2,1)} %get-tuple-element.142.refs_1_), channel_id=1, source_target_pairs={{0,8},{4,12},{8,0},{12,4},{16,24},{20,28},{24,16},{28,20},{1,9},{5... | collective-permute-start | bytes 3538952 | tf_op jit(solution)/shard_map/ppermute | solution.py:40
  431.0 67.1 %collective-permute-start.49 = (bf16[2,4,96,768]{3,2,1,0:T(8,128)(2,1)}, bf16[2,4,96,768]{3,2,1,0:T(8,128)(2,1)}, u32[]{:S(2)}, u32[]{:S(2)}) collective-permute-start(bf16[2,4,96,768]{3,2,1,0:T(8,128)(2,1)} %get-tuple-element.143.refs_2_), channel_id=1, source_target_pairs={{0,4},{4,0},{8,12},{12,8},{16,20},{20,16},{24,28},{28,24},{1,5},{5... | collective-permute-start | bytes 3538952 | tf_op jit(solution)/shard_map/ppermute | solution.py:40
  436.7 30.1 %collective-permute-start.45 = (bf16[2,96,1152]{2,1,0:T(8,128)(2,1)}, bf16[2,96,1152]{2,1,0:T(8,128)(2,1)S(1)}, u32[]{:S(2)}, u32[]{:S(2)}) collective-permute-start(bf16[2,96,1152]{2,1,0:T(8,128)(2,1)} %get-tuple-element.144.refs_24_), channel_id=1, source_target_pairs={{0,2},{2,0},{1,3},{3,1},{4,6},{6,4},{5,7},{7,5},{8,10},{10,8},{9,1... | collective-permute-start | bytes 1327112 | tf_op jit(solution)/shard_map/ppermute | solution.py:31
  438.0 39.4 %collective-permute-start.42 = (bf16[768,768]{1,0:T(8,128)(2,1)}, bf16[768,768]{1,0:T(8,128)(2,1)S(1)}, u32[]{:S(2)}, u32[]{:S(2)}) collective-permute-start(bf16[768,768]{1,0:T(8,128)(2,1)} %get-tuple-element.136), channel_id=1, source_target_pairs={{0,2},{2,0},{1,3},{3,1},{4,6},{6,4},{5,7},{7,5},{8,10},{10,8},{9,1... | collective-permute-start | bytes 3538952 | tf_op jit(solution)/shard_map/ppermute | solution.py:31
  476.0 37.2 %collective-permute-start.48 = (bf16[2,4,96,1024]{3,2,1,0:T(8,128)(2,1)}, bf16[2,4,96,1024]{3,2,1,0:T(8,128)(2,1)S(1)}, u32[]{:S(2)}, u32[]{:S(2)}) collective-permute-start(bf16[2,4,96,1024]{3,2,1,0:T(8,128)(2,1)} %get-tuple-element.147.refs_1_), channel_id=1, source_target_pairs={{0,4},{4,0},{8,12},{12,8},{16,20},{20,16},{24,28},{28,24},{1,5},{5... | collective-permute-start | bytes 4718600 | tf_op jit(solution)/shard_map/ppermute | solution.py:40
  483.2 44.2 %collective-permute-start.55 = (bf16[2,1,192,1152]{3,2,1,0:T(8,128)(2,1)}, bf16[2,1,192,1152]{3,2,1,0:T(8,128)(2,1)}, u32[]{:S(2)}, u32[]{:S(2)}) collective-permute-start(bf16[2,1,192,1152]{3,2,1,0:T(8,128)(2,1)} %get-tuple-element.150.refs_8_), channel_id=1, source_target_pairs={{0,16},{4,20},{8,24},{12,28},{16,0},{20,4},{24,8},{28,12},{1,17},{... | collective-permute-start | bytes 2654216 | tf_op jit(solution)/shard_map/ppermute | solution.py:40
  493.2 71.1 %collective-permute-start.57 = (f32[4096]{0:T(1024)S(1)}, f32[4096]{0:T(1024)S(1)}, u32[]{:S(2)}, u32[]{:S(2)}) collective-permute-start(f32[4096]{0:T(1024)S(1)} %pad_maximum_fusion.4), channel_id=1, source_target_pairs={{0,4},{4,0},{8,12},{12,8},{16,20},{20,16},{24,28},{28,24},{1,5},{5... | collective-permute-start | bytes 49160 | tf_op jit(solution)/shard_map/ppermute | solution.py:40
  498.1 42.6 %collective-permute-start.53 = (bf16[2,96,1152]{2,1,0:T(8,128)(2,1)}, bf16[2,96,1152]{2,1,0:T(8,128)(2,1)S(1)}, u32[]{:S(2)}, u32[]{:S(2)}) collective-permute-start(bf16[2,96,1152]{2,1,0:T(8,128)(2,1)} %get-tuple-element.156.refs_3_), channel_id=1, source_target_pairs={{0,2},{2,0},{1,3},{3,1},{4,6},{6,4},{5,7},{7,5},{8,10},{10,8},{9,1... | collective-permute-start | bytes 1327112 | tf_op jit(solution)/shard_map/ppermute | solution.py:31
  518.5 42.4 %collective-permute-start.52 = (bf16[2,2,96,1024]{3,2,1,0:T(8,128)(2,1)}, bf16[2,2,96,1024]{3,2,1,0:T(8,128)(2,1)S(1)}, u32[]{:S(2)}, u32[]{:S(2)}) collective-permute-start(bf16[2,2,96,1024]{3,2,1,0:T(8,128)(2,1)} %get-tuple-element.158.refs_1_), channel_id=1, source_target_pairs={{0,8},{4,12},{8,0},{12,4},{16,24},{20,28},{24,16},{28,20},{1,9},{5... | collective-permute-start | bytes 2359304 | tf_op jit(solution)/shard_map/ppermute | solution.py:40
  527.4 36.8 %collective-permute-start.51 = (bf16[768,768]{1,0:T(8,128)(2,1)}, bf16[768,768]{1,0:T(8,128)(2,1)S(1)}, u32[]{:S(2)}, u32[]{:S(2)}) collective-permute-start(bf16[768,768]{1,0:T(8,128)(2,1)} %sum_output.1.refs_2_), channel_id=1, source_target_pairs={{0,0},{1,2},{2,1},{3,3},{4,4},{5,6},{6,5},{7,7},{8,8},{9,10},{10,9... | collective-permute-start | bytes 3538952 | tf_op jit(solution)/shard_map/ppermute | solution.py:48
  540.7 40.7 %collective-permute-start.61 = (bf16[2,1,96,768]{3,2,1,0:T(8,128)(2,1)}, bf16[2,1,96,768]{3,2,1,0:T(8,128)(2,1)S(1)}, u32[]{:S(2)}, u32[]{:S(2)}) collective-permute-start(bf16[2,1,96,768]{3,2,1,0:T(8,128)(2,1)} %get-tuple-element.165.refs_3_), channel_id=1, source_target_pairs={{0,16},{4,20},{8,24},{12,28},{16,0},{20,4},{24,8},{28,12},{1,17},{... | collective-permute-start | bytes 884744 | tf_op jit(solution)/shard_map/ppermute | solution.py:40
  543.6 34.6 %collective-permute-start.62 = (bf16[2,96,1152]{2,1,0:T(8,128)(2,1)}, bf16[2,96,1152]{2,1,0:T(8,128)(2,1)S(1)}, u32[]{:S(2)}, u32[]{:S(2)}) collective-permute-start(bf16[2,96,1152]{2,1,0:T(8,128)(2,1)} %get-tuple-element.166.refs_3_), channel_id=1, source_target_pairs={{0,8},{4,12},{8,0},{12,4},{16,24},{20,28},{24,16},{28,20},{1,9},{5... | collective-permute-start | bytes 1327112 | tf_op jit(solution)/shard_map/ppermute | solution.py:40
  564.3 34.4 %collective-permute-start.56 = (bf16[2,1,96,1024]{3,2,1,0:T(8,128)(2,1)}, bf16[2,1,96,1024]{3,2,1,0:T(8,128)(2,1)S(1)}, u32[]{:S(2)}, u32[]{:S(2)}) collective-permute-start(bf16[2,1,96,1024]{3,2,1,0:T(8,128)(2,1)} %get-tuple-element.168.refs_1_), channel_id=1, source_target_pairs={{0,16},{4,20},{8,24},{12,28},{16,0},{20,4},{24,8},{28,12},{1,17},{... | collective-permute-start | bytes 1179656 | tf_op jit(solution)/shard_map/ppermute | solution.py:40
  (111 other events, 1029.3 us)

commit v4 on v3

--- a/solution.py
+++ b/solution.py
@@ -390,27 +390,37 @@
 
 
 def place_rows(scalars, pieces, after=()):
-    length, width = pieces[0][0][0].shape
-    flat = [array for group in pieces for pair in group for array in pair]
+    length, width = pieces[0][0].shape
+    flat = [array for piece in pieces for array in piece[:2]]
 
     def kernel(s, *refs):
         srcs, out, sems = refs[:len(flat)], refs[len(flat)], refs[len(flat) + 1]
         pairs = []
         for i, src in enumerate(srcs):
-            group, side, token = i // 4, (i // 2) % 2, i % 2
-            place = jnp.where(s[SAME] == 1, token, 1 - token) * length
-            if i == len(srcs) - 1:
-                place = (1 - s[ROW]) * length
-            elif i == len(srcs) - 2:
-                place = s[ROW] * length
+            _, _, group, side = pieces[i // 2]
+            place = jnp.where(s[SAME] == 1, i % 2, 1 - i % 2) * length
             pairs.append((src, out.at[rows_at(2 * group * length + place, length),
                                       side * width:(side + 1) * width]))
         copies(pairs, sems)
 
     return run(kernel, [(scalars, SCALARS)] + [(a, ANY) for a in flat],
-               [shape((2 * len(pieces) * length, 2 * width), BF)], after=after,
+               [shape((4 * length, 2 * width), BF)], after=after,
                scratch=[pltpu.SemaphoreType.DMA((len(flat),))], limit=48,
                estimate=cost(0, 16 * len(flat) * length * width // 4), name="place_rows")[0]
+
+
+def place_last(scalars, both, rows, after=()):
+    _, length, width = both.shape
+
+    def kernel(s, both, _, out, buffer, sems):
+        copies([(both.at[i], buffer.at[i]) for i in range(2)], sems)
+        copies([(buffer.at[i], out.at[rows_at(2 * length + jnp.where(s[ROW] == i, 0, length), length),
+                                      width:]) for i in range(2)], sems)
+
+    return run(kernel, [(scalars, SCALARS), (both, ANY), (rows, ANY)], [shape(rows.shape, BF)], after=after,
+               out_specs=[ANY], aliases={2: 0},
+               scratch=[pltpu.VMEM(both.shape, BF), pltpu.SemaphoreType.DMA((2,))], limit=48,
+               estimate=cost(0, 8 * length * width), name="place_last")[0]
 
 
 def copy_of(array, after):
@@ -593,11 +603,12 @@
         scaled = db[...] * gains
         mean = jnp.sum(scaled * normed, axis=1, keepdims=True) / D
         value = g[...].astype(F32) + rstd * (scaled - normed * mean)
-        dh[...] = value
         low[...] = value.astype(BF)
+        pl.when(s[SAME] == 1)(lambda: dh.__setitem__(..., value[:, :width]))
+        pl.when(s[SAME] == 0)(lambda: dh.__setitem__(..., value[:, width:]))
 
     tile = TILE // 2
-    outs = [shape((length, 2 * width), F32), shape((length, 2 * width), BF), shape((1, 2 * width), F32)]
+    outs = [shape((length, width), F32), shape((length, 2 * width), BF), shape((1, 2 * width), F32)]
     return run(kernel, [(scalars, SCALARS)] + [both_tiled(both, tile), tiled(h, tile), tiled(r, tile)]
                + [fixed(gain), fixed(gain_far), tiled(cot, tile)], outs, after=after,
                grid=(length // tile,),
@@ -688,15 +699,12 @@
         gain_part[...] += jnp.sum(da * normed, axis=0, keepdims=True)
         scaled = da * jnp.concatenate([gain[...], gain_far[...]], axis=1)
         mean = jnp.sum(scaled * normed, axis=1, keepdims=True) / D
-        value = (dh[...] + r[...] * (scaled - normed * mean)).astype(BF)
-
-        @pl.when(s[SAME] == 1)
-        def _():
-            out[...] = value[:, :width]
-
-        @pl.when(s[SAME] == 0)
-        def _():
-            out[...] = value[:, width:]
+
+        def put(half):
+            out[...] = (dh[...] + r[...] * (scaled[:, half] - normed[:, half] * mean)).astype(BF)
+
+        pl.when(s[SAME] == 1)(lambda: put(slice(0, width)))
+        pl.when(s[SAME] == 0)(lambda: put(slice(width, 2 * width)))
 
     tile = TILE // 2
     outs = [shape((length, width), BF), shape((1, 2 * width), F32)]
@@ -964,20 +972,23 @@
     cot_other = swap_col(cot)
     gu_fetched[1] = hold(gu_fetched[1])
     cot_other = hold(cot_other)
-    cot_near = hold(cot_near)
     h, low_near, low_far, r_two = norm_two(
         scalars, mine, other, trade_col(out_part), gains[1:], fetched_gains[1:]
     )
 
     b_row = swap_row(low_near)
     b_near = swap_bit(low_near, 1)
-    cot_row = hold(cot_row)
-    cot_low = swap_bit(cot_row[:half], 1)
+    cot_row, cot_near = hold(cot_row), hold(cot_near)
+    cot_row_other, cot_near_other = swap_col(cot_row), swap_col(cot_near)
     tokens = 4 * length
     ffn = functools.partial(
         gate_up, scalars, w_gate=w_gate, w_up=w_up, fetched=gu_fetched, total=tokens, part=part,
     )
     kept = ffn([(low_near, low_far)], first=0)
+    cot_row_other, cot_near_other = hold(cot_row_other), hold(cot_near_other)
+    cot_low = swap_bit(hold(cot_row[:half]), 1)
+    placed_cot = place_rows(scalars, [(cot, cot_other, 0, 0), (cot_row, cot_row_other, 0, 1),
+                                      (cot_near, cot_near_other, 1, 0)])
     b_row = hold(b_row)
     b_row_other = swap_col(b_row)
     b_low = swap_bit(b_row[:half], 1)
@@ -991,18 +1002,13 @@
     kept = ffn([(b_row, b_row_other), (b_near, b_near_other)], first=length, kept=kept)
     b_far = jnp.concatenate([hold(b_low), hold(b_high)], axis=0)
     b_far = trade_col(jnp.stack([b_far, b_far]))
-    cot_row_other, cot_near_other = swap_col(cot_row), swap_col(cot_near)
     kept = ffn([(b_far,)], first=3 * length, kept=kept, after=[sent_down], share=0)
     full_two, hidden, up_slope, gate_slope = kept
-    cot_row_other, cot_near_other = hold(cot_row_other), hold(cot_near_other)
     cot_far = jnp.concatenate([hold(cot_low), hold(cot_high)], axis=0)
     cot_far = trade_col(jnp.stack([cot_far, cot_far]))
     down_direct = hold(down_direct)
     down_fetched = down_direct, swap_bit(down_direct, 0)
-    full_cot = place_rows(
-        scalars, [[(cot, cot_other), (cot_row, cot_row_other)],
-                  [(cot_near, cot_near_other), (cot_far[0], cot_far[1])]],
-    )
+    full_cot = place_last(scalars, cot_far, placed_cot)
 
     piece = width // groups
     down_keep, down_send = weight_grad(scalars, full_cot, hidden, piece, part)
@@ -1011,9 +1017,46 @@
     back = functools.partial(
         norm_back, scalars, low_back, w_gate, w_up, gu_fetched
     )
+    high_bits = range(2, groups.bit_length() - 1)
+
+    def grad_high(keep, recv):
+        for bit in high_bits:
+            cut = (2, keep.size // (4 * 2 * piece * part), 2, 2 * piece, part)
+            keep, send = halve(scalars, keep.reshape(cut), recv.reshape(cut), bit)
+            recv = swap_bit(send, bit)
+        return keep, recv
+
+    def grad_row(keep, recv):
+        cut = (2, 2, piece, part)
+        near, send = sum_rows(keep.reshape(cut), recv.reshape(cut))
+        return near, swap_row(send)
+
+    def grad_near(near, far):
+        own, send = deal_near(scalars, near, far)
+        return own, swap_bit(send, 1)
+
+    def square_first(left, right):
+        keep, send = weight_grad(scalars, left, right, piece, right.shape[1])
+        return keep, swap_bit(send, 0)
+
+    def square_next(keep, recv, bit):
+        cut = (2, groups >> (bit + 1), 2, piece, keep.shape[-1])
+        keep, send = halve(scalars, keep.reshape(cut), recv.reshape(cut), bit)
+        return keep, swap_bit(send, bit)
+
+    def square_row(keep, recv):
+        near, send = sum_rows(keep, recv)
+        return near, swap_row(send)
+
+    def square_last(near, far):
+        return sum_plain(near, far).reshape(piece, -1)
+
+    last_bits = range(2, groups.bit_length() - 1)
+
     far_both = trade_col(back(3 * length, length, stacked=True)[0])
     across = (far_both[0].astype(F32) + far_both[1].astype(F32)).astype(BF)
     to_row, to_near = across[:half], across[half:]
+    down = grad_high(down_keep, down_recv)
     rest_keep, rest_send = back(0, 3 * length, after=[to_row, to_near])
     via_row, via_near = swap_row(to_row), swap_bit(to_near, 1)
     gate_keep, gate_send = weight_grad(scalars, full_two, low_back, piece, part, 0)
@@ -1022,43 +1065,7 @@
     to_row, to_near = sum_near(rest_keep, rest_got, via_row, via_near, length)
     via_row, via_near = swap_row(to_row), swap_bit(to_near, 1)
 
-    high_bits = range(2, groups.bit_length() - 1)
-
-    def grad_high(keep, recv):
-        for bit in high_bits:
-            cut = (2, keep.size // (4 * 2 * piece * part), 2, 2 * piece, part)
-            keep, send = halve(scalars, keep.reshape(cut), recv.reshape(cut), bit)
-            recv = swap_bit(send, bit)
-        return keep, recv
-
-    def grad_row(keep, recv):
-        cut = (2, 2, piece, part)
-        near, send = sum_rows(keep.reshape(cut), recv.reshape(cut))
-        return near, swap_row(send)
-
-    def grad_near(near, far):
-        own, send = deal_near(scalars, near, far)
-        return own, swap_bit(send, 1)
-
-    def square_first(left, right):
-        keep, send = weight_grad(scalars, left, right, piece, right.shape[1])
-        return keep, swap_bit(send, 0)
-
-    def square_next(keep, recv, bit):
-        cut = (2, groups >> (bit + 1), 2, piece, keep.shape[-1])
-        keep, send = halve(scalars, keep.reshape(cut), recv.reshape(cut), bit)
-        return keep, swap_bit(send, bit)
-
-    def square_row(keep, recv):
-        near, send = sum_rows(keep, recv)
-        return near, swap_row(send)
-
-    def square_last(near, far):
-        return sum_plain(near, far).reshape(piece, -1)
-
-    last_bits = range(2, groups.bit_length() - 1)
-
-    down = grad_high(down_keep, down_recv)
+    down = down[0], hold(down[1])
     out_keep, out_send = down_project(scalars, hidden, w_down, down_fetched)
     out_got = swap_col(out_send)
     up_keep, up_send = weight_grad(scalars, full_two, low_back, piece, part, 1)
@@ -1067,23 +1074,24 @@
     first = 3 * length
     to_row, to_near = sum_far(out_keep, out_got, first)
     via_row, via_near = swap_row(to_row), swap_bit(to_near, 1)
+    down = grad_row(*down)
     dh, low_mid, gain_two_part = middle_back(
         scalars, trade_col(normed_grad), h, r_two, gains[1:], fetched_gains[1:], full_cot,
     )
     gate = grad_high(gate_keep, gate_recv)
+    down = down[0], hold(down[1])
+    out_sum = square_first(low_mid, attended)
     to_row, to_near = sum_near(out_keep, out_got, via_row, via_near, length)
     via_row, via_near = swap_row(to_row), swap_bit(to_near, 1)
     up_recv = hold(up_recv)
-    out_sum = square_first(low_mid, attended)
-    down = grad_row(*down)
     back_low, bias_part, in_part = attend_back(
         scalars, low_mid, q, k, v, lse, seg_col, seg_row, w_out, out_fetched, w_query, w_key,
         w_value, qkv_fetched, cosine, sine,
     )
-    down = down[0], hold(down[1])
     qkv_sum = square_first(low_one, back_low)
-    via_row, via_near = hold(via_row), hold(via_near)
+    via_row = hold(via_row)
     up = grad_high(up_keep, up_recv)
+    via_near = hold(via_near)
     input_grad, gain_one_part = input_back(
         scalars, trade_col(in_part), mine, other, r_one, gains[:1], fetched_gains[:1], dh
     )
@@ -1099,30 +1107,31 @@
         return value + hold(swap(value))
 
     gate = grad_row(*gate)
+    qkv_sum = square_next(*qkv_sum, 1)
+    small = small_step(small, lambda value: swap_bit(value, 0))
     out_sum = square_next(*out_sum, 1)
-    qkv_sum = square_next(*qkv_sum, 1)
     input_grad = hold(input_grad).astype(F32)
     output = turn_square(sum_output(scalars, out_keep, out_got, via_row, via_near, h))
     up = grad_row(*up)
     for bit in last_bits:
-        out_sum = square_next(*out_sum, bit)
+        qkv_sum = square_next(*qkv_sum, bit)
     gate = grad_near(*gate)
     down = grad_near(*down)
+    output = hold(output)
+    small = small_step(small, lambda value: swap_bit(value, 1))
+    up = grad_near(*up)
     for bit in last_bits:
-        qkv_sum = square_next(*qkv_sum, bit)
-    output = hold(output)
-    small = small_step(small, lambda value: swap_bit(value, 0))
+        out_sum = square_next(*out_sum, bit)
+    qkv_sum = square_row(*qkv_sum)
     gate_grad = lay_columns(scalars, *gate, overlap)
+    for bit in last_bits:
+        small = small_step(small, lambda value, bit=bit: swap_bit(value, bit))
+    qkv_grads = sum_split(*qkv_sum, (query_width, key_width, key_width))
+    down_grad = lay_columns(scalars, *down, overlap).T
     out_sum = square_row(*out_sum)
-    up = grad_near(*up)
-    down_grad = lay_columns(scalars, *down, overlap).T
-    for bit in range(1, groups.bit_length() - 1):
-        small = small_step(small, lambda value, bit=bit: swap_bit(value, bit))
-    qkv_sum = square_row(*qkv_sum)
+    up_grad = lay_columns(scalars, *up, overlap)
+    small = small_step(small, swap_row)
     out_grad = square_last(*out_sum).T
-    small = small_step(small, swap_row)
-    up_grad = lay_columns(scalars, *up, overlap)
-    qkv_grads = sum_split(*qkv_sum, (query_width, key_width, key_width))
     gain_sums = pick(small[total_width:].reshape(2, 2, width), row, 1)
 
     return (

time: 621 us -> 587 us (0.945)
  waiting for transfers between devices: 91.8 us -> 47.7 us
  starting transfers between devices: 96.5 us -> 115 us
    ppermute x37, waiting for transfers between devices: 76.5 us -> 24 us  [swap_bit(): return lax.ppermute(value, 'dp', [(i, i ^ 1 << bit) for i in range(size)])]
    ppermute x20, starting transfers between devices: 22 us -> 31.8 us  [swap_row(): return lax.ppermute(value, 'row', [(0, 1), (1, 0)])]
    all_to_all x3 -> x2, blocking collectives: 19.6 us -> 13.5 us  [trade_col(): return lax.all_to_all(value, 'col', 0, 0)]
    all_to_all x3 -> x4, starting transfers between devices: 16.7 us -> 21 us  [trade_col(): return lax.all_to_all(value, 'col', 0, 0)]
    pallas_call x79 -> x82, Pallas kernels: 347 us -> 347 us  [run(): pl.pallas_call(body, grid=grid if grid is not None else (), in_specs=[spe...]
    unnamed x145 -> x153, local copies, waits for them, and re-layouts: 37.7 us -> 37.7 us
  transfers between devices with their start and end apart: 71 -> 72, of which waited for: 17 -> 16; matrix products, arithmetic and copies ran while one was open for 3% -> 3% of each run, Pallas kernels for 56% -> 60%
where the time goes in v4:
time: 587 us; the launch traced here: 580 us
  Pallas kernels  347 us (59%)
  starting transfers between devices  115 us (20%)
  waiting for transfers between devices  47.7 us (8%)
  local copies, waits for them, and re-layouts  46.4 us (8%)
  blocking collectives  13.5 us (2%)
  other arithmetic  8.48 us (1%)
    pallas_call x82, Pallas kernels, run(): pl.pallas_call(body, grid=grid if grid is not None else (), in_specs=[spe...  347 us
    ppermute x37, starting transfers between devices, swap_bit(): return lax.ppermute(value, 'dp', [(i, i ^ 1 << bit) for i in range(size)])  40.8 us
    unnamed x153, local copies, waits for them, and re-layouts  37.7 us
    ppermute x20, starting transfers between devices, swap_row(): return lax.ppermute(value, 'row', [(0, 1), (1, 0)])  31.8 us
    ppermute x37, waiting for transfers between devices, swap_bit(): return lax.ppermute(value, 'dp', [(i, i ^ 1 << bit) for i in range(size)])  24 us
    all_to_all x4, starting transfers between devices, trade_col(): return lax.all_to_all(value, 'col', 0, 0)  21 us
    ppermute x20, waiting for transfers between devices, swap_row(): return lax.ppermute(value, 'row', [(0, 1), (1, 0)])  17.5 us
    ppermute x8, starting transfers between devices, swap_col(): return lax.ppermute(value, 'col', [(0, 1), (1, 0)])  15.1 us
  transfers between devices with their start and end apart: 72, of which 16 were waited for; matrix products, arithmetic and copies ran while one was open for 3% of the time, Pallas kernels for 60%

profile of v4, /device:TPU:0, one launch (start us, length us, event | category | flops | bytes accessed | tf_op | source)
XLA Modules:
  0.0 579.9 jit_solution(12863749667915879753)
XLA Ops:
  9.7 14.4 %collective-permute-start.1 = (bf16[768,768]{1,0:T(8,128)(2,1)S(1)}, bf16[768,768]{1,0:T(8,128)(2,1)S(1)}, u32[]{:S(2)}, u32[]{:S(2)}) collective-permute-start(bf16[768,768]{1,0:T(8,128)(2,1)S(1)} %collective-permute-done.refs_1_.refs_2_), channel_id=1, source_target_pairs={{0,1},{1,0},{2,3},{3,2},{4,5},{5,4},{6,7},{7,6},{8,9},{9,8},{10,11... | collective-permute-start | bytes 3538952 | tf_op jit(solution)/shard_map/ppermute | solution.py:35
  60.2 8.2 %qkv.1 = (bf16[768,768]{1,0:T(8,128)(2,1)}, bf16[768,128]{1,0:T(8,128)(2,1)}, bf16[768,128]{1,0:T(8,128)(2,1)}, bf16[768,1536]{1,0:T(8,128)(2,1)}, f32[768,1]{1,0:T(8,128)}) custom-call(s32[13]{0:T(128)} %copy-done.30, bf16[768,768]{1,0:T(8,128)(2,1)} %copy-done.37, bf16[768,768]{1,0:T(8,128)(2,1)} %copy-done.38, ...), custom_call_target="tpu_custom_call" | custom-call | flops 24159191040 | bytes 125829120 | tf_op jit(solution)/shard_map/qkv/pallas_call | solution.py:82
  72.0 13.6 %attention.1 = (bf16[768,768]{1,0:T(8,128)(2,1)}, f32[768,128]{1,0:T(8,128)}, bf16[2,768,1536]{2,1,0:T(8,128)(2,1)}) custom-call(s32[13]{0:T(128)} %copy-done.30, bf16[768,768]{1,0:T(8,128)(2,1)} %get-tuple-element.99.refs_1_.refs_2_, bf16[768,128]{1,0:T(8,128)(2,1)} %get-tuple-element.100.refs_2_.refs_3_, ...), custom_call_target="tpu_custom_call" | custom-call | flops 36238786560 | bytes 125829120 | tf_op jit(solution)/shard_map/attention/pallas_call | solution.py:82
  89.5 6.0 %all-to-all-start = ((bf16[2,768,1536]{2,1,0:T(8,128)(2,1)}), bf16[2,768,1536]{2,1,0:T(8,128)(2,1)}, u32[]{:S(2)}, u32[]{:S(2)}) async-start(bf16[2,768,1536]{2,1,0:T(8,128)(2,1)} %get-tuple-element.103.refs_1_), calls=%async_computation | async-start | bytes 9437184 | tf_op jit(solution)/shard_map/all_to_all | solution.py:44
  100.4 8.7 %norm_two.1 = (f32[768,1536]{1,0:T(8,128)}, bf16[768,768]{1,0:T(8,128)(2,1)}, bf16[768,768]{1,0:T(8,128)(2,1)}, f32[768,1]{1,0:T(8,128)}) custom-call(s32[13]{0:T(128)} %copy-done.30, bf16[768,768]{1,0:T(8,128)(2,1)} %copy-done.37, bf16[768,768]{1,0:T(8,128)(2,1)} %copy-done.38, bf16[2,768,1536]{2,1,0:T(8,128)(2,1)} %all-to-all-done.refs_3_, ...), custom_call_target="tpu_custom_call" | custom-call | flops 117964800 | bytes 167772160 | tf_op jit(solution)/shard_map/norm_two/pallas_call | solution.py:82
  113.5 12.3 %gate_up.3 = (bf16[3072,1536]{1,0:T(8,128)(2,1)}, bf16[3072,1152]{1,0:T(8,128)(2,1)}, bf16[3072,1152]{1,0:T(8,128)(2,1)}, bf16[3072,1152]{1,0:T(8,128)(2,1)}) custom-call(s32[13]{0:T(128)} %copy-done.30, bf16[768,768]{1,0:T(8,128)(2,1)} %get-tuple-element.104.refs_1_, bf16[768,768]{1,0:T(8,128)(2,1)} %get-tuple-element.106.refs_2_, ...), custom_call_target="tpu_custom_call" | custom-call | flops 54358179840 | bytes 125829120 | tf_op jit(solution)/shard_map/gate_up/pallas_call | solution.py:82
  127.6 6.3 %place_rows.1.refs_1_.refs_2_ = bf16[3072,1536]{1,0:T(8,128)(2,1)} custom-call(s32[13]{0:T(128)S(1)} %copy-done.31, bf16[768,768]{1,0:T(8,128)(2,1)} %copy_of.1.refs_12_.refs_1_, bf16[768,768]{1,0:T(8,128)(2,1)S(1)} %copy-done.2, bf16[768,768]{1,0:T(8,128)(2,1)S(1)} %hold.36.refs_1_.refs_3_, bf16[768,768]{1,0:T(8,128)(2,1)S(1)} %hold.38.refs_1_.refs_4_, ...), custom_call_target="tpu_custom_call" | custom-call | bytes 141557760 | tf_op jit(solution)/shard_map/place_rows/pallas_call | solution.py:82
  149.5 19.0 %gate_up.4 = (bf16[3072,1536]{1,0:T(8,128)(2,1)}, bf16[3072,1152]{1,0:T(8,128)(2,1)}, bf16[3072,1152]{1,0:T(8,128)(2,1)}, bf16[3072,1152]{1,0:T(8,128)(2,1)}) custom-call(s32[13]{0:T(128)} %copy-done.30, bf16[768,768]{1,0:T(8,128)(2,1)} %copy-done.5, ...), custom_call_target="tpu_custom_call", output_to_operand_aliasing={{0}: (11, {}), {1}: (12, {}), {2}: (13, {}), {3}: (14, {})} | custom-call | flops 108716359680 | bytes 125829120 | tf_op jit(solution)/shard_map/gate_up/pallas_call | solution.py:82
  170.2 6.5 %all_to_all.30.refs_1_ = bf16[2,768,768]{2,1,0:T(8,128)(2,1)} all-to-all(bf16[2,768,768]{2,1,0:T(8,128)(2,1)S(1)} %pad_maximum_fusion), channel_id=1, replica_groups=mesh['dp'=8,'row'=2,'col'=2] {'col'}, dimensions={0} | all-to-all | bytes 4718592 | tf_op jit(solution)/shard_map/all_to_all | solution.py:44
  176.7 12.3 %gate_up.5 = (bf16[3072,1536]{1,0:T(8,128)(2,1)}, bf16[3072,1152]{1,0:T(8,128)(2,1)}, bf16[3072,1152]{1,0:T(8,128)(2,1)}, bf16[3072,1152]{1,0:T(8,128)(2,1)}) custom-call(s32[13]{0:T(128)} %copy-done.30, bf16[2,768,768]{2,1,0:T(8,128)(2,1)} %all_to_all.30.refs_1_, ...), custom_call_target="tpu_custom_call", output_to_operand_aliasing={{0}: (8, {}), {1}: (9, {}), {2}: (10, {}), {3}: (11, {})} | custom-call | tf_op jit(solution)/shard_map/gate_up/pallas_call | solution.py:82
  200.6 18.6 %weight_grad.5 = (bf16[2,4,96,1152]{3,2,1,0:T(8,128)(2,1)}, bf16[2,4,96,1152]{3,2,1,0:T(8,128)(2,1)}) custom-call(s32[13]{0:T(128)} %copy-done.30, bf16[3072,1536]{1,0:T(8,128)(2,1)} %place_last.1.refs_1_.refs_3_.refs_6_, bf16[3072,1152]{1,0:T(8,128)(2,1)} %get-tuple-element.115.refs_2_.refs_1_, bf16[3072,1536]{1,0:T(8,128)(2,1)} %place_last.1.refs_1_.refs_3_.refs_6_), custom_call_target="tpu_custom_call" | custom-call | flops 108716359680 | bytes 235929600 | tf_op jit(solution)/shard_map/weight_grad/pallas_call | solution.py:82
  220.7 21.3 %hidden_back.1.refs_1_.refs_8_.refs_2_ = bf16[3072,2304]{1,0:T(8,128)(2,1)} custom-call(s32[13]{0:T(128)} %copy-done.30, bf16[3072,1536]{1,0:T(8,128)(2,1)} %place_last.1.refs_1_.refs_3_.refs_6_, bf16[3072,1152]{1,0:T(8,128)(2,1)} %get-tuple-element.119.refs_2_, bf16[3072,1152]{1,0:T(8,128)(2,1)} %get-tuple-element.116.refs_1_.refs_3_, ...), custom_call_target="tpu_custom_call" | custom-call | flops 108716359680 | bytes 430080000 | tf_op jit(solution)/shard_map/hidden_back/pallas_call | solution.py:82
  242.1 11.7 %norm_back.2.refs_3_ = bf16[2,768,768]{2,1,0:T(8,128)(2,1)} custom-call(s32[13]{0:T(128)} %copy-done.30, bf16[3072,2304]{1,0:T(8,128)(2,1)} %hidden_back.1.refs_1_.refs_8_.refs_2_, bf16[768,4480]{1,0:T(8,128)(2,1)} %refs_2_.12, bf16[768,4480]{1,0:T(8,128)(2,1)} %refs_3_.9, bf16[192,2304]{1,0:T(8,128)(2,1)} %hold.32.refs_16_.refs_5_.refs_7_.refs_4_, ...), custom_call_target="tpu_custom_call" | custom-call | flops 54358179840 | bytes 145326080 | tf_op jit(solution)/shard_map/norm_back/pallas_call | solution.py:82
  253.8 7.0 %all_to_all.31 = bf16[2,768,768]{2,1,0:T(8,128)(2,1)S(1)} all-to-all(bf16[2,768,768]{2,1,0:T(8,128)(2,1)} %norm_back.2.refs_3_), channel_id=1, replica_groups=mesh['dp'=8,'row'=2,'col'=2] {'col'}, dimensions={0} | all-to-all | bytes 4718592 | tf_op jit(solution)/shard_map/all_to_all | solution.py:44
  270.0 24.3 %norm_back.3 = (bf16[2304,768]{1,0:T(8,128)(2,1)}, bf16[2304,768]{1,0:T(8,128)(2,1)}) custom-call(s32[13]{0:T(128)} %copy-done.30, bf16[3072,2304]{1,0:T(8,128)(2,1)} %hidden_back.1.refs_1_.refs_8_.refs_2_, bf16[768,4480]{1,0:T(8,128)(2,1)} %refs_2_.12, bf16[768,4480]{1,0:T(8,128)(2,1)} %refs_3_.9, bf16[192,2304]{1,0:T(8,128)(2,1)} %hold.32.refs_16_.refs_5_.refs_7_.refs_4_, ...), custom_call_target="tpu_custom_call" | custom-call | flops 163074539520 | bytes 268206080 | tf_op jit(solution)/shard_map/norm_back/pallas_call | solution.py:82
  294.4 18.8 %weight_grad.6 = (bf16[2,4,96,1152]{3,2,1,0:T(8,128)(2,1)}, bf16[2,4,96,1152]{3,2,1,0:T(8,128)(2,1)}) custom-call(s32[13]{0:T(128)} %copy-done.30, bf16[3072,1536]{1,0:T(8,128)(2,1)} %get-tuple-element.123.refs_1_, bf16[3072,2304]{1,0:T(8,128)(2,1)} %hidden_back.1.refs_1_.refs_8_.refs_2_, bf16[2304,768]{1,0:T(8,128)(2,1)} %get-tuple-element.122.refs_3_), custom_call_target="tpu_custom_call" | custom-call | flops 108716359680 | bytes 235929600 | tf_op jit(solution)/shard_map/weight_grad/pallas_call | solution.py:82
  316.6 4.5 sum_near.2
  324.5 18.9 %down_project.1 = (bf16[3072,768]{1,0:T(8,128)(2,1)}, bf16[3072,768]{1,0:T(8,128)(2,1)}) custom-call(s32[13]{0:T(128)} %copy-done.30, bf16[3072,1152]{1,0:T(8,128)(2,1)} %get-tuple-element.115.refs_2_.refs_1_, bf16[4480,768]{1,0:T(8,128)(2,1)} %refs_2_.13, bf16[576,768]{1,0:T(8,128)(2,1)} %hold.50.refs_3_.refs_5_, bf16[576,768]{1,0:T(8,128)(2,1)} %copy-done.55, ...), custom_call_target="tpu_custom_call" | custom-call | flops 108716359680 | bytes 245760000 | tf_op jit(solution)/shard_map/down_project/pallas_call | solution.py:82
  343.5 18.9 %weight_grad.7 = (bf16[2,4,96,1152]{3,2,1,0:T(8,128)(2,1)}, bf16[2,4,96,1152]{3,2,1,0:T(8,128)(2,1)}) custom-call(s32[13]{0:T(128)} %copy-done.30, bf16[3072,1536]{1,0:T(8,128)(2,1)} %get-tuple-element.123.refs_1_, bf16[3072,2304]{1,0:T(8,128)(2,1)} %hidden_back.1.refs_1_.refs_8_.refs_2_, bf16[3072,768]{1,0:T(8,128)(2,1)} %get-tuple-element.127.refs_3_), custom_call_target="tpu_custom_call" | custom-call | flops 108716359680 | bytes 235929600 | tf_op jit(solution)/shard_map/weight_grad/pallas_call | solution.py:82
  362.9 4.6 sum_own.1.refs_2_
  367.5 4.9 all-to-all-start.4
  381.1 8.7 %middle_back.1 = (f32[768,768]{1,0:T(8,128)}, bf16[768,1536]{1,0:T(8,128)(2,1)}, f32[1,1536]{1,0:T(1,128)}) custom-call(s32[13]{0:T(128)} %copy-done.30, bf16[2,768,768]{2,1,0:T(8,128)(2,1)} %all-to-all-done.4.refs_1_, f32[768,1536]{1,0:T(8,128)} %get-tuple-element.132.refs_2_.refs_5_, f32[768,1]{1,0:T(8,128)} %get-tuple-element.105.refs_1_.refs_3_, ...), custom_call_target="tpu_custom_call" | custom-call | flops 176947200 | bytes 209715200 | tf_op jit(solution)/shard_map/middle_back/pallas_call | solution.py:82
  396.1 5.2 weight_grad.8
  405.1 4.8 sum_near.3
  413.7 22.5 %attention_back.1 = (bf16[768,1024]{1,0:T(8,128)(2,1)}, f32[1,1024]{1,0:T(1,128)}, bf16[2,768,1536]{2,1,0:T(8,128)(2,1)}) custom-call(s32[13]{0:T(128)} %copy-done.30, bf16[768,1536]{1,0:T(8,128)(2,1)} %get-tuple-element.135.refs_1_, bf16[768,768]{1,0:T(8,128)(2,1)} %get-tuple-element.99.refs_1_.refs_2_, ...), custom_call_target="tpu_custom_call" | custom-call | flops 87577067520 | bytes 209715200 | tf_op jit(solution)/shard_map/attention_back/pallas_call | solution.py:82
  436.2 5.8 %all-to-all-start.5 = ((bf16[2,768,1536]{2,1,0:T(8,128)(2,1)}), bf16[2,768,1536]{2,1,0:T(8,128)(2,1)}, u32[]{:S(2)}, u32[]{:S(2)}) async-start(bf16[2,768,1536]{2,1,0:T(8,128)(2,1)} %get-tuple-element.146.refs_3_), calls=%async_computation.5 | async-start | bytes 9437184 | tf_op jit(solution)/shard_map/all_to_all | solution.py:44
  442.1 6.1 %weight_grad.9 = (bf16[2,4,96,1024]{3,2,1,0:T(8,128)(2,1)}, bf16[2,4,96,1024]{3,2,1,0:T(8,128)(2,1)}) custom-call(s32[13]{0:T(128)} %copy-done.30, bf16[768,1536]{1,0:T(8,128)(2,1)} %get-tuple-element.142.refs_1_, bf16[768,1024]{1,0:T(8,128)(2,1)} %get-tuple-element.145.refs_2_, bf16[2,768,1536]{2,1,0:T(8,128)(2,1)} %get-tuple-element.146.refs_3_), custom_call_target="tpu_custom_call" | custom-call | flops 24159191040 | bytes 55050240 | tf_op jit(solution)/shard_map/weight_grad/pallas_call | solution.py:82
  458.7 7.7 %input_back.1 = (bf16[768,768]{1,0:T(8,128)(2,1)}, f32[1,1536]{1,0:T(1,128)}) custom-call(s32[13]{0:T(128)} %copy-done.30, bf16[2,768,1536]{2,1,0:T(8,128)(2,1)} %all-to-all-done.5.refs_1_, bf16[768,768]{1,0:T(8,128)(2,1)} %copy-done.37, bf16[768,768]{1,0:T(8,128)(2,1)} %copy-done.38, f32[768,1]{1,0:T(8,128)} %get-tuple-element.102.refs_1_.refs_4_, ...), custom_call_target="tpu_custom_call" | custom-call | flops 176947200 | bytes 167772160 | tf_op jit(solution)/shard_map/input_back/pallas_call | solution.py:82
  473.6 11.7 %collective-permute-done.50 = bf16[2,4,96,1024]{3,2,1,0:T(8,128)(2,1)S(1)} collective-permute-done((bf16[2,4,96,1024]{3,2,1,0:T(8,128)(2,1)}, bf16[2,4,96,1024]{3,2,1,0:T(8,128)(2,1)S(1)}, u32[]{:S(2)}, u32[]{:S(2)}) %collective-permute-start.50) | collective-permute-done | bytes 1572896 | tf_op jit(solution)/shard_map/ppermute | solution.py:40
  501.8 5.8 sum_output.1.refs_2_
  525.8 8.6 %collective-permute-done.58.refs_2_ = bf16[2,96,1152]{2,1,0:T(8,128)(2,1)S(1)} collective-permute-done((bf16[2,96,1152]{2,1,0:T(8,128)(2,1)}, bf16[2,96,1152]{2,1,0:T(8,128)(2,1)S(1)}, u32[]{:S(2)}, u32[]{:S(2)}) %collective-permute-start.58) | collective-permute-done | bytes 442400 | tf_op jit(solution)/shard_map/ppermute | solution.py:31
  544.4 10.2 %collective-permute-start.60 = (bf16[1,96,1024]{2,1,0:T(8,128)(2,1)}, bf16[1,96,1024]{2,1,0:T(8,128)(2,1)S(1)}, u32[]{:S(2)}, u32[]{:S(2)}) collective-permute-start(bf16[1,96,1024]{2,1,0:T(8,128)(2,1)} %get-tuple-element.174.refs_3_), channel_id=1, source_target_pairs={{0,2},{2,0},{1,3},{3,1},{4,6},{6,4},{5,7},{7,5},{8,10},{10,8},{9,1... | collective-permute-start | bytes 589832 | tf_op jit(solution)/shard_map/ppermute | solution.py:31
  (392 shorter events, 220.0 us)
Async XLA Ops:
  9.7 49.4 %collective-permute-start.1 = (bf16[768,768]{1,0:T(8,128)(2,1)S(1)}, bf16[768,768]{1,0:T(8,128)(2,1)S(1)}, u32[]{:S(2)}, u32[]{:S(2)}) collective-permute-start(bf16[768,768]{1,0:T(8,128)(2,1)S(1)} %collective-permute-done.refs_1_.refs_2_), channel_id=1, source_target_pairs={{0,1},{1,0},{2,3},{3,2},{4,5},{5,4},{6,7},{7,6},{8,9},{9,8},{10,11... | collective-permute-start | bytes 3538952 | tf_op jit(solution)/shard_map/ppermute | solution.py:35
  53.3 32.4 %collective-permute-start.16 = (bf16[192,2304]{1,0:T(8,128)(2,1)S(1)}, bf16[192,2304]{1,0:T(8,128)(2,1)S(1)}, u32[]{:S(2)}, u32[]{:S(2)}) collective-permute-start(bf16[192,2304]{1,0:T(8,128)(2,1)S(1)} %pack.8.refs_1_), channel_id=1, source_target_pairs={{0,2},{2,0},{1,3},{3,1},{4,6},{6,4},{5,7},{7,5},{8,10},{10,8},{9,1... | collective-permute-start | bytes 2654216 | tf_op jit(solution)/shard_map/ppermute | solution.py:31
  58.6 36.9 %collective-permute-start.15 = (bf16[192,2304]{1,0:T(8,128)(2,1)}, bf16[192,2304]{1,0:T(8,128)(2,1)}, u32[]{:S(2)}, u32[]{:S(2)}) collective-permute-start(bf16[192,2304]{1,0:T(8,128)(2,1)} %hold.32.refs_16_.refs_5_.refs_7_.refs_4_), channel_id=1, source_target_pairs={{0,4},{4,0},{8,12},{12,8},{16,20},{20,16},{24,28},{28,24},{1,5},{5... | collective-permute-start | bytes 2654216 | tf_op jit(solution)/shard_map/ppermute | solution.py:40
  70.8 41.2 %collective-permute-start.18 = (bf16[768,768]{1,0:T(8,128)(2,1)}, bf16[768,768]{1,0:T(8,128)(2,1)S(1)}, u32[]{:S(2)}, u32[]{:S(2)}) collective-permute-start(bf16[768,768]{1,0:T(8,128)(2,1)} %copy_of.1.refs_12_.refs_1_), channel_id=1, source_target_pairs={{0,2},{2,0},{1,3},{3,1},{4,6},{6,4},{5,7},{7,5},{8,10},{10,8},{9,1... | collective-permute-start | bytes 3538952 | tf_op jit(solution)/shard_map/ppermute | solution.py:31
  71.4 41.6 %collective-permute-start.21 = (bf16[768,768]{1,0:T(8,128)(2,1)}, bf16[768,768]{1,0:T(8,128)(2,1)}, u32[]{:S(2)}, u32[]{:S(2)}) collective-permute-start(bf16[768,768]{1,0:T(8,128)(2,1)} %copy_of.1.refs_12_.refs_1_), channel_id=1, source_target_pairs={{0,8},{4,12},{8,0},{12,4},{16,24},{20,28},{24,16},{28,20},{1,9},{5... | collective-permute-start | bytes 3538952 | tf_op jit(solution)/shard_map/ppermute | solution.py:40
  109.0 28.2 %collective-permute-start.17 = (bf16[768,768]{1,0:T(8,128)(2,1)}, bf16[768,768]{1,0:T(8,128)(2,1)S(1)}, u32[]{:S(2)}, u32[]{:S(2)}) collective-permute-start(bf16[768,768]{1,0:T(8,128)(2,1)} %get-tuple-element.104.refs_1_), channel_id=1, source_target_pairs={{0,2},{2,0},{1,3},{3,1},{4,6},{6,4},{5,7},{7,5},{8,10},{10,8},{9,1... | collective-permute-start | bytes 3538952 | tf_op jit(solution)/shard_map/ppermute | solution.py:31
  110.6 28.1 %collective-permute-start.25 = (bf16[768,768]{1,0:T(8,128)(2,1)}, bf16[768,768]{1,0:T(8,128)(2,1)}, u32[]{:S(2)}, u32[]{:S(2)}) collective-permute-start(bf16[768,768]{1,0:T(8,128)(2,1)} %get-tuple-element.104.refs_1_), channel_id=1, source_target_pairs={{0,8},{4,12},{8,0},{12,4},{16,24},{20,28},{24,16},{28,20},{1,9},{5... | collective-permute-start | bytes 3538952 | tf_op jit(solution)/shard_map/ppermute | solution.py:40
  140.9 48.1 %collective-permute-start.30 = (bf16[384,768]{1,0:T(8,128)(2,1)S(1)}, bf16[384,768]{1,0:T(8,128)(2,1)S(1)}, u32[]{:S(2)}, u32[]{:S(2)}) collective-permute-start(bf16[384,768]{1,0:T(8,128)(2,1)S(1)} %hold.40.refs_7_), channel_id=1, source_target_pairs={{0,8},{4,12},{8,0},{12,4},{16,24},{20,28},{24,16},{28,20},{1,9},{5... | collective-permute-start | bytes 1769480 | tf_op jit(solution)/shard_map/ppermute | solution.py:40
  144.7 44.3 %collective-permute-start.29 = (bf16[384,768]{1,0:T(8,128)(2,1)S(1)}, bf16[384,768]{1,0:T(8,128)(2,1)S(1)}, u32[]{:S(2)}, u32[]{:S(2)}) collective-permute-start(bf16[384,768]{1,0:T(8,128)(2,1)S(1)} %hold.45.refs_2_), channel_id=1, source_target_pairs={{0,2},{2,0},{1,3},{3,1},{4,6},{6,4},{5,7},{7,5},{8,10},{10,8},{9,1... | collective-permute-start | bytes 1769480 | tf_op jit(solution)/shard_map/ppermute | solution.py:31
  148.7 46.3 %collective-permute-start.28 = (bf16[576,768]{1,0:T(8,128)(2,1)}, bf16[576,768]{1,0:T(8,128)(2,1)}, u32[]{:S(2)}, u32[]{:S(2)}) collective-permute-start(bf16[576,768]{1,0:T(8,128)(2,1)} %pack.9.refs_15_.refs_12_), channel_id=1, source_target_pairs={{0,2},{2,0},{1,3},{3,1},{4,6},{6,4},{5,7},{7,5},{8,10},{10,8},{9,1... | collective-permute-start | bytes 2654216 | tf_op jit(solution)/shard_map/ppermute | solution.py:31
  219.2 44.8 %collective-permute-start.32 = (bf16[2,4,96,1152]{3,2,1,0:T(8,128)(2,1)}, bf16[2,4,96,1152]{3,2,1,0:T(8,128)(2,1)}, u32[]{:S(2)}, u32[]{:S(2)}) collective-permute-start(bf16[2,4,96,1152]{3,2,1,0:T(8,128)(2,1)} %get-tuple-element.118.refs_7_), channel_id=1, source_target_pairs={{0,4},{4,0},{8,12},{12,8},{16,20},{20,16},{24,28},{28,24},{1,5},{5... | collective-permute-start | bytes 5308424 | tf_op jit(solution)/shard_map/ppermute | solution.py:40
  262.2 52.6 %collective-permute-start.35 = (bf16[384,768]{1,0:T(8,128)(2,1)}, bf16[384,768]{1,0:T(8,128)(2,1)}, u32[]{:S(2)}, u32[]{:S(2)}) collective-permute-start(bf16[384,768]{1,0:T(8,128)(2,1)} %get-tuple-element.187.refs_8_), channel_id=1, source_target_pairs={{0,2},{2,0},{1,3},{3,1},{4,6},{6,4},{5,7},{7,5},{8,10},{10,8},{9,1... | collective-permute-start | bytes 1769480 | tf_op jit(solution)/shard_map/ppermute | solution.py:31
  262.7 52.1 %collective-permute-start.36 = (bf16[384,768]{1,0:T(8,128)(2,1)}, bf16[384,768]{1,0:T(8,128)(2,1)}, u32[]{:S(2)}, u32[]{:S(2)}) collective-permute-start(bf16[384,768]{1,0:T(8,128)(2,1)} %get-tuple-element.186.refs_9_), channel_id=1, source_target_pairs={{0,8},{4,12},{8,0},{12,4},{16,24},{20,28},{24,16},{28,20},{1,9},{5... | collective-permute-start | bytes 1769480 | tf_op jit(solution)/shard_map/ppermute | solution.py:40
  267.4 55.7 %collective-permute-start.33 = (bf16[2,1,192,1152]{3,2,1,0:T(8,128)(2,1)}, bf16[2,1,192,1152]{3,2,1,0:T(8,128)(2,1)}, u32[]{:S(2)}, u32[]{:S(2)}) collective-permute-start(bf16[2,1,192,1152]{3,2,1,0:T(8,128)(2,1)} %get-tuple-element.120.refs_10_), channel_id=1, source_target_pairs={{0,16},{4,20},{8,24},{12,28},{16,0},{20,4},{24,8},{28,12},{1,17},{... | collective-permute-start | bytes 2654216 | tf_op jit(solution)/shard_map/ppermute | solution.py:40
  313.2 76.6 %collective-permute-start.43 = (bf16[2,4,96,1152]{3,2,1,0:T(8,128)(2,1)}, bf16[2,4,96,1152]{3,2,1,0:T(8,128)(2,1)}, u32[]{:S(2)}, u32[]{:S(2)}) collective-permute-start(bf16[2,4,96,1152]{3,2,1,0:T(8,128)(2,1)} %get-tuple-element.124.refs_4_), channel_id=1, source_target_pairs={{0,4},{4,0},{8,12},{12,8},{16,20},{20,16},{24,28},{28,24},{1,5},{5... | collective-permute-start | bytes 5308424 | tf_op jit(solution)/shard_map/ppermute | solution.py:40
  321.0 41.8 %collective-permute-start.38 = (bf16[768,768]{1,0:T(8,128)(2,1)}, bf16[768,768]{1,0:T(8,128)(2,1)}, u32[]{:S(2)}, u32[]{:S(2)}) collective-permute-start(bf16[768,768]{1,0:T(8,128)(2,1)} %get-tuple-element.128), channel_id=1, source_target_pairs={{0,2},{2,0},{1,3},{3,1},{4,6},{6,4},{5,7},{7,5},{8,10},{10,8},{9,1... | collective-permute-start | bytes 3538952 | tf_op jit(solution)/shard_map/ppermute | solution.py:31
  322.5 40.4 %collective-permute-start.39 = (bf16[768,768]{1,0:T(8,128)(2,1)}, bf16[768,768]{1,0:T(8,128)(2,1)}, u32[]{:S(2)}, u32[]{:S(2)}) collective-permute-start(bf16[768,768]{1,0:T(8,128)(2,1)} %get-tuple-element.125.refs_1_), channel_id=1, source_target_pairs={{0,8},{4,12},{8,0},{12,4},{16,24},{20,28},{24,16},{28,20},{1,9},{5... | collective-permute-start | bytes 3538952 | tf_op jit(solution)/shard_map/ppermute | solution.py:40
  343.4 29.0 %collective-permute-start.37 = (bf16[3072,768]{1,0:T(8,128)(2,1)}, bf16[3072,768]{1,0:T(8,128)(2,1)}, u32[]{:S(2)}, u32[]{:S(2)}) collective-permute-start(bf16[3072,768]{1,0:T(8,128)(2,1)} %get-tuple-element.127.refs_3_), channel_id=1, source_target_pairs={{0,1},{1,0},{2,3},{3,2},{4,5},{5,4},{6,7},{7,6},{8,9},{9,8},{10,11... | collective-permute-start | bytes 14155784 | tf_op jit(solution)/shard_map/ppermute | solution.py:35
  362.4 48.8 %collective-permute-start.45 = (bf16[2,4,96,1152]{3,2,1,0:T(8,128)(2,1)}, bf16[2,4,96,1152]{3,2,1,0:T(8,128)(2,1)S(1)}, u32[]{:S(2)}, u32[]{:S(2)}) collective-permute-start(bf16[2,4,96,1152]{3,2,1,0:T(8,128)(2,1)} %get-tuple-element.129.refs_4_), channel_id=1, source_target_pairs={{0,4},{4,0},{8,12},{12,8},{16,20},{20,16},{24,28},{28,24},{1,5},{5... | collective-permute-start | bytes 5308424 | tf_op jit(solution)/shard_map/ppermute | solution.py:40
  375.4 28.9 %collective-permute-start.41 = (bf16[384,768]{1,0:T(8,128)(2,1)}, bf16[384,768]{1,0:T(8,128)(2,1)S(1)}, u32[]{:S(2)}, u32[]{:S(2)}) collective-permute-start(bf16[384,768]{1,0:T(8,128)(2,1)} %get-tuple-element.131.refs_2_), channel_id=1, source_target_pairs={{0,8},{4,12},{8,0},{12,4},{16,24},{20,28},{24,16},{28,20},{1,9},{5... | collective-permute-start | bytes 1769480 | tf_op jit(solution)/shard_map/ppermute | solution.py:40
  393.2 76.2 %collective-permute-start.51 = (bf16[2,1,192,1152]{3,2,1,0:T(8,128)(2,1)}, bf16[2,1,192,1152]{3,2,1,0:T(8,128)(2,1)}, u32[]{:S(2)}, u32[]{:S(2)}) collective-permute-start(bf16[2,1,192,1152]{3,2,1,0:T(8,128)(2,1)} %get-tuple-element.139.refs_1_), channel_id=1, source_target_pairs={{0,16},{4,20},{8,24},{12,28},{16,0},{20,4},{24,8},{28,12},{1,17},{... | collective-permute-start | bytes 2654216 | tf_op jit(solution)/shard_map/ppermute | solution.py:40
  401.3 92.3 %collective-permute-start.48 = (bf16[2,4,96,768]{3,2,1,0:T(8,128)(2,1)}, bf16[2,4,96,768]{3,2,1,0:T(8,128)(2,1)}, u32[]{:S(2)}, u32[]{:S(2)}) collective-permute-start(bf16[2,4,96,768]{3,2,1,0:T(8,128)(2,1)} %get-tuple-element.140.refs_4_), channel_id=1, source_target_pairs={{0,4},{4,0},{8,12},{12,8},{16,20},{20,16},{24,28},{28,24},{1,5},{5... | collective-permute-start | bytes 3538952 | tf_op jit(solution)/shard_map/ppermute | solution.py:40
  410.0 39.7 %collective-permute-start.44 = (bf16[768,768]{1,0:T(8,128)(2,1)}, bf16[768,768]{1,0:T(8,128)(2,1)}, u32[]{:S(2)}, u32[]{:S(2)}) collective-permute-start(bf16[768,768]{1,0:T(8,128)(2,1)} %get-tuple-element.141), channel_id=1, source_target_pairs={{0,2},{2,0},{1,3},{3,1},{4,6},{6,4},{5,7},{7,5},{8,10},{10,8},{9,1... | collective-permute-start | bytes 3538952 | tf_op jit(solution)/shard_map/ppermute | solution.py:31
  410.5 46.0 %collective-permute-start.46 = (bf16[768,768]{1,0:T(8,128)(2,1)}, bf16[768,768]{1,0:T(8,128)(2,1)S(1)}, u32[]{:S(2)}, u32[]{:S(2)}) collective-permute-start(bf16[768,768]{1,0:T(8,128)(2,1)} %get-tuple-element.144.refs_1_), channel_id=1, source_target_pairs={{0,8},{4,12},{8,0},{12,4},{16,24},{20,28},{24,16},{28,20},{1,9},{5... | collective-permute-start | bytes 3538952 | tf_op jit(solution)/shard_map/ppermute | solution.py:40
  448.2 37.2 %collective-permute-start.50 = (bf16[2,4,96,1024]{3,2,1,0:T(8,128)(2,1)}, bf16[2,4,96,1024]{3,2,1,0:T(8,128)(2,1)S(1)}, u32[]{:S(2)}, u32[]{:S(2)}) collective-permute-start(bf16[2,4,96,1024]{3,2,1,0:T(8,128)(2,1)} %get-tuple-element.147.refs_1_), channel_id=1, source_target_pairs={{0,4},{4,0},{8,12},{12,8},{16,20},{20,16},{24,28},{28,24},{1,5},{5... | collective-permute-start | bytes 4718600 | tf_op jit(solution)/shard_map/ppermute | solution.py:40
  454.4 53.1 %collective-permute-start.55 = (bf16[2,1,192,1152]{3,2,1,0:T(8,128)(2,1)}, bf16[2,1,192,1152]{3,2,1,0:T(8,128)(2,1)}, u32[]{:S(2)}, u32[]{:S(2)}) collective-permute-start(bf16[2,1,192,1152]{3,2,1,0:T(8,128)(2,1)} %get-tuple-element.149.refs_1_), channel_id=1, source_target_pairs={{0,16},{4,20},{8,24},{12,28},{16,0},{20,4},{24,8},{28,12},{1,17},{... | collective-permute-start | bytes 2654216 | tf_op jit(solution)/shard_map/ppermute | solution.py:40
  469.4 28.8 %collective-permute-start.47 = (bf16[768,768]{1,0:T(8,128)(2,1)}, bf16[768,768]{1,0:T(8,128)(2,1)S(1)}, u32[]{:S(2)}, u32[]{:S(2)}) collective-permute-start(bf16[768,768]{1,0:T(8,128)(2,1)} %get-tuple-element.151), channel_id=1, source_target_pairs={{0,0},{1,2},{2,1},{3,3},{4,4},{5,6},{6,5},{7,7},{8,8},{9,10},{10,9... | collective-permute-start | bytes 3538952 | tf_op jit(solution)/shard_map/ppermute | solution.py:48
  485.3 31.7 %collective-permute-start.53 = (bf16[2,96,1152]{2,1,0:T(8,128)(2,1)}, bf16[2,96,1152]{2,1,0:T(8,128)(2,1)S(1)}, u32[]{:S(2)}, u32[]{:S(2)}) collective-permute-start(bf16[2,96,1152]{2,1,0:T(8,128)(2,1)} %get-tuple-element.157.refs_3_), channel_id=1, source_target_pairs={{0,2},{2,0},{1,3},{3,1},{4,6},{6,4},{5,7},{7,5},{8,10},{10,8},{9,1... | collective-permute-start | bytes 1327112 | tf_op jit(solution)/shard_map/ppermute | solution.py:31
  493.6 31.2 %collective-permute-start.59 = (f32[4096]{0:T(1024)S(1)}, f32[4096]{0:T(1024)S(1)}, u32[]{:S(2)}, u32[]{:S(2)}) collective-permute-start(f32[4096]{0:T(1024)S(1)} %fusion.8), channel_id=1, source_target_pairs={{0,8},{4,12},{8,0},{12,4},{16,24},{20,28},{24,16},{28,20},{1,9},{5... | collective-permute-start | bytes 49160 | tf_op jit(solution)/shard_map/ppermute | solution.py:40
  498.2 39.5 %collective-permute-start.57 = (bf16[2,2,96,768]{3,2,1,0:T(8,128)(2,1)}, bf16[2,2,96,768]{3,2,1,0:T(8,128)(2,1)S(1)}, u32[]{:S(2)}, u32[]{:S(2)}) collective-permute-start(bf16[2,2,96,768]{3,2,1,0:T(8,128)(2,1)} %get-tuple-element.159.refs_1_), channel_id=1, source_target_pairs={{0,8},{4,12},{8,0},{12,4},{16,24},{20,28},{24,16},{28,20},{1,9},{5... | collective-permute-start | bytes 1769480 | tf_op jit(solution)/shard_map/ppermute | solution.py:40
  524.8 38.0 %collective-permute-start.66 = (bf16[2,96,1152]{2,1,0:T(8,128)(2,1)S(1)}, bf16[2,96,1152]{2,1,0:T(8,128)(2,1)S(1)}, u32[]{:S(2)}, u32[]{:S(2)}) collective-permute-start(bf16[2,96,1152]{2,1,0:T(8,128)(2,1)S(1)} %copy-done.27), channel_id=1, source_target_pairs={{0,8},{4,12},{8,0},{12,4},{16,24},{20,28},{24,16},{28,20},{1,9},{5... | collective-permute-start | bytes 1327112 | tf_op jit(solution)/shard_map/ppermute | solution.py:40
  537.7 32.1 %collective-permute-start.64 = (bf16[2,96,1152]{2,1,0:T(8,128)(2,1)}, bf16[2,96,1152]{2,1,0:T(8,128)(2,1)S(1)}, u32[]{:S(2)}, u32[]{:S(2)}) collective-permute-start(bf16[2,96,1152]{2,1,0:T(8,128)(2,1)} %get-tuple-element.171.refs_3_), channel_id=1, source_target_pairs={{0,8},{4,12},{8,0},{12,4},{16,24},{20,28},{24,16},{28,20},{1,9},{5... | collective-permute-start | bytes 1327112 | tf_op jit(solution)/shard_map/ppermute | solution.py:40
  (116 other events, 1041.5 us)

commit v5 on v4

--- a/solution.py
+++ b/solution.py
@@ -627,30 +627,33 @@
 
     def kernel(s, low, q, k, v, lse, seg_col, seg_row, w_out, *refs):
         out_fetched, (wq, wk, wv), refs = refs[:QUARTERS], refs[QUARTERS:QUARTERS + 3], refs[QUARTERS + 3:]
-        fetched, (cosine, sine, back, bias, part, wo, w, do, dk, dv) = refs[:QUARTERS], refs[QUARTERS:]
+        fetched, (cosine, sine, back, bias, part, wo, w, do, dk, dv, lse_t) = refs[:QUARTERS], refs[QUARTERS:]
         wo[:, :width] = w_out[...]
         for piece, rows in placed(s, out_fetched, 0, qw):
             wo[rows, width:] = piece[...]
         do[...] = dot_right(low[...], wo[...]).astype(BF)
         dk[...] = jnp.zeros_like(dk)
         dv[...] = jnp.zeros_like(dv)
+        lse_t[...] = jnp.transpose(lse[...])
         for start in range(0, length, TILE):
             keys = start + TILE
-            allowed = allowed_keys(seg_col, seg_row, start, TILE, keys)
             rows = slice(start, start + TILE)
+            places = lax.broadcasted_iota(jnp.int32, (keys, TILE), 0)
+            asked = lax.broadcasted_iota(jnp.int32, (keys, TILE), 1) + start
+            allowed = (seg_col[:keys, :] == seg_row[:, rows]) & (places <= asked)
             c, t = cosine[rows, :], sine[rows, :]
             for head in range(heads):
                 pair = head // (heads // pairs)
                 place = slice(head * HD, (head + 1) * HD)
                 mine = slice(pair * HD, (pair + 1) * HD)
-                scores = dot_right(q[rows, place], k[:keys, mine]) * HD ** (-0.5)
-                probs = jnp.where(allowed, jnp.exp(scores - lse[rows, head:head + 1]), 0.0)
-                grads = dot_right(do[rows, place], v[:keys, mine])
-                delta = jnp.sum(probs * grads, axis=1, keepdims=True)
+                scores = dot_right(k[:keys, mine], q[rows, place]) * HD ** (-0.5)
+                probs = jnp.where(allowed, jnp.exp(scores - lse_t[head:head + 1, rows]), 0.0)
+                grads = dot_right(v[:keys, mine], do[rows, place])
+                delta = jnp.sum(probs * grads, axis=0, keepdims=True)
                 score_grad = (probs * (grads - delta)).astype(BF)
-                dv[:keys, mine] += dot_left(probs.astype(BF), do[rows, place])
-                dk[:keys, mine] += dot_left(score_grad, q[rows, place])
-                u = dot(score_grad, k[:keys, mine]) * HD ** (-0.5)
+                dv[:keys, mine] += dot(probs.astype(BF), do[rows, place])
+                dk[:keys, mine] += dot(score_grad, q[rows, place])
+                u = dot_left(score_grad, k[:keys, mine]) * HD ** (-0.5)
                 back[rows, place] = (u * c - pltpu.roll(u, HD // 2, 1) * t).astype(BF)
         for pair in range(pairs):
             u = dk[:, pair * HD:(pair + 1) * HD] * HD ** (-0.5)
@@ -674,7 +677,7 @@
                after=after,
                scratch=[pltpu.VMEM((qw, 2 * width), BF), pltpu.VMEM((2 * width, total), BF),
                         pltpu.VMEM((length, qw), BF), pltpu.VMEM((length, kw), F32),
-                        pltpu.VMEM((length, kw), F32)],
+                        pltpu.VMEM((length, kw), F32), pltpu.VMEM((LANES, length), F32)],
                estimate=cost(10 * length * length * qw + 2 * length * 2 * width * (qw + total), 20 * MIB,
                              heads * length * length), name="attention_back")
 
@@ -1111,21 +1114,21 @@
     small = small_step(small, lambda value: swap_bit(value, 0))
     out_sum = square_next(*out_sum, 1)
     input_grad = hold(input_grad).astype(F32)
+    up = grad_row(*up)
     output = turn_square(sum_output(scalars, out_keep, out_got, via_row, via_near, h))
-    up = grad_row(*up)
     for bit in last_bits:
         qkv_sum = square_next(*qkv_sum, bit)
     gate = grad_near(*gate)
     down = grad_near(*down)
-    output = hold(output)
     small = small_step(small, lambda value: swap_bit(value, 1))
     up = grad_near(*up)
     for bit in last_bits:
         out_sum = square_next(*out_sum, bit)
+    output = hold(output)
     qkv_sum = square_row(*qkv_sum)
-    gate_grad = lay_columns(scalars, *gate, overlap)
     for bit in last_bits:
         small = small_step(small, lambda value, bit=bit: swap_bit(value, bit))
+    gate_grad = lay_columns(scalars, *gate, overlap)
     qkv_grads = sum_split(*qkv_sum, (query_width, key_width, key_width))
     down_grad = lay_columns(scalars, *down, overlap).T
     out_sum = square_row(*out_sum)

time: 587 us -> 585 us (level)
  starting transfers between devices: 115 us -> 106 us
    ppermute x37, waiting for transfers between devices: 24 us -> 38.6 us  [swap_bit(): return lax.ppermute(value, 'dp', [(i, i ^ 1 << bit) for i in range(size)])]
    ppermute x20, waiting for transfers between devices: 17.5 us -> 8.26 us  [swap_row(): return lax.ppermute(value, 'row', [(0, 1), (1, 0)])]
    ppermute x20, starting transfers between devices: 31.8 us -> 23.1 us  [swap_row(): return lax.ppermute(value, 'row', [(0, 1), (1, 0)])]
    unnamed x153 -> x161, local copies, waits for them, and re-layouts: 37.7 us -> 39.8 us
  transfers between devices with their start and end apart: 72 -> 72, of which waited for: 16 -> 19; matrix products, arithmetic and copies ran while one was open for 3% -> 3% of each run, Pallas kernels for 60% -> 60%
where the time goes in v5:
time: 585 us; the launch traced here: 578 us
  Pallas kernels  346 us (59%)
  starting transfers between devices  106 us (18%)
  waiting for transfers between devices  53.1 us (9%)
  local copies, waits for them, and re-layouts  48.4 us (8%)
  blocking collectives  13.5 us (2%)
  other arithmetic  8.5 us (1%)
    pallas_call x82, Pallas kernels, run(): pl.pallas_call(body, grid=grid if grid is not None else (), in_specs=[spe...  346 us
    ppermute x37, starting transfers between devices, swap_bit(): return lax.ppermute(value, 'dp', [(i, i ^ 1 << bit) for i in range(size)])  41.3 us
    unnamed x161, local copies, waits for them, and re-layouts  39.8 us
    ppermute x37, waiting for transfers between devices, swap_bit(): return lax.ppermute(value, 'dp', [(i, i ^ 1 << bit) for i in range(size)])  38.6 us
    ppermute x20, starting transfers between devices, swap_row(): return lax.ppermute(value, 'row', [(0, 1), (1, 0)])  23.1 us
    all_to_all x4, starting transfers between devices, trade_col(): return lax.all_to_all(value, 'col', 0, 0)  21 us
    ppermute x8, starting transfers between devices, swap_col(): return lax.ppermute(value, 'col', [(0, 1), (1, 0)])  15.1 us
    all_to_all x2, blocking collectives, trade_col(): return lax.all_to_all(value, 'col', 0, 0)  13.5 us
  transfers between devices with their start and end apart: 72, of which 19 were waited for; matrix products, arithmetic and copies ran while one was open for 3% of the time, Pallas kernels for 60%

profile of v5, /device:TPU:0, one launch (start us, length us, event | category | flops | bytes accessed | tf_op | source)
XLA Modules:
  0.0 577.8 jit_solution(15131073378909201204)
XLA Ops:
  9.7 14.4 %collective-permute-start.1 = (bf16[768,768]{1,0:T(8,128)(2,1)S(1)}, bf16[768,768]{1,0:T(8,128)(2,1)S(1)}, u32[]{:S(2)}, u32[]{:S(2)}) collective-permute-start(bf16[768,768]{1,0:T(8,128)(2,1)S(1)} %collective-permute-done.refs_1_.refs_2_), channel_id=1, source_target_pairs={{0,1},{1,0},{2,3},{3,2},{4,5},{5,4},{6,7},{7,6},{8,9},{9,8},{10,11... | collective-permute-start | bytes 3538952 | tf_op jit(solution)/shard_map/ppermute | solution.py:35
  60.2 8.2 %qkv.1 = (bf16[768,768]{1,0:T(8,128)(2,1)}, bf16[768,128]{1,0:T(8,128)(2,1)}, bf16[768,128]{1,0:T(8,128)(2,1)}, bf16[768,1536]{1,0:T(8,128)(2,1)}, f32[768,1]{1,0:T(8,128)}) custom-call(s32[13]{0:T(128)} %copy-done.33, bf16[768,768]{1,0:T(8,128)(2,1)} %copy-done.40, bf16[768,768]{1,0:T(8,128)(2,1)} %copy-done.41, ...), custom_call_target="tpu_custom_call" | custom-call | flops 24159191040 | bytes 125829120 | tf_op jit(solution)/shard_map/qkv/pallas_call | solution.py:82
  72.0 13.6 %attention.1 = (bf16[768,768]{1,0:T(8,128)(2,1)}, f32[768,128]{1,0:T(8,128)}, bf16[2,768,1536]{2,1,0:T(8,128)(2,1)}) custom-call(s32[13]{0:T(128)} %copy-done.33, bf16[768,768]{1,0:T(8,128)(2,1)} %get-tuple-element.99.refs_1_.refs_2_, bf16[768,128]{1,0:T(8,128)(2,1)} %get-tuple-element.100.refs_2_.refs_3_, ...), custom_call_target="tpu_custom_call" | custom-call | flops 36238786560 | bytes 125829120 | tf_op jit(solution)/shard_map/attention/pallas_call | solution.py:82
  89.5 6.0 %all-to-all-start = ((bf16[2,768,1536]{2,1,0:T(8,128)(2,1)}), bf16[2,768,1536]{2,1,0:T(8,128)(2,1)}, u32[]{:S(2)}, u32[]{:S(2)}) async-start(bf16[2,768,1536]{2,1,0:T(8,128)(2,1)} %get-tuple-element.103.refs_1_), calls=%async_computation | async-start | bytes 9437184 | tf_op jit(solution)/shard_map/all_to_all | solution.py:44
  100.3 8.6 %norm_two.1 = (f32[768,1536]{1,0:T(8,128)}, bf16[768,768]{1,0:T(8,128)(2,1)}, bf16[768,768]{1,0:T(8,128)(2,1)}, f32[768,1]{1,0:T(8,128)}) custom-call(s32[13]{0:T(128)} %copy-done.33, bf16[768,768]{1,0:T(8,128)(2,1)} %copy-done.40, bf16[768,768]{1,0:T(8,128)(2,1)} %copy-done.41, bf16[2,768,1536]{2,1,0:T(8,128)(2,1)} %all-to-all-done.refs_3_, ...), custom_call_target="tpu_custom_call" | custom-call | flops 117964800 | bytes 167772160 | tf_op jit(solution)/shard_map/norm_two/pallas_call | solution.py:82
  113.4 12.3 %gate_up.3 = (bf16[3072,1536]{1,0:T(8,128)(2,1)}, bf16[3072,1152]{1,0:T(8,128)(2,1)}, bf16[3072,1152]{1,0:T(8,128)(2,1)}, bf16[3072,1152]{1,0:T(8,128)(2,1)}) custom-call(s32[13]{0:T(128)} %copy-done.33, bf16[768,768]{1,0:T(8,128)(2,1)} %get-tuple-element.104.refs_1_, bf16[768,768]{1,0:T(8,128)(2,1)} %get-tuple-element.106.refs_2_, ...), custom_call_target="tpu_custom_call" | custom-call | flops 54358179840 | bytes 125829120 | tf_op jit(solution)/shard_map/gate_up/pallas_call | solution.py:82
  127.5 6.3 %place_rows.1.refs_1_.refs_2_ = bf16[3072,1536]{1,0:T(8,128)(2,1)} custom-call(s32[13]{0:T(128)S(1)} %copy-done.34, bf16[768,768]{1,0:T(8,128)(2,1)} %copy_of.1.refs_12_.refs_1_, bf16[768,768]{1,0:T(8,128)(2,1)S(1)} %copy-done.2, bf16[768,768]{1,0:T(8,128)(2,1)S(1)} %hold.36.refs_1_.refs_3_, bf16[768,768]{1,0:T(8,128)(2,1)S(1)} %hold.38.refs_1_.refs_4_, ...), custom_call_target="tpu_custom_call" | custom-call | bytes 141557760 | tf_op jit(solution)/shard_map/place_rows/pallas_call | solution.py:82
  149.4 19.1 %gate_up.4 = (bf16[3072,1536]{1,0:T(8,128)(2,1)}, bf16[3072,1152]{1,0:T(8,128)(2,1)}, bf16[3072,1152]{1,0:T(8,128)(2,1)}, bf16[3072,1152]{1,0:T(8,128)(2,1)}) custom-call(s32[13]{0:T(128)} %copy-done.33, bf16[768,768]{1,0:T(8,128)(2,1)} %copy-done.5, ...), custom_call_target="tpu_custom_call", output_to_operand_aliasing={{0}: (11, {}), {1}: (12, {}), {2}: (13, {}), {3}: (14, {})} | custom-call | flops 108716359680 | bytes 125829120 | tf_op jit(solution)/shard_map/gate_up/pallas_call | solution.py:82
  170.1 6.5 %all_to_all.30.refs_1_ = bf16[2,768,768]{2,1,0:T(8,128)(2,1)} all-to-all(bf16[2,768,768]{2,1,0:T(8,128)(2,1)S(1)} %pad_maximum_fusion), channel_id=1, replica_groups=mesh['dp'=8,'row'=2,'col'=2] {'col'}, dimensions={0} | all-to-all | bytes 4718592 | tf_op jit(solution)/shard_map/all_to_all | solution.py:44
  176.7 12.3 %gate_up.5 = (bf16[3072,1536]{1,0:T(8,128)(2,1)}, bf16[3072,1152]{1,0:T(8,128)(2,1)}, bf16[3072,1152]{1,0:T(8,128)(2,1)}, bf16[3072,1152]{1,0:T(8,128)(2,1)}) custom-call(s32[13]{0:T(128)} %copy-done.33, bf16[2,768,768]{2,1,0:T(8,128)(2,1)} %all_to_all.30.refs_1_, ...), custom_call_target="tpu_custom_call", output_to_operand_aliasing={{0}: (8, {}), {1}: (9, {}), {2}: (10, {}), {3}: (11, {})} | custom-call | tf_op jit(solution)/shard_map/gate_up/pallas_call | solution.py:82
  190.7 4.2 all-to-all-start.2
  200.5 18.7 %weight_grad.5 = (bf16[2,4,96,1152]{3,2,1,0:T(8,128)(2,1)}, bf16[2,4,96,1152]{3,2,1,0:T(8,128)(2,1)}) custom-call(s32[13]{0:T(128)} %copy-done.33, bf16[3072,1536]{1,0:T(8,128)(2,1)} %place_last.1.refs_1_.refs_3_.refs_6_, bf16[3072,1152]{1,0:T(8,128)(2,1)} %get-tuple-element.115.refs_2_.refs_1_, bf16[3072,1536]{1,0:T(8,128)(2,1)} %place_last.1.refs_1_.refs_3_.refs_6_), custom_call_target="tpu_custom_call" | custom-call | flops 108716359680 | bytes 235929600 | tf_op jit(solution)/shard_map/weight_grad/pallas_call | solution.py:82
  220.6 21.3 %hidden_back.1.refs_1_.refs_8_.refs_2_ = bf16[3072,2304]{1,0:T(8,128)(2,1)} custom-call(s32[13]{0:T(128)} %copy-done.33, bf16[3072,1536]{1,0:T(8,128)(2,1)} %place_last.1.refs_1_.refs_3_.refs_6_, bf16[3072,1152]{1,0:T(8,128)(2,1)} %get-tuple-element.119.refs_2_, bf16[3072,1152]{1,0:T(8,128)(2,1)} %get-tuple-element.116.refs_1_.refs_3_, ...), custom_call_target="tpu_custom_call" | custom-call | flops 108716359680 | bytes 430080000 | tf_op jit(solution)/shard_map/hidden_back/pallas_call | solution.py:82
  242.0 11.7 %norm_back.2.refs_3_ = bf16[2,768,768]{2,1,0:T(8,128)(2,1)} custom-call(s32[13]{0:T(128)} %copy-done.33, bf16[3072,2304]{1,0:T(8,128)(2,1)} %hidden_back.1.refs_1_.refs_8_.refs_2_, bf16[768,4480]{1,0:T(8,128)(2,1)} %refs_2_.12, bf16[768,4480]{1,0:T(8,128)(2,1)} %refs_3_.9, bf16[192,2304]{1,0:T(8,128)(2,1)} %hold.32.refs_16_.refs_5_.refs_7_.refs_4_, ...), custom_call_target="tpu_custom_call" | custom-call | flops 54358179840 | bytes 145326080 | tf_op jit(solution)/shard_map/norm_back/pallas_call | solution.py:82
  253.7 7.0 %all_to_all.31 = bf16[2,768,768]{2,1,0:T(8,128)(2,1)S(1)} all-to-all(bf16[2,768,768]{2,1,0:T(8,128)(2,1)} %norm_back.2.refs_3_), channel_id=1, replica_groups=mesh['dp'=8,'row'=2,'col'=2] {'col'}, dimensions={0} | all-to-all | bytes 4718592 | tf_op jit(solution)/shard_map/all_to_all | solution.py:44
  269.9 24.3 %norm_back.3 = (bf16[2304,768]{1,0:T(8,128)(2,1)}, bf16[2304,768]{1,0:T(8,128)(2,1)}) custom-call(s32[13]{0:T(128)} %copy-done.33, bf16[3072,2304]{1,0:T(8,128)(2,1)} %hidden_back.1.refs_1_.refs_8_.refs_2_, bf16[768,4480]{1,0:T(8,128)(2,1)} %refs_2_.12, bf16[768,4480]{1,0:T(8,128)(2,1)} %refs_3_.9, bf16[192,2304]{1,0:T(8,128)(2,1)} %hold.32.refs_16_.refs_5_.refs_7_.refs_4_, ...), custom_call_target="tpu_custom_call" | custom-call | flops 163074539520 | bytes 268206080 | tf_op jit(solution)/shard_map/norm_back/pallas_call | solution.py:82
  294.3 18.7 %weight_grad.6 = (bf16[2,4,96,1152]{3,2,1,0:T(8,128)(2,1)}, bf16[2,4,96,1152]{3,2,1,0:T(8,128)(2,1)}) custom-call(s32[13]{0:T(128)} %copy-done.33, bf16[3072,1536]{1,0:T(8,128)(2,1)} %get-tuple-element.123.refs_1_, bf16[3072,2304]{1,0:T(8,128)(2,1)} %hidden_back.1.refs_1_.refs_8_.refs_2_, bf16[2304,768]{1,0:T(8,128)(2,1)} %get-tuple-element.122.refs_3_), custom_call_target="tpu_custom_call" | custom-call | flops 108716359680 | bytes 235929600 | tf_op jit(solution)/shard_map/weight_grad/pallas_call | solution.py:82
  316.4 4.5 sum_near.2
  324.3 18.9 %down_project.1 = (bf16[3072,768]{1,0:T(8,128)(2,1)}, bf16[3072,768]{1,0:T(8,128)(2,1)}) custom-call(s32[13]{0:T(128)} %copy-done.33, bf16[3072,1152]{1,0:T(8,128)(2,1)} %get-tuple-element.115.refs_2_.refs_1_, bf16[4480,768]{1,0:T(8,128)(2,1)} %refs_2_.13, bf16[576,768]{1,0:T(8,128)(2,1)} %hold.50.refs_3_.refs_5_, bf16[576,768]{1,0:T(8,128)(2,1)} %copy-done.58, ...), custom_call_target="tpu_custom_call" | custom-call | flops 108716359680 | bytes 245760000 | tf_op jit(solution)/shard_map/down_project/pallas_call | solution.py:82
  343.3 18.9 %weight_grad.7 = (bf16[2,4,96,1152]{3,2,1,0:T(8,128)(2,1)}, bf16[2,4,96,1152]{3,2,1,0:T(8,128)(2,1)}) custom-call(s32[13]{0:T(128)} %copy-done.33, bf16[3072,1536]{1,0:T(8,128)(2,1)} %get-tuple-element.123.refs_1_, bf16[3072,2304]{1,0:T(8,128)(2,1)} %hidden_back.1.refs_1_.refs_8_.refs_2_, bf16[3072,768]{1,0:T(8,128)(2,1)} %get-tuple-element.127.refs_3_), custom_call_target="tpu_custom_call" | custom-call | flops 108716359680 | bytes 235929600 | tf_op jit(solution)/shard_map/weight_grad/pallas_call | solution.py:82
  362.7 4.6 sum_own.1.refs_2_
  367.3 4.9 all-to-all-start.4
  380.9 8.7 %middle_back.1 = (f32[768,768]{1,0:T(8,128)}, bf16[768,1536]{1,0:T(8,128)(2,1)}, f32[1,1536]{1,0:T(1,128)}) custom-call(s32[13]{0:T(128)} %copy-done.33, bf16[2,768,768]{2,1,0:T(8,128)(2,1)} %all-to-all-done.4.refs_1_, f32[768,1536]{1,0:T(8,128)} %get-tuple-element.132.refs_2_.refs_5_, f32[768,1]{1,0:T(8,128)} %get-tuple-element.105.refs_1_.refs_3_, ...), custom_call_target="tpu_custom_call" | custom-call | flops 176947200 | bytes 209715200 | tf_op jit(solution)/shard_map/middle_back/pallas_call | solution.py:82
  395.9 5.2 weight_grad.8
  404.9 4.8 sum_near.3
  413.5 21.0 %attention_back.1 = (bf16[768,1024]{1,0:T(8,128)(2,1)}, f32[1,1024]{1,0:T(1,128)}, bf16[2,768,1536]{2,1,0:T(8,128)(2,1)}) custom-call(s32[13]{0:T(128)} %copy-done.33, bf16[768,1536]{1,0:T(8,128)(2,1)} %get-tuple-element.135.refs_1_, bf16[768,768]{1,0:T(8,128)(2,1)} %get-tuple-element.99.refs_1_.refs_2_, ...), custom_call_target="tpu_custom_call" | custom-call | flops 87577067520 | bytes 209715200 | tf_op jit(solution)/shard_map/attention_back/pallas_call | solution.py:82
  434.6 5.8 %all-to-all-start.5 = ((bf16[2,768,1536]{2,1,0:T(8,128)(2,1)}), bf16[2,768,1536]{2,1,0:T(8,128)(2,1)}, u32[]{:S(2)}, u32[]{:S(2)}) async-start(bf16[2,768,1536]{2,1,0:T(8,128)(2,1)} %get-tuple-element.146.refs_3_), calls=%async_computation.5 | async-start | bytes 9437184 | tf_op jit(solution)/shard_map/all_to_all | solution.py:44
  440.4 6.1 %weight_grad.9 = (bf16[2,4,96,1024]{3,2,1,0:T(8,128)(2,1)}, bf16[2,4,96,1024]{3,2,1,0:T(8,128)(2,1)}) custom-call(s32[13]{0:T(128)} %copy-done.33, bf16[768,1536]{1,0:T(8,128)(2,1)} %get-tuple-element.142.refs_1_, bf16[768,1024]{1,0:T(8,128)(2,1)} %get-tuple-element.145.refs_2_, bf16[2,768,1536]{2,1,0:T(8,128)(2,1)} %get-tuple-element.146.refs_3_), custom_call_target="tpu_custom_call" | custom-call | flops 24159191040 | bytes 55050240 | tf_op jit(solution)/shard_map/weight_grad/pallas_call | solution.py:82
  458.5 7.7 %input_back.1 = (bf16[768,768]{1,0:T(8,128)(2,1)}, f32[1,1536]{1,0:T(1,128)}) custom-call(s32[13]{0:T(128)} %copy-done.33, bf16[2,768,1536]{2,1,0:T(8,128)(2,1)} %all-to-all-done.5.refs_1_, bf16[768,768]{1,0:T(8,128)(2,1)} %copy-done.40, bf16[768,768]{1,0:T(8,128)(2,1)} %copy-done.41, f32[768,1]{1,0:T(8,128)} %get-tuple-element.102.refs_1_.refs_4_, ...), custom_call_target="tpu_custom_call" | custom-call | flops 176947200 | bytes 167772160 | tf_op jit(solution)/shard_map/input_back/pallas_call | solution.py:82
  474.4 9.3 %collective-permute-done.51 = bf16[2,4,96,1024]{3,2,1,0:T(8,128)(2,1)S(1)} collective-permute-done((bf16[2,4,96,1024]{3,2,1,0:T(8,128)(2,1)}, bf16[2,4,96,1024]{3,2,1,0:T(8,128)(2,1)S(1)}, u32[]{:S(2)}, u32[]{:S(2)}) %collective-permute-start.51) | collective-permute-done | bytes 1572896 | tf_op jit(solution)/shard_map/ppermute | solution.py:40
  503.6 5.8 sum_output.1.refs_3_
  539.7 10.0 %collective-permute-done.62.refs_0_ = f32[4096]{0:T(1024)S(1)} collective-permute-done((f32[4096]{0:T(1024)S(1)}, f32[4096]{0:T(1024)S(1)}, u32[]{:S(2)}, u32[]{:S(2)}) %collective-permute-start.62) | collective-permute-done | bytes 16416 | tf_op jit(solution)/shard_map/ppermute | solution.py:40
  (400 shorter events, 226.5 us)
Async XLA Ops:
  9.7 49.4 %collective-permute-start.1 = (bf16[768,768]{1,0:T(8,128)(2,1)S(1)}, bf16[768,768]{1,0:T(8,128)(2,1)S(1)}, u32[]{:S(2)}, u32[]{:S(2)}) collective-permute-start(bf16[768,768]{1,0:T(8,128)(2,1)S(1)} %collective-permute-done.refs_1_.refs_2_), channel_id=1, source_target_pairs={{0,1},{1,0},{2,3},{3,2},{4,5},{5,4},{6,7},{7,6},{8,9},{9,8},{10,11... | collective-permute-start | bytes 3538952 | tf_op jit(solution)/shard_map/ppermute | solution.py:35
  53.3 32.3 %collective-permute-start.16 = (bf16[192,2304]{1,0:T(8,128)(2,1)S(1)}, bf16[192,2304]{1,0:T(8,128)(2,1)S(1)}, u32[]{:S(2)}, u32[]{:S(2)}) collective-permute-start(bf16[192,2304]{1,0:T(8,128)(2,1)S(1)} %pack.8.refs_1_), channel_id=1, source_target_pairs={{0,2},{2,0},{1,3},{3,1},{4,6},{6,4},{5,7},{7,5},{8,10},{10,8},{9,1... | collective-permute-start | bytes 2654216 | tf_op jit(solution)/shard_map/ppermute | solution.py:31
  58.6 36.9 %collective-permute-start.15 = (bf16[192,2304]{1,0:T(8,128)(2,1)}, bf16[192,2304]{1,0:T(8,128)(2,1)}, u32[]{:S(2)}, u32[]{:S(2)}) collective-permute-start(bf16[192,2304]{1,0:T(8,128)(2,1)} %hold.32.refs_16_.refs_5_.refs_7_.refs_4_), channel_id=1, source_target_pairs={{0,4},{4,0},{8,12},{12,8},{16,20},{20,16},{24,28},{28,24},{1,5},{5... | collective-permute-start | bytes 2654216 | tf_op jit(solution)/shard_map/ppermute | solution.py:40
  70.8 41.1 %collective-permute-start.18 = (bf16[768,768]{1,0:T(8,128)(2,1)}, bf16[768,768]{1,0:T(8,128)(2,1)S(1)}, u32[]{:S(2)}, u32[]{:S(2)}) collective-permute-start(bf16[768,768]{1,0:T(8,128)(2,1)} %copy_of.1.refs_12_.refs_1_), channel_id=1, source_target_pairs={{0,2},{2,0},{1,3},{3,1},{4,6},{6,4},{5,7},{7,5},{8,10},{10,8},{9,1... | collective-permute-start | bytes 3538952 | tf_op jit(solution)/shard_map/ppermute | solution.py:31
  71.3 41.6 %collective-permute-start.21 = (bf16[768,768]{1,0:T(8,128)(2,1)}, bf16[768,768]{1,0:T(8,128)(2,1)}, u32[]{:S(2)}, u32[]{:S(2)}) collective-permute-start(bf16[768,768]{1,0:T(8,128)(2,1)} %copy_of.1.refs_12_.refs_1_), channel_id=1, source_target_pairs={{0,8},{4,12},{8,0},{12,4},{16,24},{20,28},{24,16},{28,20},{1,9},{5... | collective-permute-start | bytes 3538952 | tf_op jit(solution)/shard_map/ppermute | solution.py:40
  109.0 28.2 %collective-permute-start.17 = (bf16[768,768]{1,0:T(8,128)(2,1)}, bf16[768,768]{1,0:T(8,128)(2,1)S(1)}, u32[]{:S(2)}, u32[]{:S(2)}) collective-permute-start(bf16[768,768]{1,0:T(8,128)(2,1)} %get-tuple-element.104.refs_1_), channel_id=1, source_target_pairs={{0,2},{2,0},{1,3},{3,1},{4,6},{6,4},{5,7},{7,5},{8,10},{10,8},{9,1... | collective-permute-start | bytes 3538952 | tf_op jit(solution)/shard_map/ppermute | solution.py:31
  140.9 48.1 %collective-permute-start.30 = (bf16[384,768]{1,0:T(8,128)(2,1)S(1)}, bf16[384,768]{1,0:T(8,128)(2,1)S(1)}, u32[]{:S(2)}, u32[]{:S(2)}) collective-permute-start(bf16[384,768]{1,0:T(8,128)(2,1)S(1)} %hold.40.refs_7_), channel_id=1, source_target_pairs={{0,8},{4,12},{8,0},{12,4},{16,24},{20,28},{24,16},{28,20},{1,9},{5... | collective-permute-start | bytes 1769480 | tf_op jit(solution)/shard_map/ppermute | solution.py:40
  144.7 44.3 %collective-permute-start.29 = (bf16[384,768]{1,0:T(8,128)(2,1)S(1)}, bf16[384,768]{1,0:T(8,128)(2,1)S(1)}, u32[]{:S(2)}, u32[]{:S(2)}) collective-permute-start(bf16[384,768]{1,0:T(8,128)(2,1)S(1)} %hold.45.refs_2_), channel_id=1, source_target_pairs={{0,2},{2,0},{1,3},{3,1},{4,6},{6,4},{5,7},{7,5},{8,10},{10,8},{9,1... | collective-permute-start | bytes 1769480 | tf_op jit(solution)/shard_map/ppermute | solution.py:31
  148.7 46.3 %collective-permute-start.28 = (bf16[576,768]{1,0:T(8,128)(2,1)}, bf16[576,768]{1,0:T(8,128)(2,1)}, u32[]{:S(2)}, u32[]{:S(2)}) collective-permute-start(bf16[576,768]{1,0:T(8,128)(2,1)} %pack.9.refs_15_.refs_12_), channel_id=1, source_target_pairs={{0,2},{2,0},{1,3},{3,1},{4,6},{6,4},{5,7},{7,5},{8,10},{10,8},{9,1... | collective-permute-start | bytes 2654216 | tf_op jit(solution)/shard_map/ppermute | solution.py:31
  219.2 44.8 %collective-permute-start.32 = (bf16[2,4,96,1152]{3,2,1,0:T(8,128)(2,1)}, bf16[2,4,96,1152]{3,2,1,0:T(8,128)(2,1)}, u32[]{:S(2)}, u32[]{:S(2)}) collective-permute-start(bf16[2,4,96,1152]{3,2,1,0:T(8,128)(2,1)} %get-tuple-element.118.refs_7_), channel_id=1, source_target_pairs={{0,4},{4,0},{8,12},{12,8},{16,20},{20,16},{24,28},{28,24},{1,5},{5... | collective-permute-start | bytes 5308424 | tf_op jit(solution)/shard_map/ppermute | solution.py:40
  262.1 52.5 %collective-permute-start.35 = (bf16[384,768]{1,0:T(8,128)(2,1)}, bf16[384,768]{1,0:T(8,128)(2,1)}, u32[]{:S(2)}, u32[]{:S(2)}) collective-permute-start(bf16[384,768]{1,0:T(8,128)(2,1)} %get-tuple-element.187.refs_8_), channel_id=1, source_target_pairs={{0,2},{2,0},{1,3},{3,1},{4,6},{6,4},{5,7},{7,5},{8,10},{10,8},{9,1... | collective-permute-start | bytes 1769480 | tf_op jit(solution)/shard_map/ppermute | solution.py:31
  262.6 52.0 %collective-permute-start.36 = (bf16[384,768]{1,0:T(8,128)(2,1)}, bf16[384,768]{1,0:T(8,128)(2,1)}, u32[]{:S(2)}, u32[]{:S(2)}) collective-permute-start(bf16[384,768]{1,0:T(8,128)(2,1)} %get-tuple-element.186.refs_9_), channel_id=1, source_target_pairs={{0,8},{4,12},{8,0},{12,4},{16,24},{20,28},{24,16},{28,20},{1,9},{5... | collective-permute-start | bytes 1769480 | tf_op jit(solution)/shard_map/ppermute | solution.py:40
  267.4 55.6 %collective-permute-start.33 = (bf16[2,1,192,1152]{3,2,1,0:T(8,128)(2,1)}, bf16[2,1,192,1152]{3,2,1,0:T(8,128)(2,1)}, u32[]{:S(2)}, u32[]{:S(2)}) collective-permute-start(bf16[2,1,192,1152]{3,2,1,0:T(8,128)(2,1)} %get-tuple-element.120.refs_10_), channel_id=1, source_target_pairs={{0,16},{4,20},{8,24},{12,28},{16,0},{20,4},{24,8},{28,12},{1,17},{... | collective-permute-start | bytes 2654216 | tf_op jit(solution)/shard_map/ppermute | solution.py:40
  313.1 76.6 %collective-permute-start.43 = (bf16[2,4,96,1152]{3,2,1,0:T(8,128)(2,1)}, bf16[2,4,96,1152]{3,2,1,0:T(8,128)(2,1)}, u32[]{:S(2)}, u32[]{:S(2)}) collective-permute-start(bf16[2,4,96,1152]{3,2,1,0:T(8,128)(2,1)} %get-tuple-element.124.refs_4_), channel_id=1, source_target_pairs={{0,4},{4,0},{8,12},{12,8},{16,20},{20,16},{24,28},{28,24},{1,5},{5... | collective-permute-start | bytes 5308424 | tf_op jit(solution)/shard_map/ppermute | solution.py:40
  320.9 41.8 %collective-permute-start.38 = (bf16[768,768]{1,0:T(8,128)(2,1)}, bf16[768,768]{1,0:T(8,128)(2,1)}, u32[]{:S(2)}, u32[]{:S(2)}) collective-permute-start(bf16[768,768]{1,0:T(8,128)(2,1)} %get-tuple-element.128), channel_id=1, source_target_pairs={{0,2},{2,0},{1,3},{3,1},{4,6},{6,4},{5,7},{7,5},{8,10},{10,8},{9,1... | collective-permute-start | bytes 3538952 | tf_op jit(solution)/shard_map/ppermute | solution.py:31
  322.3 40.4 %collective-permute-start.39 = (bf16[768,768]{1,0:T(8,128)(2,1)}, bf16[768,768]{1,0:T(8,128)(2,1)}, u32[]{:S(2)}, u32[]{:S(2)}) collective-permute-start(bf16[768,768]{1,0:T(8,128)(2,1)} %get-tuple-element.125.refs_1_), channel_id=1, source_target_pairs={{0,8},{4,12},{8,0},{12,4},{16,24},{20,28},{24,16},{28,20},{1,9},{5... | collective-permute-start | bytes 3538952 | tf_op jit(solution)/shard_map/ppermute | solution.py:40
  343.2 29.1 %collective-permute-start.37 = (bf16[3072,768]{1,0:T(8,128)(2,1)}, bf16[3072,768]{1,0:T(8,128)(2,1)}, u32[]{:S(2)}, u32[]{:S(2)}) collective-permute-start(bf16[3072,768]{1,0:T(8,128)(2,1)} %get-tuple-element.127.refs_3_), channel_id=1, source_target_pairs={{0,1},{1,0},{2,3},{3,2},{4,5},{5,4},{6,7},{7,6},{8,9},{9,8},{10,11... | collective-permute-start | bytes 14155784 | tf_op jit(solution)/shard_map/ppermute | solution.py:35
  362.2 48.8 %collective-permute-start.45 = (bf16[2,4,96,1152]{3,2,1,0:T(8,128)(2,1)}, bf16[2,4,96,1152]{3,2,1,0:T(8,128)(2,1)S(1)}, u32[]{:S(2)}, u32[]{:S(2)}) collective-permute-start(bf16[2,4,96,1152]{3,2,1,0:T(8,128)(2,1)} %get-tuple-element.129.refs_4_), channel_id=1, source_target_pairs={{0,4},{4,0},{8,12},{12,8},{16,20},{20,16},{24,28},{28,24},{1,5},{5... | collective-permute-start | bytes 5308424 | tf_op jit(solution)/shard_map/ppermute | solution.py:40
  375.2 28.9 %collective-permute-start.41 = (bf16[384,768]{1,0:T(8,128)(2,1)}, bf16[384,768]{1,0:T(8,128)(2,1)S(1)}, u32[]{:S(2)}, u32[]{:S(2)}) collective-permute-start(bf16[384,768]{1,0:T(8,128)(2,1)} %get-tuple-element.131.refs_2_), channel_id=1, source_target_pairs={{0,8},{4,12},{8,0},{12,4},{16,24},{20,28},{24,16},{28,20},{1,9},{5... | collective-permute-start | bytes 1769480 | tf_op jit(solution)/shard_map/ppermute | solution.py:40
  393.0 77.2 %collective-permute-start.52 = (bf16[2,1,192,1152]{3,2,1,0:T(8,128)(2,1)}, bf16[2,1,192,1152]{3,2,1,0:T(8,128)(2,1)}, u32[]{:S(2)}, u32[]{:S(2)}) collective-permute-start(bf16[2,1,192,1152]{3,2,1,0:T(8,128)(2,1)} %get-tuple-element.139.refs_1_), channel_id=1, source_target_pairs={{0,16},{4,20},{8,24},{12,28},{16,0},{20,4},{24,8},{28,12},{1,17},{... | collective-permute-start | bytes 2654216 | tf_op jit(solution)/shard_map/ppermute | solution.py:40
  401.1 90.9 %collective-permute-start.49 = (bf16[2,4,96,768]{3,2,1,0:T(8,128)(2,1)}, bf16[2,4,96,768]{3,2,1,0:T(8,128)(2,1)}, u32[]{:S(2)}, u32[]{:S(2)}) collective-permute-start(bf16[2,4,96,768]{3,2,1,0:T(8,128)(2,1)} %get-tuple-element.140.refs_4_), channel_id=1, source_target_pairs={{0,4},{4,0},{8,12},{12,8},{16,20},{20,16},{24,28},{28,24},{1,5},{5... | collective-permute-start | bytes 3538952 | tf_op jit(solution)/shard_map/ppermute | solution.py:40
  409.8 38.3 %collective-permute-start.44 = (bf16[768,768]{1,0:T(8,128)(2,1)}, bf16[768,768]{1,0:T(8,128)(2,1)}, u32[]{:S(2)}, u32[]{:S(2)}) collective-permute-start(bf16[768,768]{1,0:T(8,128)(2,1)} %get-tuple-element.141), channel_id=1, source_target_pairs={{0,2},{2,0},{1,3},{3,1},{4,6},{6,4},{5,7},{7,5},{8,10},{10,8},{9,1... | collective-permute-start | bytes 3538952 | tf_op jit(solution)/shard_map/ppermute | solution.py:31
  410.4 45.9 %collective-permute-start.46 = (bf16[768,768]{1,0:T(8,128)(2,1)}, bf16[768,768]{1,0:T(8,128)(2,1)S(1)}, u32[]{:S(2)}, u32[]{:S(2)}) collective-permute-start(bf16[768,768]{1,0:T(8,128)(2,1)} %get-tuple-element.144.refs_1_), channel_id=1, source_target_pairs={{0,8},{4,12},{8,0},{12,4},{16,24},{20,28},{24,16},{28,20},{1,9},{5... | collective-permute-start | bytes 3538952 | tf_op jit(solution)/shard_map/ppermute | solution.py:40
  446.5 37.2 %collective-permute-start.51 = (bf16[2,4,96,1024]{3,2,1,0:T(8,128)(2,1)}, bf16[2,4,96,1024]{3,2,1,0:T(8,128)(2,1)S(1)}, u32[]{:S(2)}, u32[]{:S(2)}) collective-permute-start(bf16[2,4,96,1024]{3,2,1,0:T(8,128)(2,1)} %get-tuple-element.147.refs_1_), channel_id=1, source_target_pairs={{0,4},{4,0},{8,12},{12,8},{16,20},{20,16},{24,28},{28,24},{1,5},{5... | collective-permute-start | bytes 4718600 | tf_op jit(solution)/shard_map/ppermute | solution.py:40
  452.8 47.3 %collective-permute-start.47 = (bf16[2,1,192,1152]{3,2,1,0:T(8,128)(2,1)}, bf16[2,1,192,1152]{3,2,1,0:T(8,128)(2,1)}, u32[]{:S(2)}, u32[]{:S(2)}) collective-permute-start(bf16[2,1,192,1152]{3,2,1,0:T(8,128)(2,1)} %get-tuple-element.149.refs_1_), channel_id=1, source_target_pairs={{0,16},{4,20},{8,24},{12,28},{16,0},{20,4},{24,8},{28,12},{1,17},{... | collective-permute-start | bytes 2654216 | tf_op jit(solution)/shard_map/ppermute | solution.py:40
  483.7 32.1 %collective-permute-start.57 = (bf16[2,96,1152]{2,1,0:T(8,128)(2,1)}, bf16[2,96,1152]{2,1,0:T(8,128)(2,1)S(1)}, u32[]{:S(2)}, u32[]{:S(2)}) collective-permute-start(bf16[2,96,1152]{2,1,0:T(8,128)(2,1)} %get-tuple-element.158.refs_3_), channel_id=1, source_target_pairs={{0,2},{2,0},{1,3},{3,1},{4,6},{6,4},{5,7},{7,5},{8,10},{10,8},{9,1... | collective-permute-start | bytes 1327112 | tf_op jit(solution)/shard_map/ppermute | solution.py:31
  492.0 30.6 %collective-permute-start.56 = (f32[4096]{0:T(1024)S(1)}, f32[4096]{0:T(1024)S(1)}, u32[]{:S(2)}, u32[]{:S(2)}) collective-permute-start(f32[4096]{0:T(1024)S(1)} %fusion.8), channel_id=1, source_target_pairs={{0,8},{4,12},{8,0},{12,4},{16,24},{20,28},{24,16},{28,20},{1,9},{5... | collective-permute-start | bytes 49160 | tf_op jit(solution)/shard_map/ppermute | solution.py:40
  496.6 30.2 %collective-permute-start.54 = (bf16[2,2,96,768]{3,2,1,0:T(8,128)(2,1)}, bf16[2,2,96,768]{3,2,1,0:T(8,128)(2,1)S(1)}, u32[]{:S(2)}, u32[]{:S(2)}) collective-permute-start(bf16[2,2,96,768]{3,2,1,0:T(8,128)(2,1)} %get-tuple-element.160.refs_1_), channel_id=1, source_target_pairs={{0,8},{4,12},{8,0},{12,4},{16,24},{20,28},{24,16},{28,20},{1,9},{5... | collective-permute-start | bytes 1769480 | tf_op jit(solution)/shard_map/ppermute | solution.py:40
  522.5 29.3 %collective-permute-start.61 = (bf16[2,96,1152]{2,1,0:T(8,128)(2,1)S(1)}, bf16[2,96,1152]{2,1,0:T(8,128)(2,1)S(1)}, u32[]{:S(2)}, u32[]{:S(2)}) collective-permute-start(bf16[2,96,1152]{2,1,0:T(8,128)(2,1)S(1)} %copy-done.65), channel_id=1, source_target_pairs={{0,8},{4,12},{8,0},{12,4},{16,24},{20,28},{24,16},{28,20},{1,9},{5... | collective-permute-start | bytes 1327112 | tf_op jit(solution)/shard_map/ppermute | solution.py:40
  523.6 34.5 %collective-permute-start.66 = (bf16[2,96,1152]{2,1,0:T(8,128)(2,1)S(1)}, bf16[2,96,1152]{2,1,0:T(8,128)(2,1)S(1)}, u32[]{:S(2)}, u32[]{:S(2)}) collective-permute-start(bf16[2,96,1152]{2,1,0:T(8,128)(2,1)S(1)} %copy-done.28), channel_id=1, source_target_pairs={{0,8},{4,12},{8,0},{12,4},{16,24},{20,28},{24,16},{28,20},{1,9},{5... | collective-permute-start | bytes 1327112 | tf_op jit(solution)/shard_map/ppermute | solution.py:40
  531.2 30.1 %collective-permute-start.65 = (bf16[2,1,96,768]{3,2,1,0:T(8,128)(2,1)}, bf16[2,1,96,768]{3,2,1,0:T(8,128)(2,1)S(1)}, u32[]{:S(2)}, u32[]{:S(2)}) collective-permute-start(bf16[2,1,96,768]{3,2,1,0:T(8,128)(2,1)} %get-tuple-element.171.refs_1_), channel_id=1, source_target_pairs={{0,16},{4,20},{8,24},{12,28},{16,0},{20,4},{24,8},{28,12},{1,17},{... | collective-permute-start | bytes 884744 | tf_op jit(solution)/shard_map/ppermute | solution.py:40
  537.1 30.5 %collective-permute-start.64 = (bf16[2,96,1152]{2,1,0:T(8,128)(2,1)S(1)}, bf16[2,96,1152]{2,1,0:T(8,128)(2,1)S(1)}, u32[]{:S(2)}, u32[]{:S(2)}) collective-permute-start(bf16[2,96,1152]{2,1,0:T(8,128)(2,1)S(1)} %copy-done.63), channel_id=1, source_target_pairs={{0,8},{4,12},{8,0},{12,4},{16,24},{20,28},{24,16},{28,20},{1,9},{5... | collective-permute-start | bytes 1327112 | tf_op jit(solution)/shard_map/ppermute | solution.py:40
  (120 other events, 1041.0 us)
